TPU v7x, 32 devices: a whole 2x2x4 slice. The times are simulated.
32 devices in a mesh: req: 8 (over z, y), grp: 4 (over x, core).
Axes of the slice: x: 2, y: 2, z: 4, core: 2. Of those that a mesh axis runs over, the one named last changes fastest.
Arguments:
- suffix_queries: bfloat16 [4, 1024, 1024], P('grp', 'req'), may hold values from -140 to 140
- suffix_keys: bfloat16 [4, 1024, 1024], P('grp', 'req'), may hold values from -6 to 6
- suffix_values: bfloat16 [4, 1024, 1024], P('grp', 'req'), may hold values from -6 to 6
- prefix_cache: bfloat16 [4, 32, 2048], P('grp', 'req'), may hold values from -6 to 6
- residual: bfloat16 [4, 1024, 2048], P('grp', 'req'), may hold values from -6 to 6
- out_weight: bfloat16 [1024, 2048], P(('req', 'grp')), may hold values from -0.1875 to 0.1875
- norm_gain: float32 [2048], replicated, may hold values from 0.5 to 1.5
- routes: int32 [4, 1024, 4], P('grp', 'req'), may hold values from 0 to 7, all different within a row; in each aligned block of 128 rows (0 to 127, 128 to 255, ..., all dimensions but the last counted through in order) at most 80 rows name the same one
- route_weights: float32 [4, 1024, 4], P('grp', 'req'), may hold values from 0.05 to 0.6
- lengths: int32 [4, 16], P('grp'), may hold values from 1 to 256, 1024 in all within a row
- migrate: int32 [2, 64], P(None, 'req'), may hold values 0 or 1
- expert_gate: bfloat16 [8, 2048, 704], P('req', None, 'grp'), may hold values from -0.125 to 0.125
- expert_up: bfloat16 [8, 2048, 704], P('req', None, 'grp'), may hold values from -0.125 to 0.125
- expert_down: bfloat16 [8, 704, 2048], P('req', 'grp'), may hold values from -0.21875 to 0.21875
- shared_gate: bfloat16 [2048, 2816], P(None, 'grp'), may hold values from -0.125 to 0.125
- shared_up: bfloat16 [2048, 2816], P(None, 'grp'), may hold values from -0.125 to 0.125
- shared_down: bfloat16 [2816, 2048], P('grp'), may hold values from -0.109375 to 0.109375
- shared_router: bfloat16 [2048], replicated, may hold values from -0.125 to 0.125
Outputs:
- hidden_out: bfloat16 [4, 1024, 2048], P('grp', 'req')
- suffix_cache: bfloat16 [4, 1024, 2048], P('grp', 'req')
Inputs may be any that keep to these rules, and one draw needn't show every extreme that they name: In each aligned block of 128 tokens no expert is named by more than 80 routes, a bound that some block reaches. Each group's lengths sum to 1024; the longest is exactly 256.
All inputs are finite; a program needn't handle non-finite values. No bound on the sum of `migrate` on one device may be relied on, other than what follows from the above.
Results may differ from a plain program's by a relative error of at most 0.0069.
Values may be sent and summed in bfloat16 or wider, within the bound.
No kernel may reach another device: no remote copies, remote signals or barrier semaphores. Data moves between devices by JAX's collectives and lax.ppermute only.
A program may use at most 128 MiB of HBM per device.

v0:
```python
import jax
import jax.numpy as jnp
from jax import lax
from jax.sharding import PartitionSpec as P

D = 2048
HD = 128
HEADS = 8
TOP = 4
PG = 16


ROPE_BASE = 1000000.0
EPSILON = 1e-06


def swapped(array, axis, stride):
    return lax.ppermute(array, axis, [(i, i ^ 1 << stride) for i in range(lax.axis_size(axis))])


def shifted(block, axis, distance):
    devices = range(lax.axis_size(axis))
    route = [(i - distance, i) for i in devices if i - distance in devices]
    return lax.ppermute(block, axis, route)


def request_index(token_ids, length_row):
    request_ends = jnp.cumsum(length_row)
    starts = request_ends - length_row
    request = jnp.sum((token_ids[:, None] >= request_ends[None, :]).astype(jnp.int32), axis=1)
    onehot = request[:, None] == jnp.arange(length_row.shape[0], dtype=jnp.int32)[None, :]
    opening = jnp.sum(jnp.where(onehot, starts[None, :], 0), axis=1)
    return (request, token_ids - opening)


def rope_rows(entries, positions):
    half_size = HD // 2
    indices = jnp.arange(half_size, dtype=jnp.float32)
    inv_freq = jnp.power(ROPE_BASE, -2.0 * indices / HD)
    angles = positions[:, None] * inv_freq[None, :]
    cosine = jnp.cos(angles)[:, None, :]
    sine_part = jnp.sin(angles)[:, None, :]
    per_head = entries.astype(jnp.float32).reshape(entries.shape[0], HEADS, HD)
    first_half = per_head[..., :half_size]
    second = per_head[..., half_size:]
    turned = jnp.concatenate(
        [first_half * cosine - second * sine_part, second * cosine + first_half * sine_part],
        axis=-1,
    )
    return turned.reshape(entries.shape[0], HEADS * HD).astype(jnp.bfloat16)


def attend(query_block, key_rows, value_rows, allowed):
    count_rows = query_block.shape[0]
    query_heads = query_block.reshape(count_rows, HEADS, HD)
    key_heads = key_rows.reshape(key_rows.shape[0], HEADS, HD)
    value_heads = value_rows.reshape(value_rows.shape[0], HEADS, HD)
    scores = jnp.einsum(
        "qhd,khd->hqk", query_heads, key_heads, preferred_element_type=jnp.float32
    ) * HD ** (-0.5)
    scores = jnp.where(allowed[None], scores, -1e30)
    highest = jnp.max(scores, axis=2, keepdims=True)
    weights = jnp.where(allowed[None], jnp.exp(scores - highest), 0.0)
    totals = jnp.sum(weights, axis=2, keepdims=True)
    probabilities = weights.astype(jnp.bfloat16)
    blended = (
        jnp.einsum("hqk,khd->hqd", probabilities, value_heads, preferred_element_type=jnp.float32)
        / totals
    )
    return jnp.transpose(blended, (1, 0, 2)).reshape(count_rows, HEADS * HD).astype(jnp.bfloat16)


def expert_outputs(matrix_rows, gate_matrix, up_matrix, down_matrix):
    gate_part = jnp.dot(matrix_rows, gate_matrix, preferred_element_type=jnp.float32)
    up_part = jnp.dot(matrix_rows, up_matrix, preferred_element_type=jnp.float32)
    hidden = (jax.nn.silu(gate_part) * up_part).astype(jnp.bfloat16)
    return jnp.dot(hidden, down_matrix, preferred_element_type=jnp.float32).astype(jnp.bfloat16)


def local(
    suffix_queries,
    suffix_keys,
    suffix_values,
    prefix_cache,
    residual,
    out_weight,
    norm_gain,
    routes,
    route_weights,
    lengths,
    migrate,
    expert_gate,
    expert_up,
    expert_down,
    shared_gate,
    shared_up,
    shared_down,
    shared_router,
):
    local_rows = suffix_queries.shape[1]
    request_devices = lax.axis_size("req")
    device_row = lax.axis_index("req")
    group_row = lax.axis_index("grp")
    history_depth = min(8, request_devices // 4)
    prefix_len = prefix_cache.shape[1] * request_devices
    width_all = HEADS * HD
    token_ids = device_row * local_rows + jnp.arange(local_rows, dtype=jnp.int32)
    request, offset = request_index(token_ids, lengths[0])
    positions = (prefix_len + offset).astype(jnp.float32)
    query_turned = rope_rows(suffix_queries[0], positions)
    key_turned = rope_rows(suffix_keys[0], positions)
    own_cache = jnp.concatenate([key_turned, suffix_values[0]], axis=1)
    partner = swapped(own_cache, "grp", 1)
    pair_row = group_row // 4 * 2 + group_row % 2
    page_flags = jnp.sum(
        jnp.where((jnp.arange(migrate.shape[0], dtype=jnp.int32) == pair_row)[:, None], migrate, 0),
        axis=0,
    )
    page_moved = jnp.repeat(page_flags, PG) == 1
    suffix_cache = jnp.where(page_moved[:, None], partner, own_cache)
    prefix_rows = lax.all_gather(prefix_cache[0], "req", axis=0, tiled=True)
    blocks = [own_cache]
    for distance in range(1, history_depth + 1):
        blocks.append(shifted(own_cache, "req", distance))
    window = jnp.concatenate(blocks, axis=0)
    block_device = device_row - jnp.arange(history_depth + 1, dtype=jnp.int32)
    key_ids = (
        block_device[:, None] * local_rows + jnp.arange(local_rows, dtype=jnp.int32)[None, :]
    ).reshape(-1)
    history_request = request_index(jnp.maximum(key_ids, 0), lengths[0])[0]
    allowed = (
        (key_ids[None, :] >= 0)
        & (history_request[None, :] == request[:, None])
        & (key_ids[None, :] <= token_ids[:, None])
    )
    allowed = jnp.concatenate([jnp.ones((local_rows, prefix_len), jnp.bool_), allowed], axis=1)
    key_rows = jnp.concatenate([prefix_rows[:, :width_all], window[:, :width_all]], axis=0)
    value_rows = jnp.concatenate([prefix_rows[:, width_all:], window[:, width_all:]], axis=0)
    attention = attend(query_turned, key_rows, value_rows, allowed)
    out_full = lax.all_gather(out_weight, ("req", "grp"), axis=0, tiled=True)
    state = residual[0].astype(jnp.float32) + jnp.dot(
        attention, out_full, preferred_element_type=jnp.float32
    )
    normed = (
        state * lax.rsqrt(jnp.mean(state * state, axis=1, keepdims=True) + EPSILON) * norm_gain
    ).astype(jnp.bfloat16)
    shard_rows = lax.all_gather(normed, "grp", axis=0, tiled=True)
    gate_part = jnp.dot(shard_rows, shared_gate, preferred_element_type=jnp.float32)
    up_part = jnp.dot(shard_rows, shared_up, preferred_element_type=jnp.float32)
    shared_hidden = (jax.nn.silu(gate_part) * up_part).astype(jnp.bfloat16)
    shared_out = lax.psum_scatter(
        jnp.dot(shared_hidden, shared_down, preferred_element_type=jnp.float32).astype(
            jnp.bfloat16
        ),
        "grp",
        scatter_dimension=0,
        tiled=True,
    ).astype(jnp.float32)
    shared_scale = jax.nn.sigmoid(
        jnp.dot(normed, shared_router, preferred_element_type=jnp.float32)
    )
    capacity = local_rows * TOP * 5 // (4 * request_devices)
    flat_experts = routes[0].reshape(-1)
    onehot = (
        flat_experts[:, None] == jnp.arange(request_devices, dtype=jnp.int32)[None, :]
    ).astype(jnp.int32)
    earlier = jnp.cumsum(onehot, axis=0) - onehot
    slot_index = jnp.sum(earlier * onehot, axis=1)
    source_rows = jnp.repeat(normed, TOP, axis=0)
    outgoing = (
        jnp.zeros((request_devices, capacity, D), jnp.bfloat16)
        .at[flat_experts, slot_index]
        .set(source_rows)
    )
    gate_all, up_all, down_all = (
        lax.all_gather(expert_gate, "grp", axis=2, tiled=True),
        lax.all_gather(expert_up, "grp", axis=2, tiled=True),
        lax.all_gather(expert_down, "grp", axis=1, tiled=True),
    )
    arrived = lax.all_to_all(outgoing, "req", split_axis=0, concat_axis=0, tiled=True)
    slot_count = arrived.shape[1]
    finished = expert_outputs(arrived.reshape(-1, D), gate_all[0], up_all[0], down_all[0])
    finished = finished.reshape(request_devices, slot_count, D)
    returned = lax.all_to_all(finished, "req", split_axis=0, concat_axis=0, tiled=True)
    route_rows = returned[flat_experts, slot_index].astype(jnp.float32)
    weighted = route_rows * route_weights[0].reshape(-1)[:, None]
    routed = jnp.sum(weighted.reshape(local_rows, TOP, D), axis=1)
    final = state + shared_scale[:, None] * shared_out + routed
    return (final.astype(jnp.bfloat16)[None], suffix_cache[None])


def solution(mesh):
    placed = (
        P("grp", "req", None),
        P("grp", "req", None),
        P("grp", "req", None),
        P("grp", "req", None),
        P("grp", "req", None),
        P(("req", "grp"), None),
        P(),
        P("grp", "req", None),
        P("grp", "req", None),
        P("grp", None),
        P(None, "req"),
        P("req", None, "grp"),
        P("req", None, "grp"),
        P("req", "grp", None),
        P(None, "grp"),
        P(None, "grp"),
        P("grp", None),
        P(),
    )
    return jax.shard_map(
        local,
        mesh=mesh,
        in_specs=placed,
        out_specs=(P("grp", "req", None), P("grp", "req", None)),
        check_vma=False,
    )
```

profile of v0, /device:TPU:0, one launch (start us, length us, event | category | flops | bytes accessed | tf_op | source)
XLA Modules:
  0.0 389.9 jit_solution(17183582388143868010)
XLA Ops:
  21.8 2.7 subtract_convert_fusion.1
  27.4 5.7 %collective-permute-start.1 = (bf16[128,2048]{0,1:T(8,128)(2,1)}, bf16[128,2048]{0,1:T(8,128)(2,1)}, u32[]{:S(2)}, u32[]{:S(2)}) collective-permute-start(bf16[128,2048]{0,1:T(8,128)(2,1)} %pad_maximum_fusion.3), channel_id=1, source_target_pairs={{0,8},{4,12},{8,16},{12,20},{16,24},{20,28},{1,9},{5,13},{9,17},{1... | collective-permute-start | bytes 1572872 | tf_op jit(solution)/shard_map/ppermute | solution.py:24
  33.0 4.2 %collective-permute-start = (bf16[128,2048]{0,1:T(8,128)(2,1)}, bf16[128,2048]{0,1:T(8,128)(2,1)}, u32[]{:S(2)}, u32[]{:S(2)}) collective-permute-start(bf16[128,2048]{0,1:T(8,128)(2,1)} %pad_maximum_fusion.3), channel_id=1, source_target_pairs={{0,4},{4,8},{8,12},{12,16},{16,20},{20,24},{24,28},{1,5},{5,9},{9,... | collective-permute-start | bytes 1572872 | tf_op jit(solution)/shard_map/ppermute | solution.py:24
  37.6 59.1 %all-gather = bf16[1,32,2048]{2,0,1:T(2,128)(2,1)} all-gather(bf16[1,4,2048]{2,0,1:T(2,128)(2,1)S(1)} %copy.65), channel_id=2, replica_groups=mesh['req'=8,'grp'=4] {'req'}, dimensions={1}, use_global_device_ids=true | all-gather | bytes 147456 | tf_op jit(solution)/shard_map/all_gather | solution.py:121
  101.7 2.5 pad_maximum_fusion.1
  106.5 3.0 multiply_select_fusion
  109.5 3.7 fusion.11
  113.2 3.1 multiply_reduce_fusion.1
  121.6 2.5 broadcast_in_dim.69
  124.0 4.0 %reshape.267 = bf16[512,2048]{1,0:T(8,128)(2,1)} reshape(bf16[128,4,2048]{2,1,0:T(4,128)(2,1)} %broadcast_in_dim.69) | data formatting | bytes 4194304 | tf_op jit(solution)/shard_map/reshape | solution.py:169
  129.9 92.3 %scatter_fusion = bf16[8,80,2048]{2,1,0:T(8,128)(2,1)} fusion(bf16[8,80,2048]{2,1,0:T(8,128)(2,1)} %broadcast_in_dim.68, s32[512]{0:T(512)S(1)} %bitcast.90, bf16[512,2048]{1,0:T(8,128)(2,1)} %reshape.267), kind=kCustom, calls=%fused_computation.1 | custom fusion | bytes 6295552 | tf_op jit(solution)/shard_map/scatter | solution.py:173
  222.2 4.4 %all-to-all-start = ((bf16[8,80,2048]{2,1,0:T(8,128)(2,1)}), bf16[8,80,2048]{2,1,0:T(8,128)(2,1)}, u32[]{:S(2)}, u32[]{:S(2)}) async-start(bf16[8,80,2048]{2,1,0:T(8,128)(2,1)} %scatter_fusion), calls=%async_computation.1 | async-start | bytes 5242880 | tf_op jit(solution)/shard_map/all_to_all | solution.py:180
  227.3 5.2 %fusion.49 = f32[512,704]{0,1:T(8,128)} fusion(bf16[512,2048]{1,0:T(8,128)(2,1)} %all-gather.9.cloned.1.call-done, bf16[2048,704]{0,1:T(8,128)(2,1)} %param.32), kind=kOutput, calls=%fused_computation.90 | convolution fusion | flops 1476395008 | bytes 6422528 | tf_op jit(solution)/shard_map/dot_general | solution.py:148
  232.5 44.0 %all-to-all-done = bf16[8,80,2048]{2,1,0:T(8,128)(2,1)} async-done(((bf16[8,80,2048]{2,1,0:T(8,128)(2,1)}), bf16[8,80,2048]{2,1,0:T(8,128)(2,1)}, u32[]{:S(2)}, u32[]{:S(2)}) %all-to-all-start) | async-done | bytes 2621472 | tf_op jit(solution)/shard_map/all_to_all | solution.py:180
  276.5 6.3 %fusion.4 = f32[640,704]{0,1:T(8,128)} fusion(bf16[640,2048]{1,0:T(8,128)(2,1)} %bitcast.21, bf16[1,2048,704]{1,2,0:T(8,128)(2,1)} %all-gather.11.cloned.1.call-done), kind=kOutput, calls=%fused_computation.9 | convolution fusion | flops 1845493760 | bytes 7307264 | tf_op jit(solution)/shard_map/dot_general | solution.py:74
  282.8 13.6 %convolution_convert_fusion = bf16[640,2048]{1,0:T(8,128)(2,1)} fusion(bf16[1,704,2048]{2,1,0:T(8,128)(2,1)} %all-gather.15.cloned.1.call-done, f32[640,704]{0,1:T(8,128)} %fusion.4, bf16[640,2048]{1,0:T(8,128)(2,1)} %bitcast.21, bf16[1,2048,704]{1,2,0:T(8,128)(2,1)} %all-gather.13.cloned.1.call-done), kind=kOutput, calls=%fused_computation.4 | convolution fusion | flops 3695001600 | bytes 12812288 | tf_op jit(solution)/shard_map/dot_general | solution.py:77
  296.4 4.4 %all-to-all-start.1 = ((bf16[8,80,2048]{2,1,0:T(8,128)(2,1)}), bf16[8,80,2048]{2,1,0:T(8,128)(2,1)}, u32[]{:S(2)}, u32[]{:S(2)}) async-start(bf16[8,80,2048]{2,1,0:T(8,128)(2,1)} %bitcast.99), calls=%async_computation.2 | async-start | bytes 5242880 | tf_op jit(solution)/shard_map/all_to_all | solution.py:184
  301.1 7.7 %convolution_convert_fusion.1 = bf16[512,2048]{1,0:T(8,128)(2,1)} fusion(bf16[704,2048]{1,0:T(8,128)(2,1)S(1)} %copy-done, bf16[512,2048]{1,0:T(8,128)(2,1)} %all-gather.9.cloned.1.call-done, bf16[2048,704]{0,1:T(8,128)(2,1)} %param.33, f32[512,704]{0,1:T(8,128)} %fusion.49), kind=kOutput, calls=%fused_computation.5 | convolution fusion | flops 2956001280 | bytes 11403264 | tf_op jit(solution)/shard_map/dot_general | solution.py:152
  310.6 7.7 %collective-permute-done.2 = bf16[128,2048]{0,1:T(8,128)(2,1)} collective-permute-done((bf16[128,2048]{0,1:T(8,128)(2,1)}, bf16[128,2048]{0,1:T(8,128)(2,1)}, u32[]{:S(2)}, u32[]{:S(2)}) %collective-permute-start.2) | collective-permute-done | bytes 524320 | tf_op jit(solution)/shard_map/ppermute | solution.py:18
  322.8 33.4 %all-to-all-done.1 = bf16[8,80,2048]{2,1,0:T(8,128)(2,1)} async-done(((bf16[8,80,2048]{2,1,0:T(8,128)(2,1)}), bf16[8,80,2048]{2,1,0:T(8,128)(2,1)}, u32[]{:S(2)}, u32[]{:S(2)}) %all-to-all-start.1) | async-done | bytes 2621472 | tf_op jit(solution)/shard_map/all_to_all | solution.py:184
  356.2 13.1 %gather_fusion = bf16[512,2048]{1,0:T(8,128)(2,1)} fusion(bf16[8,80,2048]{2,1,0:T(8,128)(2,1)} %all-to-all-done.1, s32[512]{0:T(512)S(1)} %bitcast.89), kind=kCustom, calls=%fused_computation | custom fusion | bytes 4198400 | tf_op jit(solution)/shard_map/gather | solution.py:185
  369.3 4.8 %reshape.258 = f32[128,4,2048]{2,1,0:T(4,128)} reshape(bf16[512,2048]{1,0:T(8,128)(2,1)} %gather_fusion) | data formatting | bytes 6291456 | tf_op jit(solution)/shard_map/convert_element_type | solution.py:185
  374.0 6.3 %multiply_reduce_fusion = f32[128,2048]{1,0:T(8,128)} fusion(f32[128,4,2048]{2,1,0:T(4,128)} %reshape.258, f32[128,4]{1,0:T(8,128)S(1)} %copy.79), kind=kLoop, calls=%fused_computation.3 | loop fusion | flops 1835008 | bytes 5244928 | tf_op jit(solution)/shard_map/reduce_sum | solution.py:187
  380.4 2.7 fusion.19
  (110 shorter events, 39.1 us)
Async XLA Ops:
  7.2 293.9 %copy-start = (bf16[704,2048]{1,0:T(8,128)(2,1)S(1)}, bf16[704,2048]{1,0:T(8,128)(2,1)}, u32[]{:S(2)}) copy-start(bf16[704,2048]{1,0:T(8,128)(2,1)} %param.34) | copy-start | bytes 8650756
  7.2 8.0 %copy-start.14 = (s32[1,16]{1,0:T(1,128)S(1)}, s32[1,16]{1,0:T(1,128)}, u32[]{:S(2)}) copy-start(s32[1,16]{1,0:T(1,128)} %param.27) | copy-start | bytes 196
  7.2 106.0 %all-gather.7.cloned.1.call-start = ((), (), s32[]{:S(2)}) async-start(), calls=%async_computation.3 | async-start | bytes 4325376 | tf_op jit(solution)/shard_map/all_gather | solution.py:140
  7.9 219.3 %all-gather.9.cloned.1.call-start = ((), (), s32[]{:S(2)}) async-start(), calls=%async_computation.4 | async-start | bytes 2621440 | tf_op jit(solution)/shard_map/all_gather | solution.py:147
  9.2 90.9 %copy-start.3 = (bf16[1,128,1024]{1,2,0:T(8,128)(2,1)}, bf16[1,128,1024]{1,2,0:T(8,128)(2,1)S(1)}, u32[]{:S(2)}) copy-start(bf16[1,128,1024]{1,2,0:T(8,128)(2,1)S(1)} %copy.71) | copy-start | bytes 786436
  21.8 15.5 %copy-start.8 = (bf16[1,4,2048]{2,1,0:T(4,128)(2,1)S(1)}, bf16[1,4,2048]{2,1,0:T(4,128)(2,1)}, u32[]{:S(2)}) copy-start(bf16[1,4,2048]{2,1,0:T(4,128)(2,1)} %param.21) | copy-start | bytes 49156
  26.5 75.0 %copy-start.4 = (bf16[128,8,128]{0,2,1:T(8,128)(2,1)}, bf16[128,8,128]{0,2,1:T(8,128)(2,1)S(1)}, u32[]{:S(2)}) copy-start(bf16[128,8,128]{0,2,1:T(8,128)(2,1)S(1)} %copy.70) | copy-start | bytes 786436
  27.4 72.7 %collective-permute-start.1 = (bf16[128,2048]{0,1:T(8,128)(2,1)}, bf16[128,2048]{0,1:T(8,128)(2,1)}, u32[]{:S(2)}, u32[]{:S(2)}) collective-permute-start(bf16[128,2048]{0,1:T(8,128)(2,1)} %pad_maximum_fusion.3), channel_id=1, source_target_pairs={{0,8},{4,12},{8,16},{12,20},{16,24},{20,28},{1,9},{5,13},{9,17},{1... | collective-permute-start | bytes 1572872 | tf_op jit(solution)/shard_map/ppermute | solution.py:24
  33.0 67.0 %collective-permute-start = (bf16[128,2048]{0,1:T(8,128)(2,1)}, bf16[128,2048]{0,1:T(8,128)(2,1)}, u32[]{:S(2)}, u32[]{:S(2)}) collective-permute-start(bf16[128,2048]{0,1:T(8,128)(2,1)} %pad_maximum_fusion.3), channel_id=1, source_target_pairs={{0,4},{4,8},{8,12},{12,16},{16,20},{20,24},{24,28},{1,5},{5,9},{9,... | collective-permute-start | bytes 1572872 | tf_op jit(solution)/shard_map/ppermute | solution.py:24
  101.7 2.6 copy-start.5
  101.7 2.6 copy-start.6
  109.5 3.7 copy-start.7
  113.2 4.1 %copy-start.9 = (f32[2048]{0:T(1024)S(1)}, f32[2048]{0:T(1024)}, u32[]{:S(2)}) copy-start(f32[2048]{0:T(1024)} %param.24) | copy-start | bytes 24580
  116.3 3.3 copy-start.11
  118.2 3.3 copy-start.2
  118.3 114.2 %all-gather.11.cloned.1.call-start = ((), (), s32[]{:S(2)}) async-start(), calls=%async_computation.6 | async-start | bytes 3604480 | tf_op jit(solution)/shard_map/all_gather | solution.py:176
  119.0 163.8 %all-gather.15.cloned.1.call-start = ((), (), s32[]{:S(2)}) async-start(), calls=%async_computation.8 | async-start | bytes 3604480 | tf_op jit(solution)/shard_map/all_gather | solution.py:178
  222.2 54.3 %all-to-all-start = ((bf16[8,80,2048]{2,1,0:T(8,128)(2,1)}), bf16[8,80,2048]{2,1,0:T(8,128)(2,1)}, u32[]{:S(2)}, u32[]{:S(2)}) async-start(bf16[8,80,2048]{2,1,0:T(8,128)(2,1)} %scatter_fusion), calls=%async_computation.1 | async-start | bytes 5242880 | tf_op jit(solution)/shard_map/all_to_all | solution.py:180
  226.6 56.2 %all-gather.13.cloned.1.call-start = ((), (), s32[]{:S(2)}) async-start(), calls=%async_computation.7 | async-start | bytes 3604480 | tf_op jit(solution)/shard_map/all_gather | solution.py:177
  296.4 59.8 %all-to-all-start.1 = ((bf16[8,80,2048]{2,1,0:T(8,128)(2,1)}), bf16[8,80,2048]{2,1,0:T(8,128)(2,1)}, u32[]{:S(2)}, u32[]{:S(2)}) async-start(bf16[8,80,2048]{2,1,0:T(8,128)(2,1)} %bitcast.99), calls=%async_computation.2 | async-start | bytes 5242880 | tf_op jit(solution)/shard_map/all_to_all | solution.py:184
  300.8 79.6 %reduce-scatter.2.cloned.1.call-start = ((), (), s32[]{:S(2)}) async-start(), calls=%async_computation.5 | async-start | bytes 2621440 | tf_op jit(solution)/shard_map/reduce_scatter | solution.py:151
  308.8 1.5 copy-start.10
  308.8 1.6 copy-start.13
  308.8 9.6 %collective-permute-start.2 = (bf16[128,2048]{0,1:T(8,128)(2,1)}, bf16[128,2048]{0,1:T(8,128)(2,1)}, u32[]{:S(2)}, u32[]{:S(2)}) collective-permute-start(bf16[128,2048]{0,1:T(8,128)(2,1)} %pad_maximum_fusion.3), channel_id=1, source_target_pairs={{0,2},{1,3},{2,0},{3,1},{4,6},{5,7},{6,4},{7,5},{8,10},{9,11},{10,... | collective-permute-start | bytes 1572872 | tf_op jit(solution)/shard_map/ppermute | solution.py:18
  (2 other events, 2.4 us)
Sparse Core Ops, SparseCore 0:
  10.9 69.1 all-gather.6
  118.4 20.0 all-gather.8
  140.0 27.0 all-gather.10
  168.5 27.0 all-gather.14
  228.7 28.4 all-gather.12
  308.9 32.2 reduce-scatter.1
where the time goes:
time: 393 us; the launch traced here: 390 us
  local copies, waits for them, and re-layouts  140 us (36%)
  waiting for transfers between devices  87.5 us (22%)
  blocking collectives  59.1 us (15%)
  matrix products  45.1 us (11%)
  other arithmetic  23.1 us (6%)
  starting transfers between devices  20.7 us (5%)
  between operations  14.4 us (4%)
    scatter x1, local copies, waits for them, and re-layouts, local(): outgoing = jnp.zeros((request_devices, capacity, D), jnp.bfloat16).at[fla...  92.3 us
    all_gather x1, blocking collectives, local(): prefix_rows = lax.all_gather(prefix_cache[0], 'req', axis=0, tiled=True)  59.1 us
    all_to_all x1, waiting for transfers between devices, local(): lax.all_to_all(outgoing, 'req', split_axis=0, concat_axis=0, tiled=True)  44 us
    all_to_all x1, waiting for transfers between devices, local(): lax.all_to_all(finished, 'req', split_axis=0, concat_axis=0, tiled=True)  33.4 us
    unnamed x41, local copies, waits for them, and re-layouts  14.6 us
    dot_general x1, matrix products, expert_outputs(): jnp.dot(hidden, down_matrix, preferred_element_type=jnp.float32)  13.6 us
    gather x1, local copies, waits for them, and re-layouts, local(): route_rows = returned[flat_experts, slot_index].astype(jnp.float32)  13.1 us
    ppermute x2, starting transfers between devices, shifted(): return lax.ppermute(block, axis, route)  9.92 us
  transfers between devices with their start and end apart: 11, of which 3 were waited for; matrix products, arithmetic and copies ran while one was open for 48% of the time, Pallas kernels for 0%

commit v1 on v0

v1 whole, which is shorter than its diff:
```python
import functools
import math

import jax
import jax.numpy as jnp
import numpy as np
from jax import lax
from jax.experimental import pallas as pl
from jax.experimental.pallas import tpu as pltpu
from jax.sharding import PartitionSpec as P

D = 2048
HD = 128
HEADS = 8
WIDTH = HEADS * HD
TOP = 4
PG = 16
ROPE_BASE = 1000000.0
EPSILON = 1e-06
F32 = jnp.float32
BF16 = jnp.bfloat16
VMEM = pl.BlockSpec(memory_space=pltpu.VMEM)
SMEM = pl.BlockSpec(memory_space=pltpu.SMEM)
ANY = pl.BlockSpec(memory_space=pl.ANY)
NT = (((1,), (1,)), ((), ()))


def request_starts(lengths_ref, token_ids):
    start = jnp.zeros_like(token_ids)
    end = jnp.int32(0)
    for request in range(lengths_ref.shape[1]):
        end = end + lengths_ref[0, request]
        start = jnp.where(token_ids >= end, end, start)
    return start


def rope_kernel(prefix_len, lengths_ref, place_ref, inv_ref, q_ref, k_ref, v_ref, turned_ref, cache_ref):
    rows = q_ref.shape[0]
    shape = (rows, HD)
    token_ids = place_ref[0] * rows + lax.broadcasted_iota(jnp.int32, shape, 0)
    offset = token_ids - request_starts(lengths_ref, token_ids)
    angles = (prefix_len + offset).astype(F32) * inv_ref[...]
    cosine = jnp.cos(angles)
    sine = jnp.sin(angles)
    sine = jnp.where(lax.broadcasted_iota(jnp.int32, shape, 1) < HD // 2, -sine, sine)
    for head in range(HEADS):
        cols = slice(head * HD, (head + 1) * HD)
        for source, target in ((q_ref, turned_ref), (k_ref, cache_ref)):
            entries = source[:, cols].astype(F32)
            turned = entries * cosine + pltpu.roll(entries, HD // 2, 1) * sine
            target[:, cols] = turned.astype(BF16)
    cache_ref[:, WIDTH:] = v_ref[...]


def attend_kernel(depth, lengths_ref, place_ref, q_ref, prefix_ref, *refs):
    blocks, out_ref = refs[: depth + 1], refs[depth + 1]
    rows = q_ref.shape[0]
    prefix_len = prefix_ref.shape[0]
    first = place_ref[0] * rows
    ids = lax.broadcasted_iota(jnp.int32, (rows, rows), 0) + first
    start = request_starts(lengths_ref, ids)
    allowed = [jnp.ones((rows, prefix_len), jnp.bool_)]
    for distance in range(depth + 1):
        keys = lax.broadcasted_iota(jnp.int32, (rows, rows), 1) + (first - distance * rows)
        allowed.append((keys <= ids) & (keys >= start))
    bias = jnp.concatenate([jnp.where(a, 0.0, -1e30) for a in allowed], axis=1)
    keep = bias == 0.0
    sources = (prefix_ref,) + blocks
    for head in range(HEADS):
        cols = slice(head * HD, (head + 1) * HD)
        values_at = slice(WIDTH + head * HD, WIDTH + (head + 1) * HD)
        keys = jnp.concatenate([s[:, cols] for s in sources], axis=0)
        values = jnp.concatenate([s[:, values_at] for s in sources], axis=0)
        scores = lax.dot_general(q_ref[:, cols], keys, NT, preferred_element_type=F32)
        scores = jnp.where(keep, scores * HD ** (-0.5), -1e30)
        highest = jnp.max(scores, axis=1, keepdims=True)
        weights = jnp.where(keep, jnp.exp(scores - highest), 0.0)
        total = jnp.sum(weights, axis=1, keepdims=True)
        blended = jnp.dot(weights.astype(BF16), values, preferred_element_type=F32) / total
        out_ref[:, cols] = blended.astype(BF16)


def slot_experts(slots, capacity, experts, shape, dim):
    slot = lax.broadcasted_iota(jnp.int32, shape, dim).astype(F32)
    expert = jnp.floor((slot + 0.5) * (1.0 / capacity))
    return expert, slot - expert * capacity


def members(routes_ref, experts):
    rows = routes_ref.shape[0]
    numbers = lax.broadcasted_iota(jnp.int32, (rows, experts), 1)
    found = [routes_ref[:, k : k + 1] == numbers for k in range(TOP)]
    member = jnp.where(found[0] | found[1] | found[2] | found[3], 1.0, 0.0)
    above = lax.broadcasted_iota(jnp.int32, (rows, rows), 0) > lax.broadcasted_iota(
        jnp.int32, (rows, rows), 1
    )
    rank = jnp.dot(
        jnp.where(above, 1.0, 0.0).astype(BF16), member.astype(BF16), preferred_element_type=F32
    )
    return found, jnp.where(member > 0.5, rank, -1.0).astype(BF16)


def project_kernel(
    experts, capacity, moves, count, place_ref, attn_ref, residual_ref, gain_ref, router_ref, routes_ref, *refs
):
    pieces = refs[:count]
    state_ref, normed_ref, scale_ref, out_ref, weight, sem = refs[count:]
    for piece, source, rows, target in moves(place_ref):
        pltpu.make_async_copy(
            pieces[piece].at[pl.ds(source, rows)], weight.at[pl.ds(target, rows)], sem
        ).start()
    _, rank = members(routes_ref, experts)
    slots = experts * capacity
    slot_expert, slot_rank = slot_experts(slots, capacity, experts, (slots, 128), 0)
    columns = lax.broadcasted_iota(jnp.int32, (slots, experts), 1).astype(F32)
    select = jnp.where(slot_expert[:, :experts] == columns, 1.0, 0.0).astype(BF16)
    wanted = lax.dot_general(select, rank, NT, preferred_element_type=F32)
    pick = jnp.where(wanted == slot_rank, 1.0, 0.0).astype(BF16)
    pltpu.make_async_copy(weight, weight, sem).wait()
    step = 512
    square = jnp.zeros((attn_ref.shape[0], 1), F32)
    for at in range(0, D, step):
        cols = slice(at, at + step)
        part = residual_ref[:, cols].astype(F32) + jnp.dot(
            attn_ref[...], weight[:, cols], preferred_element_type=F32
        )
        state_ref[:, cols] = part
        square = square + jnp.sum(part * part, axis=1, keepdims=True)
    factor = lax.rsqrt(square * (1.0 / D) + EPSILON)
    logit = jnp.zeros_like(square)
    for at in range(0, D, step):
        cols = slice(at, at + step)
        normed = (state_ref[:, cols] * factor * gain_ref[:, cols]).astype(BF16)
        normed_ref[:, cols] = normed
        logit = logit + jnp.sum(
            normed.astype(F32) * router_ref[:, cols].astype(F32), axis=1, keepdims=True
        )
        out_ref[:, cols] = jnp.dot(pick, normed, preferred_element_type=F32).astype(BF16)
    scale_ref[...] = jnp.broadcast_to(jax.nn.sigmoid(logit), scale_ref.shape)


def ffn_kernel(xs, shards, outs, shard_rows, *refs):
    x_refs, refs = refs[:xs], refs[xs:]
    g_refs, refs = refs[:shards], refs[shards:]
    u_refs, refs = refs[:shards], refs[shards:]
    d_refs, refs = refs[:shards], refs[shards:]
    out_refs, refs = refs[:outs], refs[outs:]
    x, gate, up, down, hidden, sems = refs
    hid = shards * shard_rows
    padded = hidden.shape[1]
    waits = []
    at = 0
    for ref in x_refs:
        pltpu.make_async_copy(ref, x.at[pl.ds(at, ref.shape[0])], sems.at[0]).start()
        at += ref.shape[0]
    for target, sources, sem in ((gate, g_refs, 1), (up, u_refs, 2), (down, d_refs, 3)):
        for number, ref in enumerate(sources):
            pltpu.make_async_copy(
                ref, target.at[pl.ds(number * shard_rows, shard_rows)], sems.at[sem]
            ).start()
    if padded > hid:
        for target in (gate, up, down):
            target[hid:, :] = jnp.zeros((padded - hid, D), BF16)

    def wait(target, rows, sem):
        part = target.at[pl.ds(0, rows)]
        pltpu.make_async_copy(part, part, sems.at[sem]).wait()

    wait(x, x.shape[0], 0)
    wait(gate, hid, 1)
    wait(up, hid, 2)
    chunk = 256

    @pl.loop(0, padded // chunk)
    def _(j):
        rows = pl.ds(pl.multiple_of(j * chunk, chunk), chunk)
        g = lax.dot_general(x[...], gate[rows, :], NT, preferred_element_type=F32)
        u = lax.dot_general(x[...], up[rows, :], NT, preferred_element_type=F32)
        hidden[:, rows] = (g / (1.0 + jnp.exp(-g)) * u).astype(BF16)

    wait(down, hid, 3)

    @pl.loop(0, D // chunk)
    def _(j):
        cols = pl.ds(pl.multiple_of(j * chunk, chunk), chunk)
        result = jnp.dot(hidden[...], down[:, cols], preferred_element_type=F32).astype(BF16)
        at = 0
        for ref in out_refs:
            ref[:, cols] = result[at : at + ref.shape[0]]
            at += ref.shape[0]


def ffn(x_list, gates, ups, downs, out_rows):
    shard_rows = gates[0].shape[0]
    shards = len(gates)
    padded = -(-shards * shard_rows // 256) * 256
    rows = sum(x.shape[0] for x in x_list)
    return pl.pallas_call(
        functools.partial(ffn_kernel, len(x_list), shards, len(out_rows), shard_rows),
        out_shape=[jax.ShapeDtypeStruct((n, D), BF16) for n in out_rows],
        in_specs=[ANY] * (len(x_list) + 3 * shards),
        out_specs=[VMEM] * len(out_rows),
        scratch_shapes=[
            pltpu.VMEM((rows, D), BF16),
            pltpu.VMEM((padded, D), BF16),
            pltpu.VMEM((padded, D), BF16),
            pltpu.VMEM((padded, D), BF16),
            pltpu.VMEM((rows, padded), BF16),
            pltpu.SemaphoreType.DMA((4,)),
        ],
        compiler_params=pltpu.CompilerParams(vmem_limit_bytes=48 << 20),
        cost_estimate=pl.CostEstimate(
            flops=6 * rows * padded * D, bytes_accessed=6 * padded * D + 4 * rows * D, transcendentals=rows * padded
        ),
    )(*x_list, *gates, *ups, *downs)


def combine_kernel(
    experts, capacity, state_ref, scale_ref, routes_ref, weights_ref, back_ref, keep_ref, sib_ref, far_ref, out_ref
):
    found, rank = members(routes_ref, experts)
    slots = experts * capacity
    slot_expert, slot_rank = slot_experts(slots, capacity, experts, (experts, slots), 1)
    numbers = lax.broadcasted_iota(jnp.int32, (experts, slots), 0).astype(F32)
    select = jnp.where(slot_expert == numbers, 1.0, 0.0).astype(BF16)
    mine = jnp.dot(rank, select, preferred_element_type=F32) == slot_rank[:1]
    weight = jnp.zeros(rank.shape, F32)
    for k in range(TOP):
        weight = weight + jnp.where(found[k], weights_ref[:, k : k + 1], 0.0)
    high = weight.astype(BF16)
    low = (weight - high.astype(F32)).astype(BF16)
    spread = [
        jnp.where(mine, jnp.dot(part, select, preferred_element_type=F32), 0.0).astype(BF16)
        for part in (high, low)
    ]
    rows = state_ref.shape[0]
    scale = scale_ref[:, :1]
    step = 512
    for at in range(0, D, step):
        cols = slice(at, at + step)
        back = back_ref[:, cols]
        routed = jnp.dot(spread[0], back, preferred_element_type=F32) + jnp.dot(
            spread[1], back, preferred_element_type=F32
        )
        shared = (
            keep_ref[:rows, cols].astype(F32)
            + sib_ref[:rows, cols].astype(F32)
            + far_ref[:, cols].astype(F32)
        )
        out_ref[:, cols] = (state_ref[:, cols] + scale * shared + routed).astype(BF16)


def vmem_call(kernel, out_shape, specs, limit=32, scratch=(), flops=0):
    return pl.pallas_call(
        kernel,
        out_shape=out_shape,
        in_specs=specs,
        out_specs=jax.tree.map(lambda _: VMEM, out_shape),
        scratch_shapes=scratch,
        compiler_params=pltpu.CompilerParams(vmem_limit_bytes=limit << 20),
        cost_estimate=pl.CostEstimate(flops=flops, bytes_accessed=4 << 20, transcendentals=0),
    )


def shape(*dims, dtype=BF16):
    return jax.ShapeDtypeStruct(dims, dtype)


def grp_move(array, flip):
    return lax.ppermute(array, "grp", [(i, i ^ flip) for i in range(lax.axis_size("grp"))])


def req_shift(array, distance):
    devices = range(lax.axis_size("req"))
    return lax.ppermute(array, "req", [(i - distance, i) for i in devices if i - distance in devices])


def gather_projection(out_weight, requests):
    part = out_weight.shape[0]
    if requests != 8:
        full = lax.all_gather(out_weight, ("req", "grp"), axis=0, tiled=True)
        return [full], lambda place_ref: [(0, 0, full.shape[0], 0)]
    half = part // 2
    ring = [out_weight] + [
        lax.ppermute(out_weight, "req", [(i, (i + 2 * d) % 8) for i in range(8)]) for d in range(1, 4)
    ]

    def over_y(array):
        return lax.ppermute(array, "req", [(i, i ^ 1) for i in range(8)])

    first = jnp.concatenate([w[:half] for w in ring], axis=0)
    second = jnp.concatenate([w[half:] for w in ring], axis=0)
    first = jnp.concatenate([first, over_y(first)], axis=0)
    second = jnp.concatenate([second, grp_move(second, 2)], axis=0)
    first = jnp.concatenate([first, grp_move(first, 2)], axis=0)
    second = jnp.concatenate([second, over_y(second)], axis=0)
    pieces = [first, second, grp_move(first, 1), grp_move(second, 1)]

    def moves(place_ref):
        req, grp = place_ref[0], place_ref[1]
        listing = []
        for number in range(4):
            for outer in range(2):
                for inner in range(2):
                    for d in range(4):
                        y_flip, x_flip = (inner, outer) if number % 2 == 0 else (outer, inner)
                        row = lax.rem(req + 8 - 2 * d, 8) ^ y_flip
                        col = grp ^ (2 * x_flip + number // 2)
                        target = (row * 4 + col) * part + (number % 2) * half
                        source = ((outer * 2 + inner) * 4 + d) * half
                        listing.append((number, source, half, pl.multiple_of(target, half)))
        return listing

    return pieces, moves


def local(
    suffix_queries,
    suffix_keys,
    suffix_values,
    prefix_cache,
    residual,
    out_weight,
    norm_gain,
    routes,
    route_weights,
    lengths,
    migrate,
    expert_gate,
    expert_up,
    expert_down,
    shared_gate,
    shared_up,
    shared_down,
    shared_router,
):
    rows = suffix_queries.shape[1]
    requests = lax.axis_size("req")
    req = lax.axis_index("req")
    grp = lax.axis_index("grp")
    depth = min(8, requests // 4)
    prefix_len = prefix_cache.shape[1] * requests
    capacity = rows * TOP * 5 // (4 * requests)
    place = jnp.stack([req, grp]).astype(jnp.int32)

    inverse = ROPE_BASE ** (-2.0 * np.arange(HD // 2) / HD)
    inverse = jnp.asarray(np.concatenate([inverse, inverse])[None].astype(np.float32))
    query_turned, own_cache = vmem_call(
        functools.partial(rope_kernel, prefix_len),
        [shape(rows, WIDTH), shape(rows, 2 * WIDTH)],
        [SMEM, SMEM] + [VMEM] * 4,
    )(lengths, place, inverse, suffix_queries[0], suffix_keys[0], suffix_values[0])

    prefix_rows = lax.all_gather(prefix_cache[0], "req", axis=0, tiled=True)
    history = [req_shift(own_cache, distance) for distance in range(1, depth + 1)]
    pieces, moves = gather_projection(out_weight, requests)

    attention = vmem_call(
        functools.partial(attend_kernel, depth),
        shape(rows, WIDTH),
        [SMEM, SMEM] + [VMEM] * (3 + depth),
    )(lengths, place, query_turned, prefix_rows, own_cache, *history)

    slots = requests * capacity
    state, normed, scale, outgoing = pl.pallas_call(
        functools.partial(project_kernel, requests, capacity, moves, len(pieces)),
        out_shape=[shape(rows, D, dtype=F32), shape(rows, D), shape(rows, HD, dtype=F32), shape(slots, D)],
        in_specs=[SMEM] + [VMEM] * 5 + [ANY] * len(pieces),
        out_specs=[VMEM] * 4,
        scratch_shapes=[pltpu.VMEM((WIDTH, D), BF16), pltpu.SemaphoreType.DMA],
        compiler_params=pltpu.CompilerParams(vmem_limit_bytes=32 << 20),
        cost_estimate=pl.CostEstimate(flops=2 * rows * WIDTH * D, bytes_accessed=8 << 20, transcendentals=0),
    )(place, attention, residual[0], norm_gain[None], shared_router[None], routes[0], *pieces)

    arrived = lax.all_to_all(
        outgoing.reshape(requests, capacity, D), "req", split_axis=0, concat_axis=0, tiled=True
    ).reshape(slots, D)

    mine = [jnp.swapaxes(expert_gate[0], 0, 1), jnp.swapaxes(expert_up[0], 0, 1), expert_down[0]]
    far = [grp_move(w, 2) for w in mine]
    shards = [mine, [grp_move(w, 1) for w in mine], far, [grp_move(w, 1) for w in far]]

    far_rows = grp_move(normed, 2)
    sib_rows = grp_move(normed, 1)
    far_sib_rows = grp_move(far_rows, 1)
    keep, send = ffn(
        [normed, far_rows, sib_rows, far_sib_rows],
        [jnp.swapaxes(shared_gate, 0, 1)],
        [jnp.swapaxes(shared_up, 0, 1)],
        [shared_down],
        [2 * rows, 2 * rows],
    )
    from_sib = grp_move(send, 1)
    pair_sum = (keep[rows:].astype(F32) + from_sib[rows:].astype(F32)).astype(BF16)
    from_far = grp_move(pair_sum, 2)

    (finished,) = ffn(
        [arrived], [s[0] for s in shards], [s[1] for s in shards], [s[2] for s in shards], [slots]
    )
    back = lax.all_to_all(
        finished.reshape(requests, capacity, D), "req", split_axis=0, concat_axis=0, tiled=True
    ).reshape(slots, D)

    final = vmem_call(
        functools.partial(combine_kernel, requests, capacity), shape(rows, D), [VMEM] * 8
    )(state, scale, routes[0], route_weights[0], back, keep, from_sib, from_far)

    partner = grp_move(own_cache, 2)
    pair_row = grp // 4 * 2 + grp % 2
    flags = jnp.sum(
        jnp.where((jnp.arange(migrate.shape[0], dtype=jnp.int32) == pair_row)[:, None], migrate, 0), axis=0
    )
    page_moved = jnp.repeat(flags, PG) == 1
    suffix_cache = jnp.where(page_moved[:, None], partner, own_cache)
    return (final[None], suffix_cache[None])


def solution(mesh):
    placed = (
        P("grp", "req", None),
        P("grp", "req", None),
        P("grp", "req", None),
        P("grp", "req", None),
        P("grp", "req", None),
        P(("req", "grp"), None),
        P(),
        P("grp", "req", None),
        P("grp", "req", None),
        P("grp", None),
        P(None, "req"),
        P("req", None, "grp"),
        P("req", None, "grp"),
        P("req", "grp", None),
        P(None, "grp"),
        P(None, "grp"),
        P("grp", None),
        P(),
    )
    return jax.shard_map(
        local,
        mesh=mesh,
        in_specs=placed,
        out_specs=(P("grp", "req", None), P("grp", "req", None)),
        check_vma=False,
    )
```

time: 393 us -> 256 us (0.65)
  local copies, waits for them, and re-layouts: 140 us -> 20.1 us
  matrix products: 45.1 us -> 0 us
  Pallas kernels: 0 us -> 40.2 us
  waiting for transfers between devices: 87.5 us -> 107 us
  other arithmetic: 23.1 us -> 4.29 us
  starting transfers between devices: 20.7 us -> 39.1 us
  blocking collectives: 59.1 us -> 43.2 us
  between operations: 14.4 us -> 1.04 us
    ppermute x3 -> x26, waiting for transfers between devices: 7.75 us -> 100 us  [the longest x19 87.3 us: grp_move(): lax.ppermute(array, 'grp', [(i, i ^ flip) for i in range(lax.axis_size('g...]
    scatter x1 -> x0, local copies, waits for them, and re-layouts: 92.3 us -> none  [local(): outgoing = jnp.zeros((request_devices, capacity, D), jnp.bfloat16).at[fla...]
    all_to_all x2, waiting for transfers between devices: 77.5 us -> 7.25 us  [the longest x1 5.37 us: local(): lax.all_to_all(finished.reshape(requests, capacity, D), 'req', split_axis...]
    dot_general x8 -> x0, matrix products: 42.8 us -> none  [the longest x1 13.6 us: expert_outputs(): jnp.dot(hidden, down_matrix, preferred_element_type=jnp.float32)]
    pallas_call x0 -> x6, Pallas kernels: none -> 40.2 us  [the longest x2 23 us: ffn(): pl.pallas_call(functools.partial(ffn_kernel, len(x_list), shards, len(out...]
    ppermute x3 -> x26, starting transfers between devices: 11.3 us -> 30.6 us  [the longest x19 10.8 us: grp_move(): lax.ppermute(array, 'grp', [(i, i ^ flip) for i in range(lax.axis_size('g...]
    all_gather x1, blocking collectives: 59.1 us -> 43.2 us  [local(): prefix_rows = lax.all_gather(prefix_cache[0], 'req', axis=0, tiled=True)]
    gather x1 -> x0, local copies, waits for them, and re-layouts: 13.1 us -> none  [local(): route_rows = returned[flat_experts, slot_index].astype(jnp.float32)]
  transfers between devices with their start and end apart: 11 -> 28, of which waited for: 3 -> 15; matrix products, arithmetic and copies ran while one was open for 48% -> 2% of each run, Pallas kernels for 0% -> 6%
where the time goes in v1:
time: 256 us; the launch traced here: 255 us
  waiting for transfers between devices  107 us (42%)
  blocking collectives  43.2 us (17%)
  Pallas kernels  40.2 us (16%)
  starting transfers between devices  39.1 us (15%)
  local copies, waits for them, and re-layouts  20.1 us (8%)
  other arithmetic  4.29 us (2%)
    ppermute x19, waiting for transfers between devices, grp_move(): lax.ppermute(array, 'grp', [(i, i ^ flip) for i in range(lax.axis_size('g...  87.3 us
    all_gather x1, blocking collectives, local(): prefix_rows = lax.all_gather(prefix_cache[0], 'req', axis=0, tiled=True)  43.2 us
    pallas_call x2, Pallas kernels, ffn(): pl.pallas_call(functools.partial(ffn_kernel, len(x_list), shards, len(out...  23 us
    unnamed x78, local copies, waits for them, and re-layouts  19.8 us
    ppermute x19, starting transfers between devices, grp_move(): lax.ppermute(array, 'grp', [(i, i ^ flip) for i in range(lax.axis_size('g...  10.8 us
    ppermute x2, starting transfers between devices, req_shift(): lax.ppermute(array, 'req', [(i - distance, i) for i in devices if i - dis...  9.54 us
    pallas_call x1, Pallas kernels, local(): pl.pallas_call(functools.partial(project_kernel, requests, capacity, move...  8.77 us
    ppermute x3, starting transfers between devices, gather_projection(): lax.ppermute(out_weight, 'req', [(i, (i + 2 * d) % 8) for i in range(8)])  7.01 us
  transfers between devices with their start and end apart: 28, of which 15 were waited for; matrix products, arithmetic and copies ran while one was open for 2% of the time, Pallas kernels for 6%

profile of v1, /device:TPU:0, one launch (start us, length us, event | category | flops | bytes accessed | tf_op | source)
XLA Modules:
  0.0 255.3 jit_solution(6206257823521395802)
XLA Ops:
  0.6 3.1 %collective-permute-start.2 = (bf16[32,2048]{1,0:T(8,128)(2,1)}, bf16[32,2048]{1,0:T(8,128)(2,1)S(1)}, u32[]{:S(2)}, u32[]{:S(2)}) collective-permute-start(bf16[32,2048]{1,0:T(8,128)(2,1)} %param.24), channel_id=1, source_target_pairs={{0,8},{4,12},{8,16},{12,20},{16,24},{20,28},{24,0},{28,4},{1,9},{5... | collective-permute-start | bytes 393224 | tf_op jit(solution)/shard_map/ppermute | solution.py:285
  3.7 2.6 %collective-permute-start.3 = (bf16[32,2048]{1,0:T(8,128)(2,1)}, bf16[32,2048]{1,0:T(8,128)(2,1)S(1)}, u32[]{:S(2)}, u32[]{:S(2)}) collective-permute-start(bf16[32,2048]{1,0:T(8,128)(2,1)} %param.24), channel_id=1, source_target_pairs={{0,16},{4,20},{8,24},{12,28},{16,0},{20,4},{24,8},{28,12},{1,17},{... | collective-permute-start | bytes 393224 | tf_op jit(solution)/shard_map/ppermute | solution.py:285
  10.4 4.8 %collective-permute-done.3 = bf16[32,2048]{1,0:T(8,128)(2,1)S(1)} collective-permute-done((bf16[32,2048]{1,0:T(8,128)(2,1)}, bf16[32,2048]{1,0:T(8,128)(2,1)S(1)}, u32[]{:S(2)}, u32[]{:S(2)}) %collective-permute-start.3) | collective-permute-done | bytes 131104 | tf_op jit(solution)/shard_map/ppermute | solution.py:285
  18.5 5.0 %collective-permute-done.5 = bf16[64,2048]{1,0:T(8,128)(2,1)S(1)} collective-permute-done((bf16[64,2048]{1,0:T(8,128)(2,1)S(1)}, bf16[64,2048]{1,0:T(8,128)(2,1)S(1)}, u32[]{:S(2)}, u32[]{:S(2)}) %collective-permute-start.5) | collective-permute-done | bytes 262176 | tf_op jit(solution)/shard_map/ppermute | solution.py:289
  26.8 9.8 %collective-permute-done.6 = bf16[128,2048]{1,0:T(8,128)(2,1)S(1)} collective-permute-done((bf16[128,2048]{1,0:T(8,128)(2,1)S(1)}, bf16[128,2048]{1,0:T(8,128)(2,1)S(1)}, u32[]{:S(2)}, u32[]{:S(2)}) %collective-permute-start.6) | collective-permute-done | bytes 524320 | tf_op jit(solution)/shard_map/ppermute | solution.py:270
  39.2 4.2 %collective-permute-start = (bf16[128,2048]{1,0:T(8,128)(2,1)S(1)}, bf16[128,2048]{1,0:T(8,128)(2,1)}, u32[]{:S(2)}, u32[]{:S(2)}) collective-permute-start(bf16[128,2048]{1,0:T(8,128)(2,1)S(1)} %get-tuple-element.11.refs_0_), channel_id=1, source_target_pairs={{0,4},{4,8},{8,12},{12,16},{16,20},{20,24},{24,28},{1,5},{5,9},{9,... | collective-permute-start | bytes 1572872 | tf_op jit(solution)/shard_map/ppermute | solution.py:275
  43.5 5.3 %collective-permute-start.1 = (bf16[128,2048]{1,0:T(8,128)(2,1)S(1)}, bf16[128,2048]{1,0:T(8,128)(2,1)}, u32[]{:S(2)}, u32[]{:S(2)}) collective-permute-start(bf16[128,2048]{1,0:T(8,128)(2,1)S(1)} %get-tuple-element.11.refs_0_), channel_id=1, source_target_pairs={{0,8},{4,12},{8,16},{12,20},{16,24},{20,28},{1,9},{5,13},{9,17},{1... | collective-permute-start | bytes 1572872 | tf_op jit(solution)/shard_map/ppermute | solution.py:275
  48.8 43.2 %all-gather = bf16[1,32,2048]{2,0,1:T(2,128)(2,1)S(1)} all-gather(bf16[1,4,2048]{2,0,1:T(2,128)(2,1)S(1)} %copy.26), channel_id=2, replica_groups=mesh['req'=8,'grp'=4] {'req'}, dimensions={1}, use_global_device_ids=true | all-gather | bytes 147456 | tf_op jit(solution)/shard_map/all_gather | solution.py:354
  93.2 3.7 %shard_map.195.attn_ref = bf16[128,1024]{1,0:T(8,128)(2,1)S(1)} custom-call(s32[1,16]{1,0:T(1,128)S(1)} %copy-done.11, s32[2]{0:T(128)S(1)} %pad_add_fusion.place_ref, bf16[128,1024]{1,0:T(8,128)(2,1)S(1)} %copy-done.9, bf16[32,2048]{1,0:T(8,128)(2,1)S(1)} %bitcast.31, bf16[128,2048]{1,0:T(8,128)(2,1)S(1)} %get-tuple-element.11.refs_0_, ...), custom_call_target="tpu_custom_call" | custom-call | bytes 4194304 | tf_op jit(solution)/shard_map/pallas_call | solution.py:358
  98.0 8.8 %shard_map.196 = (f32[128,2048]{1,0:T(8,128)S(1)}, bf16[128,2048]{1,0:T(8,128)(2,1)S(1)}, f32[128,128]{1,0:T(8,128)S(1)}, bf16[640,2048]{1,0:T(8,128)(2,1)}) custom-call(s32[2]{0:T(128)S(1)} %pad_add_fusion.place_ref, bf16[128,1024]{1,0:T(8,128)(2,1)S(1)} %shard_map.195.attn_ref, bf16[128,2048]{1,0:T(8,128)(2,1)S(1)} %bitcast.32, f32[1,2048]{1,0:T(1,128)S(1)} %bitcast.37, ...), custom_call_target="tpu_custom_call" | custom-call | flops 536870912 | bytes 8388608 | tf_op jit(solution)/shard_map/pallas_call | solution.py:365
  108.6 4.5 %all-to-all-start = ((bf16[8,80,2048]{2,1,0:T(8,128)(2,1)}), bf16[8,80,2048]{2,1,0:T(8,128)(2,1)}, u32[]{:S(2)}, u32[]{:S(2)}) async-start(bf16[8,80,2048]{2,1,0:T(8,128)(2,1)} %bitcast.9), calls=%async_computation | async-start | bytes 5242880 | tf_op jit(solution)/shard_map/all_to_all | solution.py:375
  117.0 15.2 %collective-permute-done.12.refs_3_ = bf16[176,2048]{1,0:T(8,128)(2,1)S(1)} collective-permute-done((bf16[176,2048]{1,0:T(8,128)(2,1)S(1)}, bf16[176,2048]{1,0:T(8,128)(2,1)S(1)}, u32[]{:S(2)}, u32[]{:S(2)}) %collective-permute-start.12) | collective-permute-done | bytes 720928 | tf_op jit(solution)/shard_map/ppermute | solution.py:270
  133.1 14.6 %collective-permute-done.15.refs_7_ = bf16[176,2048]{1,0:T(8,128)(2,1)S(1)} collective-permute-done((bf16[176,2048]{1,0:T(8,128)(2,1)S(1)}, bf16[176,2048]{1,0:T(8,128)(2,1)S(1)}, u32[]{:S(2)}, u32[]{:S(2)}) %collective-permute-start.15) | collective-permute-done | bytes 720928 | tf_op jit(solution)/shard_map/ppermute | solution.py:270
  148.5 14.1 %collective-permute-done.18.refs_11_ = bf16[176,2048]{1,0:T(8,128)(2,1)S(1)} collective-permute-done((bf16[176,2048]{1,0:T(8,128)(2,1)S(1)}, bf16[176,2048]{1,0:T(8,128)(2,1)S(1)}, u32[]{:S(2)}, u32[]{:S(2)}) %collective-permute-start.18) | collective-permute-done | bytes 720928 | tf_op jit(solution)/shard_map/ppermute | solution.py:270
  173.0 12.1 %shard_map.197 = bf16[640,2048]{1,0:T(8,128)(2,1)} custom-call(bf16[640,2048]{1,0:T(8,128)(2,1)} %bitcast.10.refs_0_, bf16[176,2048]{1,0:T(8,128)(2,1)S(1)} %bitcast.40, bf16[176,2048]{1,0:T(8,128)(2,1)S(1)} %collective-permute-done.11.refs_2_, bf16[176,2048]{1,0:T(8,128)(2,1)S(1)} %copy-done.16, bf16[176,2048]{1,0:T(8,128)(2,1)S(1)} %copy-done.22, ...), custom_call_target="tpu_custom_call" | custom-call | flops 6039797760 | bytes 14680064 | tf_op jit(solution)/shard_map/pallas_call | solution.py:198
  185.1 4.0 %all-to-all-start.1 = ((bf16[8,80,2048]{2,1,0:T(8,128)(2,1)}), bf16[8,80,2048]{2,1,0:T(8,128)(2,1)S(1)}, u32[]{:S(2)}, u32[]{:S(2)}) async-start(bf16[8,80,2048]{2,1,0:T(8,128)(2,1)} %bitcast.44), calls=%async_computation.1 | async-start | bytes 5242880 | tf_op jit(solution)/shard_map/all_to_all | solution.py:400
  190.3 13.0 %collective-permute-done.20.refs_1_ = bf16[128,2048]{1,0:T(8,128)(2,1)S(1)} collective-permute-done((bf16[128,2048]{1,0:T(8,128)(2,1)}, bf16[128,2048]{1,0:T(8,128)(2,1)S(1)}, u32[]{:S(2)}, u32[]{:S(2)}) %collective-permute-start.20) | collective-permute-done | bytes 524320 | tf_op jit(solution)/shard_map/ppermute | solution.py:270
  206.3 10.9 %shard_map.198 = (bf16[256,2048]{1,0:T(8,128)(2,1)S(1)}, bf16[256,2048]{1,0:T(8,128)(2,1)}) custom-call(bf16[128,2048]{1,0:T(8,128)(2,1)S(1)} %copy-done.26, bf16[128,2048]{1,0:T(8,128)(2,1)S(1)} %collective-permute-done.20.refs_1_, bf16[128,2048]{1,0:T(8,128)(2,1)S(1)} %collective-permute-done.21.refs_2_, ...), custom_call_target="tpu_custom_call" | custom-call | flops 4831838208 | bytes 13631488 | tf_op jit(solution)/shard_map/pallas_call | solution.py:198
  221.2 2.1 add_convert_fusion
  224.7 8.4 %collective-permute-done.25 = bf16[128,2048]{1,0:T(8,128)(2,1)} collective-permute-done((bf16[128,2048]{1,0:T(8,128)(2,1)S(1)}, bf16[128,2048]{1,0:T(8,128)(2,1)}, u32[]{:S(2)}, u32[]{:S(2)}) %collective-permute-start.25) | collective-permute-done | bytes 524320 | tf_op jit(solution)/shard_map/ppermute | solution.py:270
  233.1 2.0 select_bitcast_fusion
  235.1 8.7 %collective-permute-done.24.far_ref = bf16[128,2048]{1,0:T(8,128)(2,1)} collective-permute-done((bf16[128,2048]{1,0:T(8,128)(2,1)}, bf16[128,2048]{1,0:T(8,128)(2,1)}, u32[]{:S(2)}, u32[]{:S(2)}) %collective-permute-start.24) | collective-permute-done | bytes 524320 | tf_op jit(solution)/shard_map/ppermute | solution.py:270
  243.8 5.4 %all-to-all-done.1 = bf16[8,80,2048]{2,1,0:T(8,128)(2,1)S(1)} async-done(((bf16[8,80,2048]{2,1,0:T(8,128)(2,1)}), bf16[8,80,2048]{2,1,0:T(8,128)(2,1)S(1)}, u32[]{:S(2)}, u32[]{:S(2)}) %all-to-all-start.1) | async-done | bytes 2621472 | tf_op jit(solution)/shard_map/all_to_all | solution.py:400
  251.7 3.6 %shard_map.199 = bf16[128,2048]{1,0:T(8,128)(2,1)} custom-call(f32[128,2048]{1,0:T(8,128)S(1)} %copy-done.3, f32[128,128]{1,0:T(8,128)S(1)} %get-tuple-element.13.scale_ref, s32[128,4]{1,0:T(8,128)S(1)} %bitcast.30, f32[128,4]{1,0:T(8,128)S(1)} %bitcast.33, bf16[640,2048]{1,0:T(8,128)(2,1)S(1)} %bitcast.28, bf16[256,2048]{1,0:T(8,128)(2,1)S(1)} %copy-done.1, ...), custom_call_target="tpu_custom_call" | custom-call | bytes 4194304 | tf_op jit(solution)/shard_map/pallas_call | solution.py:404
  (132 shorter events, 45.2 us)
Async XLA Ops:
  0.6 9.7 %collective-permute-start.2 = (bf16[32,2048]{1,0:T(8,128)(2,1)}, bf16[32,2048]{1,0:T(8,128)(2,1)S(1)}, u32[]{:S(2)}, u32[]{:S(2)}) collective-permute-start(bf16[32,2048]{1,0:T(8,128)(2,1)} %param.24), channel_id=1, source_target_pairs={{0,8},{4,12},{8,16},{12,20},{16,24},{20,28},{24,0},{28,4},{1,9},{5... | collective-permute-start | bytes 393224 | tf_op jit(solution)/shard_map/ppermute | solution.py:285
  3.7 11.4 %collective-permute-start.3 = (bf16[32,2048]{1,0:T(8,128)(2,1)}, bf16[32,2048]{1,0:T(8,128)(2,1)S(1)}, u32[]{:S(2)}, u32[]{:S(2)}) collective-permute-start(bf16[32,2048]{1,0:T(8,128)(2,1)} %param.24), channel_id=1, source_target_pairs={{0,16},{4,20},{8,24},{12,28},{16,0},{20,4},{24,8},{28,12},{1,17},{... | collective-permute-start | bytes 393224 | tf_op jit(solution)/shard_map/ppermute | solution.py:285
  6.3 8.9 %collective-permute-start.4 = (bf16[32,2048]{1,0:T(8,128)(2,1)}, bf16[32,2048]{1,0:T(8,128)(2,1)S(1)}, u32[]{:S(2)}, u32[]{:S(2)}) collective-permute-start(bf16[32,2048]{1,0:T(8,128)(2,1)} %param.24), channel_id=1, source_target_pairs={{0,24},{4,28},{8,0},{12,4},{16,8},{20,12},{24,16},{28,20},{1,25},{... | collective-permute-start | bytes 393224 | tf_op jit(solution)/shard_map/ppermute | solution.py:285
  15.3 8.2 %collective-permute-start.5 = (bf16[64,2048]{1,0:T(8,128)(2,1)S(1)}, bf16[64,2048]{1,0:T(8,128)(2,1)S(1)}, u32[]{:S(2)}, u32[]{:S(2)}) collective-permute-start(bf16[64,2048]{1,0:T(8,128)(2,1)S(1)} %pad_maximum_fusion), channel_id=1, source_target_pairs={{0,4},{4,0},{8,12},{12,8},{16,20},{20,16},{24,28},{28,24},{1,5},{5... | collective-permute-start | bytes 786440 | tf_op jit(solution)/shard_map/ppermute | solution.py:289
  16.9 8.2 %collective-permute-start.7 = (bf16[64,2048]{1,0:T(8,128)(2,1)S(1)}, bf16[64,2048]{1,0:T(8,128)(2,1)S(1)}, u32[]{:S(2)}, u32[]{:S(2)}) collective-permute-start(bf16[64,2048]{1,0:T(8,128)(2,1)S(1)} %pad_maximum_fusion.1), channel_id=1, source_target_pairs={{0,2},{1,3},{2,0},{3,1},{4,6},{5,7},{6,4},{7,5},{8,10},{9,11},{10,... | collective-permute-start | bytes 786440 | tf_op jit(solution)/shard_map/ppermute | solution.py:270
  23.6 13.0 %collective-permute-start.6 = (bf16[128,2048]{1,0:T(8,128)(2,1)S(1)}, bf16[128,2048]{1,0:T(8,128)(2,1)S(1)}, u32[]{:S(2)}, u32[]{:S(2)}) collective-permute-start(bf16[128,2048]{1,0:T(8,128)(2,1)S(1)} %get-tuple-element.20), channel_id=1, source_target_pairs={{0,2},{1,3},{2,0},{3,1},{4,6},{5,7},{6,4},{7,5},{8,10},{9,11},{10,... | collective-permute-start | bytes 1572872 | tf_op jit(solution)/shard_map/ppermute | solution.py:270
  25.2 12.7 %collective-permute-start.8 = (bf16[128,2048]{1,0:T(8,128)(2,1)S(1)}, bf16[128,2048]{1,0:T(8,128)(2,1)S(1)}, u32[]{:S(2)}, u32[]{:S(2)}) collective-permute-start(bf16[128,2048]{1,0:T(8,128)(2,1)S(1)} %get-tuple-element.18), channel_id=1, source_target_pairs={{0,4},{4,0},{8,12},{12,8},{16,20},{20,16},{24,28},{28,24},{1,5},{5... | collective-permute-start | bytes 1572872 | tf_op jit(solution)/shard_map/ppermute | solution.py:289
  36.6 60.3 %collective-permute-start.9 = (bf16[256,2048]{1,0:T(8,128)(2,1)S(1)}, bf16[256,2048]{1,0:T(8,128)(2,1)}, u32[]{:S(2)}, u32[]{:S(2)}) collective-permute-start(bf16[256,2048]{1,0:T(8,128)(2,1)S(1)} %constant_dynamic-update-slice_fusion.5.refs_0_), channel_id=1, source_target_pairs={{0,1},{1,0},{2,3},{3,2},{4,5},{5,4},{6,7},{7,6},{8,9},{9,8},{10,11... | collective-permute-start | bytes 3145736 | tf_op jit(solution)/shard_map/ppermute | solution.py:270
  37.9 59.0 %collective-permute-start.10 = (bf16[256,2048]{1,0:T(8,128)(2,1)S(1)}, bf16[256,2048]{1,0:T(8,128)(2,1)}, u32[]{:S(2)}, u32[]{:S(2)}) collective-permute-start(bf16[256,2048]{1,0:T(8,128)(2,1)S(1)} %constant_dynamic-update-slice_fusion.16.refs_1_), channel_id=1, source_target_pairs={{0,1},{1,0},{2,3},{3,2},{4,5},{5,4},{6,7},{7,6},{8,9},{9,8},{10,11... | collective-permute-start | bytes 3145736 | tf_op jit(solution)/shard_map/ppermute | solution.py:270
  39.2 53.0 %collective-permute-start = (bf16[128,2048]{1,0:T(8,128)(2,1)S(1)}, bf16[128,2048]{1,0:T(8,128)(2,1)}, u32[]{:S(2)}, u32[]{:S(2)}) collective-permute-start(bf16[128,2048]{1,0:T(8,128)(2,1)S(1)} %get-tuple-element.11.refs_0_), channel_id=1, source_target_pairs={{0,4},{4,8},{8,12},{12,16},{16,20},{20,24},{24,28},{1,5},{5,9},{9,... | collective-permute-start | bytes 1572872 | tf_op jit(solution)/shard_map/ppermute | solution.py:275
  43.5 48.8 %collective-permute-start.1 = (bf16[128,2048]{1,0:T(8,128)(2,1)S(1)}, bf16[128,2048]{1,0:T(8,128)(2,1)}, u32[]{:S(2)}, u32[]{:S(2)}) collective-permute-start(bf16[128,2048]{1,0:T(8,128)(2,1)S(1)} %get-tuple-element.11.refs_0_), channel_id=1, source_target_pairs={{0,8},{4,12},{8,16},{12,20},{16,24},{20,28},{1,9},{5,13},{9,17},{1... | collective-permute-start | bytes 1572872 | tf_op jit(solution)/shard_map/ppermute | solution.py:275
  108.6 58.9 %all-to-all-start = ((bf16[8,80,2048]{2,1,0:T(8,128)(2,1)}), bf16[8,80,2048]{2,1,0:T(8,128)(2,1)}, u32[]{:S(2)}, u32[]{:S(2)}) async-start(bf16[8,80,2048]{2,1,0:T(8,128)(2,1)} %bitcast.9), calls=%async_computation | async-start | bytes 5242880 | tf_op jit(solution)/shard_map/all_to_all | solution.py:375
  113.2 19.0 %collective-permute-start.12 = (bf16[176,2048]{1,0:T(8,128)(2,1)S(1)}, bf16[176,2048]{1,0:T(8,128)(2,1)S(1)}, u32[]{:S(2)}, u32[]{:S(2)}) collective-permute-start(bf16[176,2048]{1,0:T(8,128)(2,1)S(1)} %bitcast.39), channel_id=1, source_target_pairs={{0,2},{1,3},{2,0},{3,1},{4,6},{5,7},{6,4},{7,5},{8,10},{9,11},{10,... | collective-permute-start | bytes 2162696 | tf_op jit(solution)/shard_map/ppermute | solution.py:270
  114.5 33.2 %collective-permute-start.15 = (bf16[176,2048]{1,0:T(8,128)(2,1)S(1)}, bf16[176,2048]{1,0:T(8,128)(2,1)S(1)}, u32[]{:S(2)}, u32[]{:S(2)}) collective-permute-start(bf16[176,2048]{1,0:T(8,128)(2,1)S(1)} %bitcast.41), channel_id=1, source_target_pairs={{0,2},{1,3},{2,0},{3,1},{4,6},{5,7},{6,4},{7,5},{8,10},{9,11},{10,... | collective-permute-start | bytes 2162696 | tf_op jit(solution)/shard_map/ppermute | solution.py:270
  115.3 47.4 %collective-permute-start.18 = (bf16[176,2048]{1,0:T(8,128)(2,1)S(1)}, bf16[176,2048]{1,0:T(8,128)(2,1)S(1)}, u32[]{:S(2)}, u32[]{:S(2)}) collective-permute-start(bf16[176,2048]{1,0:T(8,128)(2,1)S(1)} %bitcast.49), channel_id=1, source_target_pairs={{0,2},{1,3},{2,0},{3,1},{4,6},{5,7},{6,4},{7,5},{8,10},{9,11},{10,... | collective-permute-start | bytes 2162696 | tf_op jit(solution)/shard_map/ppermute | solution.py:270
  116.5 46.2 %collective-permute-start.14 = (bf16[176,2048]{1,0:T(8,128)(2,1)S(1)}, bf16[176,2048]{1,0:T(8,128)(2,1)S(1)}, u32[]{:S(2)}, u32[]{:S(2)}) collective-permute-start(bf16[176,2048]{1,0:T(8,128)(2,1)S(1)} %bitcast.42), channel_id=1, source_target_pairs={{0,1},{1,0},{2,3},{3,2},{4,5},{5,4},{6,7},{7,6},{8,9},{9,8},{10,11... | collective-permute-start | bytes 2162696 | tf_op jit(solution)/shard_map/ppermute | solution.py:270
  116.5 47.1 %collective-permute-start.17 = (bf16[176,2048]{1,0:T(8,128)(2,1)S(1)}, bf16[176,2048]{1,0:T(8,128)(2,1)S(1)}, u32[]{:S(2)}, u32[]{:S(2)}) collective-permute-start(bf16[176,2048]{1,0:T(8,128)(2,1)S(1)} %bitcast.50), channel_id=1, source_target_pairs={{0,1},{1,0},{2,3},{3,2},{4,5},{5,4},{6,7},{7,6},{8,9},{9,8},{10,11... | collective-permute-start | bytes 2162696 | tf_op jit(solution)/shard_map/ppermute | solution.py:270
  132.2 31.4 %collective-permute-start.13 = (bf16[176,2048]{1,0:T(8,128)(2,1)S(1)}, bf16[176,2048]{1,0:T(8,128)(2,1)S(1)}, u32[]{:S(2)}, u32[]{:S(2)}) collective-permute-start(bf16[176,2048]{1,0:T(8,128)(2,1)S(1)} %collective-permute-done.12.refs_3_), channel_id=1, source_target_pairs={{0,1},{1,0},{2,3},{3,2},{4,5},{5,4},{6,7},{7,6},{8,9},{9,8},{10,11... | collective-permute-start | bytes 2162696 | tf_op jit(solution)/shard_map/ppermute | solution.py:270
  147.7 16.8 %collective-permute-start.16 = (bf16[176,2048]{1,0:T(8,128)(2,1)S(1)}, bf16[176,2048]{1,0:T(8,128)(2,1)S(1)}, u32[]{:S(2)}, u32[]{:S(2)}) collective-permute-start(bf16[176,2048]{1,0:T(8,128)(2,1)S(1)} %collective-permute-done.15.refs_7_), channel_id=1, source_target_pairs={{0,1},{1,0},{2,3},{3,2},{4,5},{5,4},{6,7},{7,6},{8,9},{9,8},{10,11... | collective-permute-start | bytes 2162696 | tf_op jit(solution)/shard_map/ppermute | solution.py:270
  185.1 64.1 %all-to-all-start.1 = ((bf16[8,80,2048]{2,1,0:T(8,128)(2,1)}), bf16[8,80,2048]{2,1,0:T(8,128)(2,1)S(1)}, u32[]{:S(2)}, u32[]{:S(2)}) async-start(bf16[8,80,2048]{2,1,0:T(8,128)(2,1)} %bitcast.44), calls=%async_computation.1 | async-start | bytes 5242880 | tf_op jit(solution)/shard_map/all_to_all | solution.py:400
  189.1 14.2 %collective-permute-start.20 = (bf16[128,2048]{1,0:T(8,128)(2,1)}, bf16[128,2048]{1,0:T(8,128)(2,1)S(1)}, u32[]{:S(2)}, u32[]{:S(2)}) collective-permute-start(bf16[128,2048]{1,0:T(8,128)(2,1)} %copy-done.25), channel_id=1, source_target_pairs={{0,2},{1,3},{2,0},{3,1},{4,6},{5,7},{6,4},{7,5},{8,10},{9,11},{10,... | collective-permute-start | bytes 1572872 | tf_op jit(solution)/shard_map/ppermute | solution.py:270
  190.3 13.0 %collective-permute-start.21 = (bf16[128,2048]{1,0:T(8,128)(2,1)}, bf16[128,2048]{1,0:T(8,128)(2,1)S(1)}, u32[]{:S(2)}, u32[]{:S(2)}) collective-permute-start(bf16[128,2048]{1,0:T(8,128)(2,1)} %copy-done.25), channel_id=1, source_target_pairs={{0,1},{1,0},{2,3},{3,2},{4,5},{5,4},{6,7},{7,6},{8,9},{9,8},{10,11... | collective-permute-start | bytes 1572872 | tf_op jit(solution)/shard_map/ppermute | solution.py:270
  218.3 14.9 %collective-permute-start.25 = (bf16[128,2048]{1,0:T(8,128)(2,1)S(1)}, bf16[128,2048]{1,0:T(8,128)(2,1)}, u32[]{:S(2)}, u32[]{:S(2)}) collective-permute-start(bf16[128,2048]{1,0:T(8,128)(2,1)S(1)} %get-tuple-element.11.refs_0_), channel_id=1, source_target_pairs={{0,2},{1,3},{2,0},{3,1},{4,6},{5,7},{6,4},{7,5},{8,10},{9,11},{10,... | collective-permute-start | bytes 1572872 | tf_op jit(solution)/shard_map/ppermute | solution.py:270
  223.3 20.6 %collective-permute-start.24 = (bf16[128,2048]{1,0:T(8,128)(2,1)}, bf16[128,2048]{1,0:T(8,128)(2,1)}, u32[]{:S(2)}, u32[]{:S(2)}) collective-permute-start(bf16[128,2048]{1,0:T(8,128)(2,1)} %add_convert_fusion), channel_id=1, source_target_pairs={{0,2},{1,3},{2,0},{3,1},{4,6},{5,7},{6,4},{7,5},{8,10},{9,11},{10,... | collective-permute-start | bytes 1572872 | tf_op jit(solution)/shard_map/ppermute | solution.py:270
  (39 other events, 485.7 us)

commit v2 on v1

v2 whole, which is shorter than its diff:
```python
import functools
import math

import jax
import jax.numpy as jnp
import numpy as np
from jax import lax
from jax.experimental import pallas as pl
from jax.experimental.pallas import tpu as pltpu
from jax.sharding import PartitionSpec as P

D = 2048
HD = 128
HEADS = 8
WIDTH = HEADS * HD
TOP = 4
PG = 16
ROPE_BASE = 1000000.0
EPSILON = 1e-06
ATTEND_COST = 20_000_000_000
F32 = jnp.float32
BF16 = jnp.bfloat16
VMEM = pl.BlockSpec(memory_space=pltpu.VMEM)
SMEM = pl.BlockSpec(memory_space=pltpu.SMEM)
HBM = pl.BlockSpec(memory_space=pltpu.HBM)
ANY = pl.BlockSpec(memory_space=pl.ANY)
NT = (((1,), (1,)), ((), ()))


def request_starts(lengths_ref, token_ids):
    start = jnp.zeros_like(token_ids)
    end = jnp.int32(0)
    for request in range(lengths_ref.shape[1]):
        end = end + lengths_ref[0, request]
        start = jnp.where(token_ids >= end, end, start)
    return start


def rope_kernel(prefix_len, lengths_ref, place_ref, inv_ref, q_ref, k_ref, v_ref, turned_ref, cache_ref):
    rows = q_ref.shape[0]
    shape = (rows, HD)
    token_ids = place_ref[0] * rows + lax.broadcasted_iota(jnp.int32, shape, 0)
    offset = token_ids - request_starts(lengths_ref, token_ids)
    angles = (prefix_len + offset).astype(F32) * inv_ref[...]
    cosine = jnp.cos(angles)
    sine = jnp.sin(angles)
    sine = jnp.where(lax.broadcasted_iota(jnp.int32, shape, 1) < HD // 2, -sine, sine)
    for head in range(HEADS):
        cols = slice(head * HD, (head + 1) * HD)
        for source, target in ((q_ref, turned_ref), (k_ref, cache_ref)):
            entries = source[:, cols].astype(F32)
            turned = entries * cosine + pltpu.roll(entries, HD // 2, 1) * sine
            target[:, cols] = turned.astype(BF16)
    cache_ref[:, WIDTH:] = v_ref[...]


def attend_kernel(depth, lengths_ref, place_ref, q_ref, prefix_ref, *refs):
    blocks, order, out_ref = refs[: depth + 1], refs[depth + 1 : -1], refs[-1]
    rows = q_ref.shape[0]
    prefix_len = prefix_ref.shape[0]
    first = place_ref[0] * rows
    ids = lax.broadcasted_iota(jnp.int32, (rows, rows), 0) + first
    start = request_starts(lengths_ref, ids)
    allowed = [jnp.ones((rows, prefix_len), jnp.bool_)]
    for distance in range(depth + 1):
        keys = lax.broadcasted_iota(jnp.int32, (rows, rows), 1) + (first - distance * rows)
        allowed.append((keys <= ids) & (keys >= start))
    bias = jnp.concatenate([jnp.where(a, 0.0, -1e30) for a in allowed], axis=1)
    keep = bias == 0.0
    sources = (prefix_ref,) + blocks
    for head in range(HEADS):
        cols = slice(head * HD, (head + 1) * HD)
        values_at = slice(WIDTH + head * HD, WIDTH + (head + 1) * HD)
        keys = jnp.concatenate([s[:, cols] for s in sources], axis=0)
        values = jnp.concatenate([s[:, values_at] for s in sources], axis=0)
        scores = lax.dot_general(q_ref[:, cols], keys, NT, preferred_element_type=F32)
        scores = jnp.where(keep, scores * HD ** (-0.5), -1e30)
        highest = jnp.max(scores, axis=1, keepdims=True)
        weights = jnp.where(keep, jnp.exp(scores - highest), 0.0)
        total = jnp.sum(weights, axis=1, keepdims=True)
        blended = jnp.dot(weights.astype(BF16), values, preferred_element_type=F32) / total
        out_ref[:, cols] = blended.astype(BF16)
    if order:
        out_ref[...] = jnp.dot(out_ref[...], order[0][...], preferred_element_type=F32).astype(BF16)


def route_kernel(experts, parts, base_ref, routing_ref, pick_ref, high_ref, low_ref):
    rows = routing_ref.shape[0]
    numbers = (lax.broadcasted_iota(jnp.int32, (rows, experts), 1) + base_ref[0]).astype(F32)
    found = [routing_ref[:, k : k + 1] == numbers for k in range(TOP)]
    member = jnp.where(found[0] | found[1] | found[2] | found[3], 1.0, 0.0)
    above = lax.broadcasted_iota(jnp.int32, (rows, rows), 0) > lax.broadcasted_iota(
        jnp.int32, (rows, rows), 1
    )
    rank = jnp.dot(
        jnp.where(above, 1.0, 0.0).astype(BF16), member.astype(BF16), preferred_element_type=F32
    )
    rank = jnp.where(member > 0.5, rank, -1.0).astype(BF16)
    weight = jnp.zeros(member.shape, F32)
    for k in range(TOP):
        weight = weight + jnp.where(found[k], routing_ref[:, TOP + k : TOP + k + 1], 0.0)
    high = weight.astype(BF16)
    low = (weight - high.astype(F32)).astype(BF16)
    at = 0
    for first, count in parts:
        slots = experts * count

        def layout(dims, dim):
            slot = lax.broadcasted_iota(jnp.int32, dims, dim).astype(F32)
            expert = jnp.floor((slot + 0.5) * (1.0 / count))
            return expert, slot - expert * count + first

        expert, place = layout((slots, rows), 0)
        expert_column = layout((slots, experts), 0)[0]
        columns = lax.broadcasted_iota(jnp.int32, (slots, experts), 1).astype(F32)
        select = jnp.where(expert_column == columns, 1.0, 0.0).astype(BF16)
        wanted = lax.dot_general(select, rank, NT, preferred_element_type=F32)
        pick_ref[at : at + slots, :] = jnp.where(wanted == place, 1.0, 0.0).astype(BF16)
        expert_row = layout((experts, slots), 1)[0]
        lines = lax.broadcasted_iota(jnp.int32, (experts, slots), 0).astype(F32)
        select = jnp.where(expert_row == lines, 1.0, 0.0).astype(BF16)
        mine = jnp.dot(rank, select, preferred_element_type=F32) == layout((rows, slots), 1)[1]
        for part, target in ((high, high_ref), (low, low_ref)):
            spread = jnp.dot(part, select, preferred_element_type=F32)
            target[:, at : at + slots] = jnp.where(mine, spread, 0.0).astype(BF16)
        at += slots


def project_kernel(count, attn_ref, residual_ref, gain_ref, router_ref, pick_ref, *refs):
    pieces, refs = refs[:count], refs[count:]
    normed_out, state_out, slots_out, normed_rows, state, picked, sems = refs
    step = 512
    square = jnp.zeros((attn_ref.shape[0], 1), F32)
    moves = []

    def move(source, target, kind, at, size=step):
        window = (slice(None), pl.ds(at, size))
        moves.append(pltpu.make_async_copy(source.at[window], target.at[window], sems.at[kind, at // step]))
        moves[-1].start()

    for at in range(0, D, step):
        cols = slice(at, at + step)
        part = residual_ref[:, cols].astype(F32)
        row = 0
        for piece in pieces:
            deep = piece.shape[0]
            part = part + jnp.dot(
                attn_ref[:, row : row + deep], piece[:, cols], preferred_element_type=F32
            )
            row += deep
        state[:, cols] = part
        move(state, state_out, 0, at)
        square = square + jnp.sum(part * part, axis=1, keepdims=True)
    factor = lax.rsqrt(square * (1.0 / D) + EPSILON)
    logit = jnp.zeros_like(square)
    for at in range(0, D, step):
        cols = slice(at, at + step)
        normed = (state[:, cols] * factor * gain_ref[:, cols]).astype(BF16)
        normed_rows[:, cols] = normed
        move(normed_rows, normed_out, 2, at)
        logit = logit + jnp.sum(
            normed.astype(F32) * router_ref[:, cols].astype(F32), axis=1, keepdims=True
        )
        picked[:, cols] = jnp.dot(pick_ref[...], normed, preferred_element_type=F32).astype(BF16)
        move(picked, slots_out, 1, at)
    state[:, D:] = jnp.broadcast_to(jax.nn.sigmoid(logit), (state.shape[0], HD))
    move(state, state_out, 0, D, HD)
    for copy in moves:
        copy.wait()


def ffn_kernel(xs, shards, outs, *refs):
    x_refs, refs = refs[:xs], refs[xs:]
    sources, refs = [refs[kind * shards : (kind + 1) * shards] for kind in range(3)], refs[3 * shards :]
    out_refs, refs = refs[:outs], refs[outs:]
    x, *weights, hidden, result, sems = refs
    gate, up, down = weights
    chunk = 256
    hid = gate.shape[0]
    steps = [(at, min(chunk, hid - at)) for at in range(0, hid, chunk)]
    x_copies = []
    at = 0
    for number, ref in enumerate(x_refs):
        x_copies.append(pltpu.make_async_copy(ref, x.at[pl.ds(at, ref.shape[0])], sems.at[4, number]))
        at += ref.shape[0]
    size = hid // shards
    loads = [(shard, first) for shard in range(shards) for first in range(0, size, size if shards > 1 else chunk)]
    copies = [[], [], []]
    ends = []
    for number, (shard, first) in enumerate(loads):
        count = size if shards > 1 else min(chunk, size - first)
        ends.append(shard * size + first + count)
        for kind in range(3):
            copies[kind].append(
                pltpu.make_async_copy(
                    sources[kind][shard].at[pl.ds(first, count)],
                    weights[kind].at[pl.ds(shard * size + first, count)],
                    sems.at[kind, number],
                )
            )
    for copy in x_copies:
        copy.start()
    for pair in zip(copies[0], copies[1]):
        for copy in pair:
            copy.start()
    for copy in copies[2]:
        copy.start()
    for copy in x_copies:
        copy.wait()
    ready = 0
    for first, count in steps:
        while ready < len(ends) and (ready == 0 or ends[ready - 1] < first + count):
            copies[0][ready].wait()
            copies[1][ready].wait()
            ready += 1
        rows = slice(first, first + count)
        g = lax.dot_general(x[...], gate[rows, :], NT, preferred_element_type=F32)
        u = lax.dot_general(x[...], up[rows, :], NT, preferred_element_type=F32)
        hidden[:, rows] = (g / (1.0 + jnp.exp(-g)) * u).astype(BF16)
    for copy in copies[2]:
        copy.wait()
    moves = []
    for number, at in enumerate(range(0, D, chunk)):
        cols = slice(at, at + chunk)
        result[:, cols] = jnp.dot(hidden[...], down[:, cols], preferred_element_type=F32).astype(BF16)
        row = 0
        for ref in out_refs:
            moves.append(
                pltpu.make_async_copy(
                    result.at[pl.ds(row, ref.shape[0]), pl.ds(at, chunk)],
                    ref.at[:, pl.ds(at, chunk)],
                    sems.at[3 if row == 0 else 5, number],
                )
            )
            moves[-1].start()
            row += ref.shape[0]
    for move in moves:
        move.wait()


def ffn(x_list, weights, out_rows):
    rows = sum(x.shape[0] for x in x_list)
    hid = sum(w.shape[0] for w in weights[0])
    spec = ANY if len(weights[0]) > 1 else HBM
    return pl.pallas_call(
        functools.partial(ffn_kernel, len(x_list), len(weights[0]), len(out_rows)),
        out_shape=[jax.ShapeDtypeStruct((n, D), BF16) for n in out_rows],
        in_specs=[ANY] * len(x_list) + [spec] * (3 * len(weights[0])),
        out_specs=[HBM] * len(out_rows),
        scratch_shapes=[
            pltpu.VMEM((rows, D), BF16),
            pltpu.VMEM((hid, D), BF16),
            pltpu.VMEM((hid, D), BF16),
            pltpu.VMEM((hid, D), BF16),
            pltpu.VMEM((rows, hid), BF16),
            pltpu.VMEM((rows, D), BF16),
            pltpu.SemaphoreType.DMA((6, 8)),
        ],
        compiler_params=pltpu.CompilerParams(vmem_limit_bytes=56 << 20),
        cost_estimate=pl.CostEstimate(
            flops=6 * rows * hid * D, bytes_accessed=6 * hid * D + 4 * rows * D, transcendentals=rows * hid
        ),
    )(*x_list, *weights[0], *weights[1], *weights[2])


def combine_kernel(count, high_ref, low_ref, *refs):
    sources, out_ref, refs = refs[:count], refs[count], refs[count + 1 :]
    held, result, sems = refs[:count], refs[count], refs[count + 1]
    rows = result.shape[0]
    loads = []
    for number, (source, target) in enumerate(zip(sources, held)):
        loads.append(pltpu.make_async_copy(source.at[pl.ds(0, target.shape[0])], target, sems.at[0, number]))
        loads[-1].start()
    for load in loads:
        load.wait()
    state, keep, sib, far, back, *relayed = held
    scale = state[:, D : D + 1]
    step = 512
    moves = []
    for at in range(0, D, step):
        cols = slice(at, at + step)
        routed = jnp.dot(high_ref[...], back[:, cols], preferred_element_type=F32) + jnp.dot(
            low_ref[...], back[:, cols], preferred_element_type=F32
        )
        for ref in relayed:
            routed = routed + ref[:, cols].astype(F32)
        shared = keep[:, cols].astype(F32) + sib[:, cols].astype(F32) + far[:, cols].astype(F32)
        result[:, cols] = (state[:, cols] + scale * shared + routed).astype(BF16)
        window = (pl.ds(0, rows), pl.ds(at, step))
        moves.append(pltpu.make_async_copy(result.at[window], out_ref.at[window], sems.at[1, at // step]))
        moves[-1].start()
    for move in moves:
        move.wait()


def pick_kernel(pick_ref, rows_ref, out_ref, picked, sems):
    step = 512
    moves = []
    for at in range(0, D, step):
        cols = slice(at, at + step)
        picked[:, cols] = jnp.dot(pick_ref[...], rows_ref[:, cols], preferred_element_type=F32).astype(BF16)
        window = (slice(None), pl.ds(at, step))
        moves.append(pltpu.make_async_copy(picked.at[window], out_ref.at[window], sems.at[at // step]))
        moves[-1].start()
    for move in moves:
        move.wait()


def relay_kernel(high_ref, low_ref, back_ref, out_ref):
    step = 512
    for at in range(0, D, step):
        cols = slice(at, at + step)
        back = back_ref[:, cols]
        routed = jnp.dot(high_ref[...], back, preferred_element_type=F32) + jnp.dot(
            low_ref[...], back, preferred_element_type=F32
        )
        out_ref[:, cols] = routed.astype(BF16)


def vmem_call(kernel, out_shape, specs, limit=8, scratch=(), flops=0):
    return pl.pallas_call(
        kernel,
        out_shape=out_shape,
        in_specs=specs,
        out_specs=jax.tree.map(lambda _: VMEM, out_shape),
        scratch_shapes=scratch,
        compiler_params=pltpu.CompilerParams(vmem_limit_bytes=limit << 20),
        cost_estimate=pl.CostEstimate(flops=flops, bytes_accessed=4 << 20, transcendentals=0),
    )


def shape(*dims, dtype=BF16):
    return jax.ShapeDtypeStruct(dims, dtype)


def grp_move(array, flip):
    return lax.ppermute(array, "grp", [(i, i ^ flip) for i in range(lax.axis_size("grp"))])


def req_shift(array, distance):
    devices = range(lax.axis_size("req"))
    return lax.ppermute(array, "req", [(i - distance, i) for i in devices if i - distance in devices])


def pack_kernel(ring_0, ring_1, ring_2, ring_3, first_ref, second_ref):
    half = ring_0.shape[0] // 2
    for number, ref in enumerate((ring_0, ring_1, ring_2, ring_3)):
        first_ref[number * half : (number + 1) * half, :] = ref[:half, :]
        second_ref[number * half : (number + 1) * half, :] = ref[half:, :]


def join_kernel(first_ref, first_far, second_ref, second_far, first_out, second_out):
    rows = second_ref.shape[0]
    first_out[:rows, :] = first_ref[...]
    first_out[rows:, :] = first_far[...]
    second_out[:rows, :] = second_ref[...]
    second_out[rows:, :] = second_far[...]


def over_y(array):
    return lax.ppermute(array, "req", [(i, i ^ 1) for i in range(8)])


def order_kernel(place_ref, out_ref):
    total = out_ref.shape[0]
    part = total // 32
    half = part // 2
    req, grp = place_ref[0], place_ref[1]
    step = 128
    for piece in range(8):
        index = lax.broadcasted_iota(jnp.int32, (1, step), 1)
        flip = lax.shift_right_logical(index, int(math.log2(4 * half))) & 1
        turn = lax.shift_right_logical(index, int(math.log2(half))) & 3
        far, swapped = piece // 2 % 2, piece % 2
        y_flip, x_flip = (far, flip) if swapped else (flip, far)
        row = ((req + 8 - 2 * turn) & 7) ^ y_flip
        column = grp ^ (2 * x_flip + piece // 4)
        target = (row * 4 + column) * part + swapped * half + (index & (half - 1))
        lines = lax.broadcasted_iota(jnp.int32, (total, step), 0)
        out_ref[:, piece * step : (piece + 1) * step] = jnp.where(lines == target, 1.0, 0.0).astype(BF16)


def gather_ring(array):
    return [array] + [
        lax.ppermute(array, "req", [(i, (i + 2 * d) % 8) for i in range(8)]) for d in range(1, 4)
    ]


def local(
    suffix_queries,
    suffix_keys,
    suffix_values,
    prefix_cache,
    residual,
    out_weight,
    norm_gain,
    routes,
    route_weights,
    lengths,
    migrate,
    expert_gate,
    expert_up,
    expert_down,
    shared_gate,
    shared_up,
    shared_down,
    shared_router,
):
    rows = suffix_queries.shape[1]
    requests = lax.axis_size("req")
    req = lax.axis_index("req")
    grp = lax.axis_index("grp")
    depth = min(8, requests // 4)
    prefix_len = prefix_cache.shape[1] * requests
    capacity = rows * TOP * 5 // (4 * requests)
    place = jnp.stack([req, grp]).astype(jnp.int32)

    inverse = ROPE_BASE ** (-2.0 * np.arange(HD // 2) / HD)
    inverse = jnp.asarray(np.concatenate([inverse, inverse])[None].astype(np.float32))
    query_turned, own_cache = vmem_call(
        functools.partial(rope_kernel, prefix_len),
        [shape(rows, WIDTH), shape(rows, 2 * WIDTH)],
        [SMEM, SMEM] + [VMEM] * 4,
    )(lengths, place, inverse, suffix_queries[0], suffix_keys[0], suffix_values[0])

    routing = jnp.concatenate([routes[0].astype(F32), route_weights[0]], axis=1)
    halves = requests == 8
    experts = requests // 2 if halves else requests
    base = (req // experts * experts).astype(jnp.int32)[None]
    slots = experts * capacity

    def route(table):
        return vmem_call(
            functools.partial(route_kernel, experts, [(0, capacity)]),
            [shape(slots, rows), shape(rows, slots), shape(rows, slots)],
            [SMEM, VMEM],
        )(base, table)

    def across(array):
        return lax.ppermute(array, "req", [(i, i ^ requests // 2) for i in range(requests)])

    pick, high, low = route(routing)

    def attend(prefix_rows, history, order):
        return vmem_call(
            functools.partial(attend_kernel, depth),
            shape(rows, WIDTH),
            [SMEM, SMEM] + [VMEM] * (3 + depth + len(order)),
            flops=ATTEND_COST,
        )(lengths, place, query_turned, prefix_rows, own_cache, *history, *order)

    mine = [jnp.swapaxes(expert_gate[0], 0, 1), jnp.swapaxes(expert_up[0], 0, 1), expert_down[0]]
    part = prefix_cache[0].reshape(-1, HD)
    prefix_rows = lax.all_to_all(
        jnp.broadcast_to(part[None], (requests, *part.shape)), "req", split_axis=0, concat_axis=0, tiled=True
    ).reshape(prefix_len, 2 * WIDTH)
    if halves:
        far_routing = across(routing)
        half = out_weight.shape[0] // 2
        ring = gather_ring(out_weight)
        far_gate = grp_move(mine[0], 2)
        *ring, late_cache, late_up, far_gate, far_routing, prefix_rows = lax.optimization_barrier(
            (*ring, own_cache, mine[1], far_gate, far_routing, prefix_rows)
        )
        first, second = vmem_call(pack_kernel, [shape(4 * half, D), shape(4 * half, D)], [VMEM] * 4)(*ring)
        first, second, late_cache = lax.optimization_barrier((first, second, late_cache))
        first_far, second_far = over_y(first), grp_move(second, 2)
        history = [req_shift(late_cache, distance) for distance in range(1, depth + 1)]
        far_pick, far_high, far_low = route(far_routing)
        order = vmem_call(order_kernel, shape(WIDTH, WIDTH), [SMEM])(place)
        far_up = grp_move(late_up, 2)
        first_far, second_far, order, pick, far_pick, far_up = lax.optimization_barrier(
            (first_far, second_far, order, pick, far_pick, far_up)
        )
        first, second = vmem_call(
            join_kernel, [shape(8 * half, D), shape(8 * half, D)], [VMEM] * 4
        )(first, first_far, second, second_far)
        attention = attend(prefix_rows, history, [order])
        near = [first, second, grp_move(first, 1), grp_move(second, 1)]
        far = [grp_move(first, 2), over_y(second)]
        *far, attention, late_down = lax.optimization_barrier((*far, attention, mine[2]))
        pieces = near[:2] + far + near[2:] + [grp_move(array, 1) for array in far]
        far_down = grp_move(late_down, 2)
    else:
        pieces = [lax.all_gather(out_weight, ("req", "grp"), axis=0, tiled=True)]
        history = [req_shift(own_cache, distance) for distance in range(1, depth + 1)]
        attention = attend(prefix_rows, history, [])
        far_gate, far_up, far_down = [grp_move(w, 2) for w in mine]

    normed, state, outgoing = pl.pallas_call(
        functools.partial(project_kernel, len(pieces)),
        out_shape=[shape(rows, D), shape(rows, D + HD, dtype=F32), shape(slots, D)],
        in_specs=[VMEM] * (5 + len(pieces)),
        out_specs=[HBM] * 3,
        scratch_shapes=[
            pltpu.VMEM((rows, D), BF16),
            pltpu.VMEM((rows, D + HD), F32),
            pltpu.VMEM((slots, D), BF16),
            pltpu.SemaphoreType.DMA((3, 5)),
        ],
        compiler_params=pltpu.CompilerParams(vmem_limit_bytes=16 << 20),
        cost_estimate=pl.CostEstimate(flops=2 * rows * WIDTH * D, bytes_accessed=8 << 20, transcendentals=0),
    )(attention, residual[0], norm_gain[None], shared_router[None], pick, *pieces)

    groups = [list(range(at, at + experts)) for at in range(0, requests, experts)] if halves else None

    def exchange(array):
        split = array.reshape(experts, capacity, D)
        return lax.all_to_all(
            split, "req", split_axis=0, concat_axis=0, axis_index_groups=groups, tiled=True
        ).reshape(slots, D)

    def both(own, other):
        return [own, grp_move(own, 1), other, grp_move(other, 1)]

    gates, ups = both(mine[0], far_gate), both(mine[1], far_up)
    arrived = exchange(outgoing)
    late_normed, late_cache, far_rows = normed, own_cache, None
    if halves:
        relay_rows = across(normed)
        relay_rows, arrived, late_normed, far_down, gates, ups = lax.optimization_barrier(
            (relay_rows, arrived, normed, far_down, gates, ups)
        )
        relay_out = pl.pallas_call(
            pick_kernel,
            out_shape=shape(slots, D),
            in_specs=[VMEM] * 2,
            out_specs=HBM,
            scratch_shapes=[pltpu.VMEM((slots, D), BF16), pltpu.SemaphoreType.DMA((4,))],
        )(far_pick, relay_rows)
        relay_arrived = exchange(relay_out)
    weights = [gates, ups, both(mine[2], far_down)]
    far_rows = grp_move(late_normed, 2)
    (finished,) = ffn([arrived], weights, [slots])
    if halves:
        relay_arrived, finished, late_cache, far_rows = lax.optimization_barrier(
            (relay_arrived, finished, own_cache, far_rows)
        )
        (relay_finished,) = ffn([relay_arrived], weights, [slots])
        relay_back = exchange(relay_finished)
        relay_finished, normed, far_rows = lax.optimization_barrier((relay_finished, normed, far_rows))
    keep, send = ffn(
        [normed, far_rows, grp_move(normed, 1), grp_move(far_rows, 1)],
        [[jnp.swapaxes(shared_gate, 0, 1)], [jnp.swapaxes(shared_up, 0, 1)], [shared_down]],
        [2 * rows, 2 * rows],
    )
    partner = grp_move(late_cache, 2)
    if halves:
        relay_back, partner, finished, keep, send = lax.optimization_barrier(
            (relay_back, partner, finished, keep, send)
        )
    from_sib = grp_move(send, 1)
    pair_sum = (keep[rows:].astype(F32) + from_sib[rows:].astype(F32)).astype(BF16)
    from_far = grp_move(pair_sum, 2)
    relayed = []
    if halves:
        relay_sum = vmem_call(relay_kernel, shape(rows, D), [VMEM] * 3)(far_high, far_low, relay_back)
        relayed = [across(relay_sum)]
    back = exchange(finished)

    sources = [state, keep, from_sib, from_far, back, *relayed]
    kept = [(rows, D + HD)] + [(rows, D)] * 3 + [(slots, D)] + [(rows, D)] * len(relayed)
    final = pl.pallas_call(
        functools.partial(combine_kernel, len(sources)),
        out_shape=shape(rows, D),
        in_specs=[VMEM] * 2 + [ANY] * len(sources),
        out_specs=HBM,
        scratch_shapes=[pltpu.VMEM(dims, source.dtype) for dims, source in zip(kept, sources)]
        + [pltpu.VMEM((rows, D), BF16), pltpu.SemaphoreType.DMA((2, 8))],
        compiler_params=pltpu.CompilerParams(vmem_limit_bytes=32 << 20),
        cost_estimate=pl.CostEstimate(flops=4 * slots * rows * D, bytes_accessed=8 << 20, transcendentals=0),
    )(high, low, *sources)

    pair_row = grp // 4 * 2 + grp % 2
    flags = jnp.sum(
        jnp.where((jnp.arange(migrate.shape[0], dtype=jnp.int32) == pair_row)[:, None], migrate, 0), axis=0
    )
    page_moved = jnp.repeat(flags, PG) == 1
    suffix_cache = jnp.where(page_moved[:, None], partner, own_cache)
    return (final[None], suffix_cache[None])


def solution(mesh):
    placed = (
        P("grp", "req", None),
        P("grp", "req", None),
        P("grp", "req", None),
        P("grp", "req", None),
        P("grp", "req", None),
        P(("req", "grp"), None),
        P(),
        P("grp", "req", None),
        P("grp", "req", None),
        P("grp", None),
        P(None, "req"),
        P("req", None, "grp"),
        P("req", None, "grp"),
        P("req", "grp", None),
        P(None, "grp"),
        P(None, "grp"),
        P("grp", None),
        P(),
    )
    return jax.shard_map(
        local,
        mesh=mesh,
        in_specs=placed,
        out_specs=(P("grp", "req", None), P("grp", "req", None)),
        check_vma=False,
    )
```

time: 256 us -> 196 us (0.77)
  blocking collectives: 43.2 us -> 0 us
  waiting for transfers between devices: 107 us -> 73.1 us
  starting transfers between devices: 39.1 us -> 54.8 us
  local copies, waits for them, and re-layouts: 20.1 us -> 16.3 us
  Pallas kernels: 40.2 us -> 43.6 us
    ppermute x19 -> x21, waiting for transfers between devices: 87.3 us -> 31.2 us  [grp_move(): lax.ppermute(array, 'grp', [(i, i ^ flip) for i in range(lax.axis_size('g...]
    all_gather x1 -> x0, blocking collectives: 43.2 us -> none  [local(): prefix_rows = lax.all_gather(prefix_cache[0], 'req', axis=0, tiled=True)]
    ppermute x3 -> x6, waiting for transfers between devices: 6.57 us -> 23.4 us  [the longest x3 23.4 us: across(): lax.ppermute(array, 'req', [(i, i ^ requests // 2) for i in range(request...]
    all_to_all x2 -> x5, starting transfers between devices: 8.5 us -> 19.2 us  [the longest x4 15.9 us: exchange(): lax.all_to_all(split, 'req', split_axis=0, concat_axis=0, axis_index_grou...]
    unnamed x78 -> x90, local copies, waits for them, and re-layouts: 19.8 us -> 13.8 us
    ppermute x3 -> x6, starting transfers between devices: 7.01 us -> 13 us  [the longest x3 6.61 us: across(): lax.ppermute(array, 'req', [(i, i ^ requests // 2) for i in range(request...]
    ppermute x2, waiting for transfers between devices: 6.21 us -> 10.9 us  [over_y(): return lax.ppermute(array, 'req', [(i, i ^ 1) for i in range(8)])]
    pallas_call x5 -> x13, Pallas kernels: 39.1 us -> 42.4 us  [the longest x3 23.8 us: ffn(): pl.pallas_call(functools.partial(ffn_kernel, len(x_list), len(weights[0])...]
  transfers between devices with their start and end apart: 28 -> 36, of which waited for: 15 -> 21; matrix products, arithmetic and copies ran while one was open for 2% -> 4% of each run, Pallas kernels for 6% -> 14%
where the time goes in v2:
time: 196 us; the launch traced here: 195 us
  waiting for transfers between devices  73.1 us (37%)
  starting transfers between devices  54.8 us (28%)
  Pallas kernels  43.6 us (22%)
  local copies, waits for them, and re-layouts  16.3 us (8%)
  other arithmetic  5.63 us (3%)
    ppermute x21, waiting for transfers between devices, grp_move(): lax.ppermute(array, 'grp', [(i, i ^ flip) for i in range(lax.axis_size('g...  31.2 us
    pallas_call x3, Pallas kernels, ffn(): pl.pallas_call(functools.partial(ffn_kernel, len(x_list), len(weights[0])...  23.8 us
    ppermute x3, waiting for transfers between devices, across(): lax.ppermute(array, 'req', [(i, i ^ requests // 2) for i in range(request...  23.4 us
    all_to_all x4, starting transfers between devices, exchange(): lax.all_to_all(split, 'req', split_axis=0, concat_axis=0, axis_index_grou...  15.9 us
    unnamed x90, local copies, waits for them, and re-layouts  13.8 us
    ppermute x21, starting transfers between devices, grp_move(): lax.ppermute(array, 'grp', [(i, i ^ flip) for i in range(lax.axis_size('g...  11.7 us
    ppermute x2, waiting for transfers between devices, over_y(): return lax.ppermute(array, 'req', [(i, i ^ 1) for i in range(8)])  10.9 us
    ppermute x2, starting transfers between devices, req_shift(): lax.ppermute(array, 'req', [(i - distance, i) for i in devices if i - dis...  8.37 us
  transfers between devices with their start and end apart: 36, of which 21 were waited for; matrix products, arithmetic and copies ran while one was open for 4% of the time, Pallas kernels for 14%

profile of v2, /device:TPU:0, one launch (start us, length us, event | category | flops | bytes accessed | tf_op | source)
XLA Modules:
  0.0 194.7 jit_solution(617996387375611314)
XLA Ops:
  0.6 3.0 %collective-permute-start.3 = (bf16[176,2048]{1,0:T(8,128)(2,1)}, bf16[176,2048]{1,0:T(8,128)(2,1)S(1)}, u32[]{:S(2)}, u32[]{:S(2)}) collective-permute-start(bf16[176,2048]{1,0:T(8,128)(2,1)} %bitcast.42), channel_id=1, source_target_pairs={{0,2},{1,3},{2,0},{3,1},{4,6},{5,7},{6,4},{7,5},{8,10},{9,11},{10,... | collective-permute-start | bytes 2162696 | tf_op jit(solution)/shard_map/ppermute | solution.py:337
  3.6 2.6 %collective-permute-start.1 = (bf16[32,2048]{1,0:T(8,128)(2,1)}, bf16[32,2048]{1,0:T(8,128)(2,1)S(1)}, u32[]{:S(2)}, u32[]{:S(2)}) collective-permute-start(bf16[32,2048]{1,0:T(8,128)(2,1)} %ring_0), channel_id=1, source_target_pairs={{0,16},{4,20},{8,24},{12,28},{16,0},{20,4},{24,8},{28,12},{1,17},{... | collective-permute-start | bytes 393224 | tf_op jit(solution)/shard_map/ppermute | solution.py:385
  11.5 3.4 %all-to-all-start = ((bf16[8,64,128]{2,1,0:T(8,128)(2,1)}), bf16[8,64,128]{2,1,0:T(8,128)(2,1)S(1)}, u32[]{:S(2)}, u32[]{:S(2)}) async-start(bf16[8,64,128]{2,1,0:T(8,128)(2,1)} %broadcast_in_dim.49), calls=%async_computation | async-start | bytes 262144 | tf_op jit(solution)/shard_map/all_to_all | solution.py:454
  16.3 2.9 %collective-permute-start.4 = (f32[128,8]{1,0:T(8,128)S(1)}, f32[128,8]{1,0:T(8,128)S(1)}, u32[]{:S(2)}, u32[]{:S(2)}) collective-permute-start(f32[128,8]{1,0:T(8,128)S(1)} %copy.23.routing_ref), channel_id=1, source_target_pairs={{0,16},{4,20},{8,24},{12,28},{16,0},{20,4},{24,8},{28,12},{1,17},{... | collective-permute-start | bytes 12296 | tf_op jit(solution)/shard_map/ppermute | solution.py:440
  27.7 4.2 %collective-permute-start.11 = (bf16[128,2048]{1,0:T(8,128)(2,1)S(1)}, bf16[128,2048]{1,0:T(8,128)(2,1)}, u32[]{:S(2)}, u32[]{:S(2)}) collective-permute-start(bf16[128,2048]{1,0:T(8,128)(2,1)S(1)} %get-tuple-element.112.refs_0_), channel_id=1, source_target_pairs={{0,8},{4,12},{8,16},{12,20},{16,24},{20,28},{1,9},{5,13},{9,17},{1... | collective-permute-start | bytes 1572872 | tf_op jit(solution)/shard_map/ppermute | solution.py:342
  31.9 4.2 %collective-permute-start.10 = (bf16[128,2048]{1,0:T(8,128)(2,1)S(1)}, bf16[128,2048]{1,0:T(8,128)(2,1)}, u32[]{:S(2)}, u32[]{:S(2)}) collective-permute-start(bf16[128,2048]{1,0:T(8,128)(2,1)S(1)} %get-tuple-element.112.refs_0_), channel_id=1, source_target_pairs={{0,4},{4,8},{8,12},{12,16},{16,20},{20,24},{24,28},{1,5},{5,9},{9,... | collective-permute-start | bytes 1572872 | tf_op jit(solution)/shard_map/ppermute | solution.py:342
  41.1 8.6 %collective-permute-done.5.first_far = bf16[64,2048]{1,0:T(8,128)(2,1)S(1)} collective-permute-done((bf16[64,2048]{1,0:T(8,128)(2,1)S(1)}, bf16[64,2048]{1,0:T(8,128)(2,1)S(1)}, u32[]{:S(2)}, u32[]{:S(2)}) %collective-permute-start.5) | collective-permute-done | bytes 262176 | tf_op jit(solution)/shard_map/ppermute | solution.py:361
  52.6 2.5 %collective-permute-start.9 = (bf16[128,2048]{1,0:T(8,128)(2,1)S(1)}, bf16[128,2048]{1,0:T(8,128)(2,1)S(1)}, u32[]{:S(2)}, u32[]{:S(2)}) collective-permute-start(bf16[128,2048]{1,0:T(8,128)(2,1)S(1)} %get-tuple-element.83.refs_1_), channel_id=1, source_target_pairs={{0,4},{4,0},{8,12},{12,8},{16,20},{20,16},{24,28},{28,24},{1,5},{5... | collective-permute-start | bytes 1572872 | tf_op jit(solution)/shard_map/ppermute | solution.py:361
  57.0 4.1 %shard_map.200.attn_ref = bf16[128,1024]{1,0:T(8,128)(2,1)S(1)} custom-call(s32[1,16]{1,0:T(1,128)S(1)} %copy-done.22, s32[2]{0:T(128)S(1)} %pad_add_fusion.place_ref, bf16[128,1024]{1,0:T(8,128)(2,1)S(1)} %copy-done.26, bf16[32,2048]{1,0:T(8,128)(2,1)S(1)} %copy-done.9, bf16[128,2048]{1,0:T(8,128)(2,1)S(1)} %get-tuple-element.112.refs_0_, ...), custom_call_target="tpu_custom_call" | custom-call | flops 20000000000 | bytes 4194304 | tf_op jit(solution)/shard_map/pallas_call | solution.py:445
  61.1 4.1 %collective-permute-done.8.refs_2_ = bf16[128,2048]{1,0:T(8,128)(2,1)S(1)} collective-permute-done((bf16[128,2048]{1,0:T(8,128)(2,1)S(1)}, bf16[128,2048]{1,0:T(8,128)(2,1)S(1)}, u32[]{:S(2)}, u32[]{:S(2)}) %collective-permute-start.8) | collective-permute-done | bytes 524320 | tf_op jit(solution)/shard_map/ppermute | solution.py:337
  70.2 3.8 %shard_map.201 = (bf16[128,2048]{1,0:T(8,128)(2,1)S(1)}, f32[128,2176]{1,0:T(8,128)S(1)}, bf16[320,2048]{1,0:T(8,128)(2,1)}) custom-call(bf16[128,1024]{1,0:T(8,128)(2,1)S(1)} %shard_map.200.attn_ref, bf16[128,2048]{1,0:T(8,128)(2,1)S(1)} %bitcast.33, f32[1,2048]{1,0:T(1,128)S(1)} %bitcast.37, bf16[1,2048]{1,0:T(2,128)(2,1)S(1)} %broadcast_in_dim.51.router_ref, ...), custom_call_target="tpu_custom_call" | custom-call | flops 536870912 | bytes 8388608 | tf_op jit(solution)/shard_map/pallas_call | solution.py:490
  75.0 3.7 %all-to-all-start.1 = ((bf16[4,80,2048]{2,1,0:T(8,128)(2,1)}), bf16[4,80,2048]{2,1,0:T(8,128)(2,1)S(1)}, u32[]{:S(2)}, u32[]{:S(2)}) async-start(bf16[4,80,2048]{2,1,0:T(8,128)(2,1)} %bitcast.15), calls=%async_computation.1 | async-start | bytes 2621440 | tf_op jit(solution)/shard_map/all_to_all | solution.py:509
  84.2 13.9 %collective-permute-done.17.refs_11_ = bf16[176,2048]{1,0:T(8,128)(2,1)S(1)} collective-permute-done((bf16[176,2048]{1,0:T(8,128)(2,1)}, bf16[176,2048]{1,0:T(8,128)(2,1)S(1)}, u32[]{:S(2)}, u32[]{:S(2)}) %collective-permute-start.17) | collective-permute-done | bytes 720928 | tf_op jit(solution)/shard_map/ppermute | solution.py:337
  99.0 5.7 %collective-permute-done.16.rows_ref = bf16[128,2048]{1,0:T(8,128)(2,1)S(1)} collective-permute-done((bf16[128,2048]{1,0:T(8,128)(2,1)S(1)}, bf16[128,2048]{1,0:T(8,128)(2,1)S(1)}, u32[]{:S(2)}, u32[]{:S(2)}) %collective-permute-start.16) | collective-permute-done | bytes 524320 | tf_op jit(solution)/shard_map/ppermute | solution.py:440
  106.9 3.0 %shard_map.202 = bf16[320,2048]{1,0:T(8,128)(2,1)} custom-call(bf16[320,128]{1,0:T(8,128)(2,1)} %copy-done.19, bf16[128,2048]{1,0:T(8,128)(2,1)} %copy-done.38), custom_call_target="tpu_custom_call" | custom-call | tf_op jit(solution)/shard_map/pallas_call | solution.py:524
  109.9 4.8 %all-to-all-start.2 = ((bf16[4,80,2048]{2,1,0:T(8,128)(2,1)}), bf16[4,80,2048]{2,1,0:T(8,128)(2,1)}, u32[]{:S(2)}, u32[]{:S(2)}) async-start(bf16[4,80,2048]{2,1,0:T(8,128)(2,1)} %bitcast.38), calls=%async_computation.2 | async-start | bytes 2621440 | tf_op jit(solution)/shard_map/all_to_all | solution.py:509
  119.0 7.3 %shard_map.203 = bf16[320,2048]{1,0:T(8,128)(2,1)} custom-call(bf16[320,2048]{1,0:T(8,128)(2,1)} %bitcast.40, bf16[176,2048]{1,0:T(8,128)(2,1)} %bitcast.43, bf16[176,2048]{1,0:T(8,128)(2,1)} %copy-done.31, bf16[176,2048]{1,0:T(8,128)(2,1)} %copy-done.30, bf16[176,2048]{1,0:T(8,128)(2,1)} %copy-done.33, bf16[176,2048]{1,0:T(8,128)(2,1)} %bitcast.48, ...), custom_call_target="tpu_custom_call" | custom-call | flops 2768240640 | bytes 11272192 | tf_op jit(solution)/shard_map/pallas_call | solution.py:245
  126.3 2.8 %collective-permute-done.24.refs_1_ = bf16[128,2048]{1,0:T(8,128)(2,1)S(1)} collective-permute-done((bf16[128,2048]{1,0:T(8,128)(2,1)S(1)}, bf16[128,2048]{1,0:T(8,128)(2,1)S(1)}, u32[]{:S(2)}, u32[]{:S(2)}) %collective-permute-start.24) | collective-permute-done | bytes 524320 | tf_op jit(solution)/shard_map/ppermute | solution.py:337
  130.7 7.3 %shard_map.204 = bf16[320,2048]{1,0:T(8,128)(2,1)} custom-call(bf16[320,2048]{1,0:T(8,128)(2,1)} %bitcast.20.refs_0_, bf16[176,2048]{1,0:T(8,128)(2,1)} %bitcast.44, bf16[176,2048]{1,0:T(8,128)(2,1)} %copy-done.31, bf16[176,2048]{1,0:T(8,128)(2,1)} %copy-done.30, bf16[176,2048]{1,0:T(8,128)(2,1)} %copy-done.33, bf16[176,2048]{1,0:T(8,128)(2,1)} %bitcast.49, ...), custom_call_target="tpu_custom_call" | custom-call | flops 2768240640 | bytes 11272192 | tf_op jit(solution)/shard_map/pallas_call | solution.py:245
  138.0 3.7 %all-to-all-start.3 = ((bf16[4,80,2048]{2,1,0:T(8,128)(2,1)}), bf16[4,80,2048]{2,1,0:T(8,128)(2,1)S(1)}, u32[]{:S(2)}, u32[]{:S(2)}) async-start(bf16[4,80,2048]{2,1,0:T(8,128)(2,1)} %bitcast.41), calls=%async_computation.3 | async-start | bytes 2621440 | tf_op jit(solution)/shard_map/all_to_all | solution.py:509
  145.3 9.3 %shard_map.205 = (bf16[256,2048]{1,0:T(8,128)(2,1)}, bf16[256,2048]{1,0:T(8,128)(2,1)}) custom-call(bf16[128,2048]{1,0:T(8,128)(2,1)} %copy-done.24, bf16[128,2048]{1,0:T(8,128)(2,1)} %copy-done.41, bf16[128,2048]{1,0:T(8,128)(2,1)} %copy-done.43, bf16[128,2048]{1,0:T(8,128)(2,1)} %copy-done.44, bf16[704,2048]{1,0:T(8,128)(2,1)} %bitcast.56, ...), custom_call_target="tpu_custom_call" | custom-call | flops 4429185024 | bytes 12845056 | tf_op jit(solution)/shard_map/pallas_call | solution.py:245
  158.1 3.7 %all-to-all-start.4 = ((bf16[4,80,2048]{2,1,0:T(8,128)(2,1)}), bf16[4,80,2048]{2,1,0:T(8,128)(2,1)S(1)}, u32[]{:S(2)}, u32[]{:S(2)}) async-start(bf16[4,80,2048]{2,1,0:T(8,128)(2,1)} %bitcast.39), calls=%async_computation.4 | async-start | bytes 2621440 | tf_op jit(solution)/shard_map/all_to_all | solution.py:509
  170.7 17.7 %collective-permute-done.30.refs_5_ = bf16[128,2048]{1,0:T(8,128)(2,1)S(1)} collective-permute-done((bf16[128,2048]{1,0:T(8,128)(2,1)}, bf16[128,2048]{1,0:T(8,128)(2,1)S(1)}, u32[]{:S(2)}, u32[]{:S(2)}) %collective-permute-start.30) | collective-permute-done | bytes 524320 | tf_op jit(solution)/shard_map/ppermute | solution.py:440
  191.6 2.9 %shard_map.207 = bf16[128,2048]{1,0:T(8,128)(2,1)} custom-call(bf16[128,320]{1,0:T(8,128)(2,1)S(1)} %copy-done.16, bf16[128,320]{1,0:T(8,128)(2,1)S(1)} %copy-done.18, f32[128,2176]{1,0:T(8,128)S(1)} %copy-done.3, bf16[256,2048]{1,0:T(8,128)(2,1)S(1)} %copy-done.1, bf16[256,2048]{1,0:T(8,128)(2,1)} %collective-permute-done.28.refs_2_, ...), custom_call_target="tpu_custom_call" | custom-call | flops 335544320 | bytes 8388608 | tf_op jit(solution)/shard_map/pallas_call | solution.py:563
  (167 shorter events, 64.3 us)
Async XLA Ops:
  0.6 25.5 %collective-permute-start.3 = (bf16[176,2048]{1,0:T(8,128)(2,1)}, bf16[176,2048]{1,0:T(8,128)(2,1)S(1)}, u32[]{:S(2)}, u32[]{:S(2)}) collective-permute-start(bf16[176,2048]{1,0:T(8,128)(2,1)} %bitcast.42), channel_id=1, source_target_pairs={{0,2},{1,3},{2,0},{3,1},{4,6},{5,7},{6,4},{7,5},{8,10},{9,11},{10,... | collective-permute-start | bytes 2162696 | tf_op jit(solution)/shard_map/ppermute | solution.py:337
  3.6 22.5 %collective-permute-start.1 = (bf16[32,2048]{1,0:T(8,128)(2,1)}, bf16[32,2048]{1,0:T(8,128)(2,1)S(1)}, u32[]{:S(2)}, u32[]{:S(2)}) collective-permute-start(bf16[32,2048]{1,0:T(8,128)(2,1)} %ring_0), channel_id=1, source_target_pairs={{0,16},{4,20},{8,24},{12,28},{16,0},{20,4},{24,8},{28,12},{1,17},{... | collective-permute-start | bytes 393224 | tf_op jit(solution)/shard_map/ppermute | solution.py:385
  6.2 19.9 %collective-permute-start = (bf16[32,2048]{1,0:T(8,128)(2,1)}, bf16[32,2048]{1,0:T(8,128)(2,1)S(1)}, u32[]{:S(2)}, u32[]{:S(2)}) collective-permute-start(bf16[32,2048]{1,0:T(8,128)(2,1)} %ring_0), channel_id=1, source_target_pairs={{0,8},{4,12},{8,16},{12,20},{16,24},{20,28},{24,0},{28,4},{1,9},{5... | collective-permute-start | bytes 393224 | tf_op jit(solution)/shard_map/ppermute | solution.py:385
  7.8 18.3 %collective-permute-start.2 = (bf16[32,2048]{1,0:T(8,128)(2,1)}, bf16[32,2048]{1,0:T(8,128)(2,1)S(1)}, u32[]{:S(2)}, u32[]{:S(2)}) collective-permute-start(bf16[32,2048]{1,0:T(8,128)(2,1)} %ring_0), channel_id=1, source_target_pairs={{0,24},{4,28},{8,0},{12,4},{16,8},{20,12},{24,16},{28,20},{1,25},{... | collective-permute-start | bytes 393224 | tf_op jit(solution)/shard_map/ppermute | solution.py:385
  11.5 13.8 %all-to-all-start = ((bf16[8,64,128]{2,1,0:T(8,128)(2,1)}), bf16[8,64,128]{2,1,0:T(8,128)(2,1)S(1)}, u32[]{:S(2)}, u32[]{:S(2)}) async-start(bf16[8,64,128]{2,1,0:T(8,128)(2,1)} %broadcast_in_dim.49), calls=%async_computation | async-start | bytes 262144 | tf_op jit(solution)/shard_map/all_to_all | solution.py:454
  27.1 22.7 %collective-permute-start.7 = (bf16[176,2048]{1,0:T(8,128)(2,1)}, bf16[176,2048]{1,0:T(8,128)(2,1)}, u32[]{:S(2)}, u32[]{:S(2)}) collective-permute-start(bf16[176,2048]{1,0:T(8,128)(2,1)} %bitcast.46), channel_id=1, source_target_pairs={{0,2},{1,3},{2,0},{3,1},{4,6},{5,7},{6,4},{7,5},{8,10},{9,11},{10,... | collective-permute-start | bytes 2162696 | tf_op jit(solution)/shard_map/ppermute | solution.py:337
  27.7 24.9 %collective-permute-start.11 = (bf16[128,2048]{1,0:T(8,128)(2,1)S(1)}, bf16[128,2048]{1,0:T(8,128)(2,1)}, u32[]{:S(2)}, u32[]{:S(2)}) collective-permute-start(bf16[128,2048]{1,0:T(8,128)(2,1)S(1)} %get-tuple-element.112.refs_0_), channel_id=1, source_target_pairs={{0,8},{4,12},{8,16},{12,20},{16,24},{20,28},{1,9},{5,13},{9,17},{1... | collective-permute-start | bytes 1572872 | tf_op jit(solution)/shard_map/ppermute | solution.py:342
  31.9 23.2 %collective-permute-start.10 = (bf16[128,2048]{1,0:T(8,128)(2,1)S(1)}, bf16[128,2048]{1,0:T(8,128)(2,1)}, u32[]{:S(2)}, u32[]{:S(2)}) collective-permute-start(bf16[128,2048]{1,0:T(8,128)(2,1)S(1)} %get-tuple-element.112.refs_0_), channel_id=1, source_target_pairs={{0,4},{4,8},{8,12},{12,16},{16,20},{20,24},{24,28},{1,5},{5,9},{9,... | collective-permute-start | bytes 1572872 | tf_op jit(solution)/shard_map/ppermute | solution.py:342
  36.0 13.7 %collective-permute-start.5 = (bf16[64,2048]{1,0:T(8,128)(2,1)S(1)}, bf16[64,2048]{1,0:T(8,128)(2,1)S(1)}, u32[]{:S(2)}, u32[]{:S(2)}) collective-permute-start(bf16[64,2048]{1,0:T(8,128)(2,1)S(1)} %get-tuple-element.74.first_ref), channel_id=1, source_target_pairs={{0,4},{4,0},{8,12},{12,8},{16,20},{20,16},{24,28},{28,24},{1,5},{5... | collective-permute-start | bytes 786440 | tf_op jit(solution)/shard_map/ppermute | solution.py:361
  36.0 13.7 %collective-permute-start.6 = (bf16[64,2048]{1,0:T(8,128)(2,1)S(1)}, bf16[64,2048]{1,0:T(8,128)(2,1)}, u32[]{:S(2)}, u32[]{:S(2)}) collective-permute-start(bf16[64,2048]{1,0:T(8,128)(2,1)S(1)} %get-tuple-element.75.second_ref), channel_id=1, source_target_pairs={{0,2},{1,3},{2,0},{3,1},{4,6},{5,7},{6,4},{7,5},{8,10},{9,11},{10,... | collective-permute-start | bytes 786440 | tf_op jit(solution)/shard_map/ppermute | solution.py:337
  50.8 17.2 %collective-permute-start.12 = (bf16[128,2048]{1,0:T(8,128)(2,1)S(1)}, bf16[128,2048]{1,0:T(8,128)(2,1)S(1)}, u32[]{:S(2)}, u32[]{:S(2)}) collective-permute-start(bf16[128,2048]{1,0:T(8,128)(2,1)S(1)} %get-tuple-element.82.refs_0_), channel_id=1, source_target_pairs={{0,1},{1,0},{2,3},{3,2},{4,5},{5,4},{6,7},{7,6},{8,9},{9,8},{10,11... | collective-permute-start | bytes 1572872 | tf_op jit(solution)/shard_map/ppermute | solution.py:337
  50.9 14.3 %collective-permute-start.8 = (bf16[128,2048]{1,0:T(8,128)(2,1)S(1)}, bf16[128,2048]{1,0:T(8,128)(2,1)S(1)}, u32[]{:S(2)}, u32[]{:S(2)}) collective-permute-start(bf16[128,2048]{1,0:T(8,128)(2,1)S(1)} %get-tuple-element.82.refs_0_), channel_id=1, source_target_pairs={{0,2},{1,3},{2,0},{3,1},{4,6},{5,7},{6,4},{7,5},{8,10},{9,11},{10,... | collective-permute-start | bytes 1572872 | tf_op jit(solution)/shard_map/ppermute | solution.py:337
  52.4 15.6 %collective-permute-start.13 = (bf16[128,2048]{1,0:T(8,128)(2,1)S(1)}, bf16[128,2048]{1,0:T(8,128)(2,1)S(1)}, u32[]{:S(2)}, u32[]{:S(2)}) collective-permute-start(bf16[128,2048]{1,0:T(8,128)(2,1)S(1)} %get-tuple-element.83.refs_1_), channel_id=1, source_target_pairs={{0,1},{1,0},{2,3},{3,2},{4,5},{5,4},{6,7},{7,6},{8,9},{9,8},{10,11... | collective-permute-start | bytes 1572872 | tf_op jit(solution)/shard_map/ppermute | solution.py:337
  52.6 14.9 %collective-permute-start.9 = (bf16[128,2048]{1,0:T(8,128)(2,1)S(1)}, bf16[128,2048]{1,0:T(8,128)(2,1)S(1)}, u32[]{:S(2)}, u32[]{:S(2)}) collective-permute-start(bf16[128,2048]{1,0:T(8,128)(2,1)S(1)} %get-tuple-element.83.refs_1_), channel_id=1, source_target_pairs={{0,4},{4,0},{8,12},{12,8},{16,20},{20,16},{24,28},{28,24},{1,5},{5... | collective-permute-start | bytes 1572872 | tf_op jit(solution)/shard_map/ppermute | solution.py:361
  75.0 31.9 %all-to-all-start.1 = ((bf16[4,80,2048]{2,1,0:T(8,128)(2,1)}), bf16[4,80,2048]{2,1,0:T(8,128)(2,1)S(1)}, u32[]{:S(2)}, u32[]{:S(2)}) async-start(bf16[4,80,2048]{2,1,0:T(8,128)(2,1)} %bitcast.15), calls=%async_computation.1 | async-start | bytes 2621440 | tf_op jit(solution)/shard_map/all_to_all | solution.py:509
  79.7 18.4 %collective-permute-start.17 = (bf16[176,2048]{1,0:T(8,128)(2,1)}, bf16[176,2048]{1,0:T(8,128)(2,1)S(1)}, u32[]{:S(2)}, u32[]{:S(2)}) collective-permute-start(bf16[176,2048]{1,0:T(8,128)(2,1)} %bitcast.50), channel_id=1, source_target_pairs={{0,2},{1,3},{2,0},{3,1},{4,6},{5,7},{6,4},{7,5},{8,10},{9,11},{10,... | collective-permute-start | bytes 2162696 | tf_op jit(solution)/shard_map/ppermute | solution.py:337
  80.9 23.8 %collective-permute-start.16 = (bf16[128,2048]{1,0:T(8,128)(2,1)S(1)}, bf16[128,2048]{1,0:T(8,128)(2,1)S(1)}, u32[]{:S(2)}, u32[]{:S(2)}) collective-permute-start(bf16[128,2048]{1,0:T(8,128)(2,1)S(1)} %get-tuple-element.115.refs_0_), channel_id=1, source_target_pairs={{0,16},{4,20},{8,24},{12,28},{16,0},{20,4},{24,8},{28,12},{1,17},{... | collective-permute-start | bytes 1572872 | tf_op jit(solution)/shard_map/ppermute | solution.py:440
  109.9 20.8 %all-to-all-start.2 = ((bf16[4,80,2048]{2,1,0:T(8,128)(2,1)}), bf16[4,80,2048]{2,1,0:T(8,128)(2,1)}, u32[]{:S(2)}, u32[]{:S(2)}) async-start(bf16[4,80,2048]{2,1,0:T(8,128)(2,1)} %bitcast.38), calls=%async_computation.2 | async-start | bytes 2621440 | tf_op jit(solution)/shard_map/all_to_all | solution.py:509
  115.2 13.9 %collective-permute-start.24 = (bf16[128,2048]{1,0:T(8,128)(2,1)S(1)}, bf16[128,2048]{1,0:T(8,128)(2,1)S(1)}, u32[]{:S(2)}, u32[]{:S(2)}) collective-permute-start(bf16[128,2048]{1,0:T(8,128)(2,1)S(1)} %get-tuple-element.115.refs_0_), channel_id=1, source_target_pairs={{0,2},{1,3},{2,0},{3,1},{4,6},{5,7},{6,4},{7,5},{8,10},{9,11},{10,... | collective-permute-start | bytes 1572872 | tf_op jit(solution)/shard_map/ppermute | solution.py:337
  138.0 20.1 %all-to-all-start.3 = ((bf16[4,80,2048]{2,1,0:T(8,128)(2,1)}), bf16[4,80,2048]{2,1,0:T(8,128)(2,1)S(1)}, u32[]{:S(2)}, u32[]{:S(2)}) async-start(bf16[4,80,2048]{2,1,0:T(8,128)(2,1)} %bitcast.41), calls=%async_computation.3 | async-start | bytes 2621440 | tf_op jit(solution)/shard_map/all_to_all | solution.py:509
  142.3 14.0 %collective-permute-start.25 = (bf16[128,2048]{1,0:T(8,128)(2,1)S(1)}, bf16[128,2048]{1,0:T(8,128)(2,1)}, u32[]{:S(2)}, u32[]{:S(2)}) collective-permute-start(bf16[128,2048]{1,0:T(8,128)(2,1)S(1)} %get-tuple-element.112.refs_0_), channel_id=1, source_target_pairs={{0,2},{1,3},{2,0},{3,1},{4,6},{5,7},{6,4},{7,5},{8,10},{9,11},{10,... | collective-permute-start | bytes 1572872 | tf_op jit(solution)/shard_map/ppermute | solution.py:337
  158.1 32.3 %all-to-all-start.4 = ((bf16[4,80,2048]{2,1,0:T(8,128)(2,1)}), bf16[4,80,2048]{2,1,0:T(8,128)(2,1)S(1)}, u32[]{:S(2)}, u32[]{:S(2)}) async-start(bf16[4,80,2048]{2,1,0:T(8,128)(2,1)} %bitcast.39), calls=%async_computation.4 | async-start | bytes 2621440 | tf_op jit(solution)/shard_map/all_to_all | solution.py:509
  163.5 24.9 %collective-permute-start.30 = (bf16[128,2048]{1,0:T(8,128)(2,1)}, bf16[128,2048]{1,0:T(8,128)(2,1)S(1)}, u32[]{:S(2)}, u32[]{:S(2)}) collective-permute-start(bf16[128,2048]{1,0:T(8,128)(2,1)} %shard_map.206), channel_id=1, source_target_pairs={{0,16},{4,20},{8,24},{12,28},{16,0},{20,4},{24,8},{28,12},{1,17},{... | collective-permute-start | bytes 1572872 | tf_op jit(solution)/shard_map/ppermute | solution.py:440
  167.8 20.5 %collective-permute-start.29 = (bf16[128,2048]{1,0:T(8,128)(2,1)}, bf16[128,2048]{1,0:T(8,128)(2,1)}, u32[]{:S(2)}, u32[]{:S(2)}) collective-permute-start(bf16[128,2048]{1,0:T(8,128)(2,1)} %add_convert_fusion), channel_id=1, source_target_pairs={{0,2},{1,3},{2,0},{3,1},{4,6},{5,7},{6,4},{7,5},{8,10},{9,11},{10,... | collective-permute-start | bytes 1572872 | tf_op jit(solution)/shard_map/ppermute | solution.py:337
  (57 other events, 554.8 us)

commit v3 on v2

--- a/solution.py
+++ b/solution.py
@@ -84,23 +84,67 @@
         out_ref[...] = jnp.dot(out_ref[...], order[0][...], preferred_element_type=F32).astype(BF16)
 
 
-def route_kernel(experts, parts, base_ref, routing_ref, pick_ref, high_ref, low_ref):
-    rows = routing_ref.shape[0]
-    numbers = (lax.broadcasted_iota(jnp.int32, (rows, experts), 1) + base_ref[0]).astype(F32)
-    found = [routing_ref[:, k : k + 1] == numbers for k in range(TOP)]
-    member = jnp.where(found[0] | found[1] | found[2] | found[3], 1.0, 0.0)
+def fill_table(routes_ref, weights_ref):
+    weights = weights_ref[...]
+    high = weights.astype(BF16)
+    low = (weights - high.astype(F32)).astype(BF16)
+    parts = [routes_ref[...].astype(F32), high.astype(F32), low.astype(F32), jnp.zeros(weights.shape, F32)]
+    return jnp.concatenate(parts, axis=0).astype(BF16)
+
+
+def table_kernel(routes_ref, weights_ref, table_ref):
+    table_ref[...] = fill_table(routes_ref, weights_ref)
+
+
+def near_kernel(weight_ref, prefix_ref, routes_ref, weights_ref, near_ref, table_ref):
+    table = fill_table(routes_ref, weights_ref)
+    table_ref[...] = table
+    rows = weight_ref.shape[0]
+    near_ref[:, :D] = weight_ref[...]
+    count = rows // prefix_ref.shape[0]
+    narrow = D // count
+    lines = lax.broadcasted_iota(jnp.int32, (rows, prefix_ref.shape[0]), 0)
+    columns = lax.broadcasted_iota(jnp.int32, (rows, prefix_ref.shape[0]), 1) * count
+    prefix = jnp.zeros((rows, narrow), F32)
+    for number in range(count):
+        spot = jnp.where(lines == columns + number, 1.0, 0.0).astype(BF16)
+        prefix = prefix + jnp.dot(
+            spot, prefix_ref[:, number * narrow : (number + 1) * narrow], preferred_element_type=F32
+        )
+    near_ref[:, D : D + narrow] = prefix.astype(BF16)
+    near_ref[: 4 * TOP, D + narrow :] = table
+    near_ref[4 * TOP :, D + narrow :] = jnp.zeros((rows - 4 * TOP, table.shape[1]), BF16)
+
+
+def route_kernel(experts, parts, relative, halves, place_ref, table_ref, pick_ref, high_ref, low_ref):
+    rows = table_ref.shape[1]
+    unit = jnp.where(
+        lax.broadcasted_iota(jnp.int32, (4 * TOP, 4 * TOP), 0) == lax.broadcasted_iota(jnp.int32, (4 * TOP, 4 * TOP), 1),
+        1.0,
+        0.0,
+    ).astype(BF16)
+    routing = lax.dot_general(table_ref[...], unit, (((0,), (0,)), ((), ())), preferred_element_type=F32)
+    plain = lax.broadcasted_iota(jnp.int32, (rows, experts), 1)
     above = lax.broadcasted_iota(jnp.int32, (rows, rows), 0) > lax.broadcasted_iota(
         jnp.int32, (rows, rows), 1
     )
-    rank = jnp.dot(
-        jnp.where(above, 1.0, 0.0).astype(BF16), member.astype(BF16), preferred_element_type=F32
-    )
-    rank = jnp.where(member > 0.5, rank, -1.0).astype(BF16)
-    weight = jnp.zeros(member.shape, F32)
-    for k in range(TOP):
-        weight = weight + jnp.where(found[k], routing_ref[:, TOP + k : TOP + k + 1], 0.0)
-    high = weight.astype(BF16)
-    low = (weight - high.astype(F32)).astype(BF16)
+    above = jnp.where(above, 1.0, 0.0).astype(BF16)
+
+    def places(turned):
+        numbers = plain
+        if halves:
+            numbers = plain ^ place_ref[0] if turned else plain + (place_ref[0] & -experts)
+        found = [routing[:, k : k + 1] == numbers.astype(F32) for k in range(TOP)]
+        member = jnp.where(found[0] | found[1] | found[2] | found[3], 1.0, 0.0)
+        rank = jnp.dot(above, member.astype(BF16), preferred_element_type=F32)
+        return found, jnp.where(member > 0.5, rank, -1.0).astype(BF16)
+
+    _, pick_rank = places(relative)
+    found, rank = places(not relative)
+    high, low = [
+        sum(jnp.where(found[k], routing[:, at + k : at + k + 1], 0.0) for k in range(TOP)).astype(BF16)
+        for at in (TOP, 2 * TOP)
+    ]
     at = 0
     for first, count in parts:
         slots = experts * count
@@ -114,7 +158,7 @@
         expert_column = layout((slots, experts), 0)[0]
         columns = lax.broadcasted_iota(jnp.int32, (slots, experts), 1).astype(F32)
         select = jnp.where(expert_column == columns, 1.0, 0.0).astype(BF16)
-        wanted = lax.dot_general(select, rank, NT, preferred_element_type=F32)
+        wanted = lax.dot_general(select, pick_rank, NT, preferred_element_type=F32)
         pick_ref[at : at + slots, :] = jnp.where(wanted == place, 1.0, 0.0).astype(BF16)
         expert_row = layout((experts, slots), 1)[0]
         lines = lax.broadcasted_iota(jnp.int32, (experts, slots), 0).astype(F32)
@@ -128,7 +172,7 @@
 
 def project_kernel(count, attn_ref, residual_ref, gain_ref, router_ref, pick_ref, *refs):
     pieces, refs = refs[:count], refs[count:]
-    normed_out, state_out, slots_out, normed_rows, state, picked, sems = refs
+    normed_out, state_out, *slots_out, normed_rows, state, picked, sems = refs
     step = 512
     square = jnp.zeros((attn_ref.shape[0], 1), F32)
     moves = []
@@ -162,18 +206,21 @@
             normed.astype(F32) * router_ref[:, cols].astype(F32), axis=1, keepdims=True
         )
         picked[:, cols] = jnp.dot(pick_ref[...], normed, preferred_element_type=F32).astype(BF16)
-        move(picked, slots_out, 1, at)
+        row = 0
+        for number, ref in enumerate(slots_out):
+            move(picked.at[pl.ds(row, ref.shape[0])], ref, 3 + number, at)
+            row += ref.shape[0]
     state[:, D:] = jnp.broadcast_to(jax.nn.sigmoid(logit), (state.shape[0], HD))
     move(state, state_out, 0, D, HD)
     for copy in moves:
         copy.wait()
 
 
-def ffn_kernel(xs, shards, outs, *refs):
+def ffn_kernel(xs, shards, outs, turn, place_ref, *refs):
     x_refs, refs = refs[:xs], refs[xs:]
     sources, refs = [refs[kind * shards : (kind + 1) * shards] for kind in range(3)], refs[3 * shards :]
     out_refs, refs = refs[:outs], refs[outs:]
-    x, *weights, hidden, result, sems = refs
+    x, *weights, hidden, result, sems, out_sems = refs
     gate, up, down = weights
     chunk = 256
     hid = gate.shape[0]
@@ -220,32 +267,43 @@
     for copy in copies[2]:
         copy.wait()
     moves = []
+    size_of = x.shape[0] // max(turn, 1)
     for number, at in enumerate(range(0, D, chunk)):
         cols = slice(at, at + chunk)
         result[:, cols] = jnp.dot(hidden[...], down[:, cols], preferred_element_type=F32).astype(BF16)
         row = 0
-        for ref in out_refs:
+        for block in range(max(turn, outs)):
+            if turn:
+                other = pl.multiple_of(((place_ref[0] & (turn - 1)) ^ block) * size_of, size_of)
+                if outs > 1:
+                    source, first, target = other, 0, out_refs[block]
+                else:
+                    source, first, target = block * size_of, other, out_refs[0]
+                count = size_of
+            else:
+                source, first, target = row, 0, out_refs[block]
+                count = target.shape[0]
+                row += count
             moves.append(
                 pltpu.make_async_copy(
-                    result.at[pl.ds(row, ref.shape[0]), pl.ds(at, chunk)],
-                    ref.at[:, pl.ds(at, chunk)],
-                    sems.at[3 if row == 0 else 5, number],
+                    result.at[pl.ds(source, count), pl.ds(at, chunk)],
+                    target.at[pl.ds(first, count), pl.ds(at, chunk)],
+                    out_sems.at[block, number],
                 )
             )
             moves[-1].start()
-            row += ref.shape[0]
     for move in moves:
         move.wait()
 
 
-def ffn(x_list, weights, out_rows):
+def ffn(x_list, weights, out_rows, place, turn=0):
     rows = sum(x.shape[0] for x in x_list)
     hid = sum(w.shape[0] for w in weights[0])
     spec = ANY if len(weights[0]) > 1 else HBM
     return pl.pallas_call(
-        functools.partial(ffn_kernel, len(x_list), len(weights[0]), len(out_rows)),
+        functools.partial(ffn_kernel, len(x_list), len(weights[0]), len(out_rows), turn),
         out_shape=[jax.ShapeDtypeStruct((n, D), BF16) for n in out_rows],
-        in_specs=[ANY] * len(x_list) + [spec] * (3 * len(weights[0])),
+        in_specs=[SMEM] + [ANY] * len(x_list) + [spec] * (3 * len(weights[0])),
         out_specs=[HBM] * len(out_rows),
         scratch_shapes=[
             pltpu.VMEM((rows, D), BF16),
@@ -254,26 +312,32 @@
             pltpu.VMEM((hid, D), BF16),
             pltpu.VMEM((rows, hid), BF16),
             pltpu.VMEM((rows, D), BF16),
-            pltpu.SemaphoreType.DMA((6, 8)),
+            pltpu.SemaphoreType.DMA((5, 8)),
+            pltpu.SemaphoreType.DMA((max(turn, len(out_rows)), 8)),
         ],
         compiler_params=pltpu.CompilerParams(vmem_limit_bytes=56 << 20),
         cost_estimate=pl.CostEstimate(
             flops=6 * rows * hid * D, bytes_accessed=6 * hid * D + 4 * rows * D, transcendentals=rows * hid
         ),
-    )(*x_list, *weights[0], *weights[1], *weights[2])
-
-
-def combine_kernel(count, high_ref, low_ref, *refs):
+    )(place, *x_list, *weights[0], *weights[1], *weights[2])
+
+
+def combine_kernel(count, backs, high_ref, low_ref, *refs):
     sources, out_ref, refs = refs[:count], refs[count], refs[count + 1 :]
-    held, result, sems = refs[:count], refs[count], refs[count + 1]
+    *held, back, result, sems = refs
     rows = result.shape[0]
+    targets = list(held)
+    row = 0
+    for source in sources[count - backs :]:
+        targets.append(back.at[pl.ds(row, source.shape[0])])
+        row += source.shape[0]
     loads = []
-    for number, (source, target) in enumerate(zip(sources, held)):
+    for number, (source, target) in enumerate(zip(sources, targets)):
         loads.append(pltpu.make_async_copy(source.at[pl.ds(0, target.shape[0])], target, sems.at[0, number]))
         loads[-1].start()
     for load in loads:
         load.wait()
-    state, keep, sib, far, back, *relayed = held
+    state, keep, sib, far, *relayed = held
     scale = state[:, D : D + 1]
     step = 512
     moves = []
@@ -293,26 +357,38 @@
         move.wait()
 
 
-def pick_kernel(pick_ref, rows_ref, out_ref, picked, sems):
+def pick_kernel(pick_ref, rows_ref, *refs):
+    *out_refs, picked, sems = refs
     step = 512
     moves = []
     for at in range(0, D, step):
         cols = slice(at, at + step)
         picked[:, cols] = jnp.dot(pick_ref[...], rows_ref[:, cols], preferred_element_type=F32).astype(BF16)
-        window = (slice(None), pl.ds(at, step))
-        moves.append(pltpu.make_async_copy(picked.at[window], out_ref.at[window], sems.at[at // step]))
-        moves[-1].start()
+        row = 0
+        for number, ref in enumerate(out_refs):
+            source = picked.at[pl.ds(row, ref.shape[0]), pl.ds(at, step)]
+            moves.append(pltpu.make_async_copy(source, ref.at[:, pl.ds(at, step)], sems.at[number, at // step]))
+            moves[-1].start()
+            row += ref.shape[0]
     for move in moves:
         move.wait()
 
 
-def relay_kernel(high_ref, low_ref, back_ref, out_ref):
+def relay_kernel(high_ref, low_ref, *refs):
+    sources, (out_ref, back, sems) = refs[:-3], refs[-3:]
+    loads = []
+    row = 0
+    for number, ref in enumerate(sources):
+        loads.append(pltpu.make_async_copy(ref, back.at[pl.ds(row, ref.shape[0])], sems.at[number]))
+        loads[-1].start()
+        row += ref.shape[0]
+    for load in loads:
+        load.wait()
     step = 512
     for at in range(0, D, step):
         cols = slice(at, at + step)
-        back = back_ref[:, cols]
-        routed = jnp.dot(high_ref[...], back, preferred_element_type=F32) + jnp.dot(
-            low_ref[...], back, preferred_element_type=F32
+        routed = jnp.dot(high_ref[...], back[:, cols], preferred_element_type=F32) + jnp.dot(
+            low_ref[...], back[:, cols], preferred_element_type=F32
         )
         out_ref[:, cols] = routed.astype(BF16)
 
@@ -342,19 +418,34 @@
     return lax.ppermute(array, "req", [(i - distance, i) for i in devices if i - distance in devices])
 
 
-def pack_kernel(ring_0, ring_1, ring_2, ring_3, first_ref, second_ref):
-    half = ring_0.shape[0] // 2
-    for number, ref in enumerate((ring_0, ring_1, ring_2, ring_3)):
-        first_ref[number * half : (number + 1) * half, :] = ref[:half, :]
-        second_ref[number * half : (number + 1) * half, :] = ref[half:, :]
-
-
-def join_kernel(first_ref, first_far, second_ref, second_far, first_out, second_out):
+def pack_kernel(ring_0, ring_1, ring_2, ring_3, first_ref, second_ref, table_ref):
+    half = second_ref.shape[0] // 4
+    ring = (ring_0, ring_1, ring_2, ring_3)
+    narrow = ring_0.shape[1] - D - table_ref.shape[1]
+    count = D // narrow
+    for number, ref in enumerate(ring):
+        first_ref[number * half : (number + 1) * half, :] = ref[:half, :D]
+        second_ref[number * half : (number + 1) * half, :] = ref[half:, :D]
+    table_ref[...] = ring_2[: 4 * TOP, D + narrow :]
+    prefix = jnp.concatenate([ref[:, D : D + narrow] for ref in ring], axis=0)
+    lines = lax.broadcasted_iota(jnp.int32, (half, prefix.shape[0]), 0) * count
+    columns = lax.broadcasted_iota(jnp.int32, (half, prefix.shape[0]), 1)
+    for number in range(count):
+        spot = jnp.where(lines + number == columns, 1.0, 0.0).astype(BF16)
+        first_ref[4 * half :, number * narrow : (number + 1) * narrow] = jnp.dot(
+            spot, prefix, preferred_element_type=F32
+        ).astype(BF16)
+
+
+def join_kernel(first_ref, first_far, second_ref, second_far, first_out, second_out, prefix_out):
     rows = second_ref.shape[0]
-    first_out[:rows, :] = first_ref[...]
-    first_out[rows:, :] = first_far[...]
+    first_out[:rows, :] = first_ref[:rows, :]
+    first_out[rows:, :] = first_far[:rows, :]
     second_out[:rows, :] = second_ref[...]
     second_out[rows:, :] = second_far[...]
+    half = prefix_out.shape[0] // 2
+    prefix_out[:half, :] = first_ref[rows:, :]
+    prefix_out[half:, :] = first_far[rows:, :]
 
 
 def over_y(array):
@@ -423,23 +514,19 @@
         [SMEM, SMEM] + [VMEM] * 4,
     )(lengths, place, inverse, suffix_queries[0], suffix_keys[0], suffix_values[0])
 
-    routing = jnp.concatenate([routes[0].astype(F32), route_weights[0]], axis=1)
     halves = requests == 8
     experts = requests // 2 if halves else requests
-    base = (req // experts * experts).astype(jnp.int32)[None]
     slots = experts * capacity
 
-    def route(table):
+    def route(table, relative):
         return vmem_call(
-            functools.partial(route_kernel, experts, [(0, capacity)]),
+            functools.partial(route_kernel, experts, [(0, capacity)], relative, halves),
             [shape(slots, rows), shape(rows, slots), shape(rows, slots)],
             [SMEM, VMEM],
-        )(base, table)
+        )(place, table)
 
     def across(array):
         return lax.ppermute(array, "req", [(i, i ^ requests // 2) for i in range(requests)])
-
-    pick, high, low = route(routing)
 
     def attend(prefix_rows, history, order):
         return vmem_call(
@@ -450,53 +537,58 @@
         )(lengths, place, query_turned, prefix_rows, own_cache, *history, *order)
 
     mine = [jnp.swapaxes(expert_gate[0], 0, 1), jnp.swapaxes(expert_up[0], 0, 1), expert_down[0]]
-    part = prefix_cache[0].reshape(-1, HD)
-    prefix_rows = lax.all_to_all(
-        jnp.broadcast_to(part[None], (requests, *part.shape)), "req", split_axis=0, concat_axis=0, tiled=True
-    ).reshape(prefix_len, 2 * WIDTH)
+    tables = [jnp.swapaxes(routes[0], 0, 1), jnp.swapaxes(route_weights[0], 0, 1)]
     if halves:
-        far_routing = across(routing)
         half = out_weight.shape[0] // 2
-        ring = gather_ring(out_weight)
+        extra = prefix_cache.shape[1] * D // out_weight.shape[0] + rows
+        near, table = vmem_call(
+            near_kernel, [shape(2 * half, D + extra), shape(4 * TOP, rows)], [VMEM] * 4
+        )(out_weight, prefix_cache[0], *tables)
+        ring = gather_ring(near)
         far_gate = grp_move(mine[0], 2)
-        *ring, late_cache, late_up, far_gate, far_routing, prefix_rows = lax.optimization_barrier(
-            (*ring, own_cache, mine[1], far_gate, far_routing, prefix_rows)
-        )
-        first, second = vmem_call(pack_kernel, [shape(4 * half, D), shape(4 * half, D)], [VMEM] * 4)(*ring)
+        history = [req_shift(own_cache, 1)]
+        *ring, late_cache, far_gate = lax.optimization_barrier((*ring, own_cache, far_gate))
+        first, second, far_table = vmem_call(
+            pack_kernel, [shape(5 * half, D), shape(4 * half, D), shape(4 * TOP, rows)], [VMEM] * 4
+        )(*ring)
         first, second, late_cache = lax.optimization_barrier((first, second, late_cache))
         first_far, second_far = over_y(first), grp_move(second, 2)
-        history = [req_shift(late_cache, distance) for distance in range(1, depth + 1)]
-        far_pick, far_high, far_low = route(far_routing)
+        history += [req_shift(late_cache, distance) for distance in range(2, depth + 1)]
+        pick, high, low = route(table, True)
+        far_pick, far_high, far_low = route(far_table, False)
         order = vmem_call(order_kernel, shape(WIDTH, WIDTH), [SMEM])(place)
-        far_up = grp_move(late_up, 2)
-        first_far, second_far, order, pick, far_pick, far_up = lax.optimization_barrier(
-            (first_far, second_far, order, pick, far_pick, far_up)
-        )
-        first, second = vmem_call(
-            join_kernel, [shape(8 * half, D), shape(8 * half, D)], [VMEM] * 4
+        first_far, second_far, order, pick, far_pick = lax.optimization_barrier(
+            (first_far, second_far, order, pick, far_pick)
+        )
+        first, second, prefix_rows = vmem_call(
+            join_kernel, [shape(8 * half, D), shape(8 * half, D), shape(2 * half, D)], [VMEM] * 4
         )(first, first_far, second, second_far)
         attention = attend(prefix_rows, history, [order])
         near = [first, second, grp_move(first, 1), grp_move(second, 1)]
         far = [grp_move(first, 2), over_y(second)]
-        *far, attention, late_down = lax.optimization_barrier((*far, attention, mine[2]))
+        far, attention, late_up, late_down = lax.optimization_barrier((far, attention, mine[1], mine[2]))
         pieces = near[:2] + far + near[2:] + [grp_move(array, 1) for array in far]
-        far_down = grp_move(late_down, 2)
+        far_up, far_down = grp_move(late_up, 2), grp_move(late_down, 2)
     else:
+        (table,) = vmem_call(table_kernel, [shape(4 * TOP, rows)], [VMEM] * 2)(*tables)
+        pick, high, low = route(table, False)
         pieces = [lax.all_gather(out_weight, ("req", "grp"), axis=0, tiled=True)]
+        prefix_rows = lax.all_gather(prefix_cache[0], "req", axis=0, tiled=True)
         history = [req_shift(own_cache, distance) for distance in range(1, depth + 1)]
         attention = attend(prefix_rows, history, [])
         far_gate, far_up, far_down = [grp_move(w, 2) for w in mine]
 
-    normed, state, outgoing = pl.pallas_call(
+    shares = [capacity] * experts if halves else [slots]
+    normed, state, *outgoing = pl.pallas_call(
         functools.partial(project_kernel, len(pieces)),
-        out_shape=[shape(rows, D), shape(rows, D + HD, dtype=F32), shape(slots, D)],
+        out_shape=[shape(rows, D), shape(rows, D + HD, dtype=F32)] + [shape(n, D) for n in shares],
         in_specs=[VMEM] * (5 + len(pieces)),
-        out_specs=[HBM] * 3,
+        out_specs=[HBM] * (2 + len(shares)),
         scratch_shapes=[
             pltpu.VMEM((rows, D), BF16),
             pltpu.VMEM((rows, D + HD), F32),
             pltpu.VMEM((slots, D), BF16),
-            pltpu.SemaphoreType.DMA((3, 5)),
+            pltpu.SemaphoreType.DMA((3 + len(shares), 5)),
         ],
         compiler_params=pltpu.CompilerParams(vmem_limit_bytes=16 << 20),
         cost_estimate=pl.CostEstimate(flops=2 * rows * WIDTH * D, bytes_accessed=8 << 20, transcendentals=0),
@@ -510,64 +602,90 @@
             split, "req", split_axis=0, concat_axis=0, axis_index_groups=groups, tiled=True
         ).reshape(slots, D)
 
+    def trade(arrays):
+        if not halves:
+            return [exchange(arrays[0])]
+        return [arrays[0]] + [
+            lax.ppermute(array, "req", [(i, i ^ flip) for i in range(requests)])
+            for flip, array in enumerate(arrays)
+            if flip
+        ]
+
     def both(own, other):
         return [own, grp_move(own, 1), other, grp_move(other, 1)]
 
-    gates, ups = both(mine[0], far_gate), both(mine[1], far_up)
-    arrived = exchange(outgoing)
-    late_normed, late_cache, far_rows = normed, own_cache, None
+    def shared(normed, far_rows):
+        return ffn(
+            [normed, far_rows, grp_move(normed, 1), grp_move(far_rows, 1)],
+            [[jnp.swapaxes(shared_gate, 0, 1)], [jnp.swapaxes(shared_up, 0, 1)], [shared_down]],
+            [2 * rows, 2 * rows],
+            place,
+        )
+
+    def spread(send, keep):
+        from_sib = grp_move(send, 1)
+        pair_sum = (keep[rows:].astype(F32) + from_sib[rows:].astype(F32)).astype(BF16)
+        return from_sib, grp_move(pair_sum, 2)
+
+    def all_weights(*others):
+        return [both(own, other) for own, other in zip(mine, others)]
+
+    arrived = trade(outgoing)
+    relayed = []
     if halves:
         relay_rows = across(normed)
-        relay_rows, arrived, late_normed, far_down, gates, ups = lax.optimization_barrier(
-            (relay_rows, arrived, normed, far_down, gates, ups)
-        )
-        relay_out = pl.pallas_call(
+        relay_rows, arrived, late_normed, far_gate, far_up, far_down, late_cache = lax.optimization_barrier(
+            (relay_rows, arrived, normed, far_gate, far_up, far_down, own_cache)
+        )
+        (relay_out,) = pl.pallas_call(
             pick_kernel,
-            out_shape=shape(slots, D),
+            out_shape=[shape(slots, D)],
             in_specs=[VMEM] * 2,
-            out_specs=HBM,
-            scratch_shapes=[pltpu.VMEM((slots, D), BF16), pltpu.SemaphoreType.DMA((4,))],
+            out_specs=[HBM],
+            scratch_shapes=[pltpu.VMEM((slots, D), BF16), pltpu.SemaphoreType.DMA((1, 4))],
         )(far_pick, relay_rows)
         relay_arrived = exchange(relay_out)
-    weights = [gates, ups, both(mine[2], far_down)]
-    far_rows = grp_move(late_normed, 2)
-    (finished,) = ffn([arrived], weights, [slots])
-    if halves:
-        relay_arrived, finished, late_cache, far_rows = lax.optimization_barrier(
-            (relay_arrived, finished, own_cache, far_rows)
-        )
-        (relay_finished,) = ffn([relay_arrived], weights, [slots])
-        relay_back = exchange(relay_finished)
+        far_rows = grp_move(late_normed, 2)
+        weights = all_weights(far_gate, far_up, far_down)
+        finished = ffn(arrived, weights, [slots], place, experts)
+        relay_arrived, finished, far_rows, weights, late_cache = lax.optimization_barrier(
+            (relay_arrived, finished, far_rows, weights, late_cache)
+        )
+        relay_finished = ffn([relay_arrived], weights, shares, place, experts)
+        relay_back = trade(relay_finished)
+        partner = grp_move(late_cache, 2)
         relay_finished, normed, far_rows = lax.optimization_barrier((relay_finished, normed, far_rows))
-    keep, send = ffn(
-        [normed, far_rows, grp_move(normed, 1), grp_move(far_rows, 1)],
-        [[jnp.swapaxes(shared_gate, 0, 1)], [jnp.swapaxes(shared_up, 0, 1)], [shared_down]],
-        [2 * rows, 2 * rows],
-    )
-    partner = grp_move(late_cache, 2)
-    if halves:
-        relay_back, partner, finished, keep, send = lax.optimization_barrier(
-            (relay_back, partner, finished, keep, send)
-        )
-    from_sib = grp_move(send, 1)
-    pair_sum = (keep[rows:].astype(F32) + from_sib[rows:].astype(F32)).astype(BF16)
-    from_far = grp_move(pair_sum, 2)
-    relayed = []
-    if halves:
-        relay_sum = vmem_call(relay_kernel, shape(rows, D), [VMEM] * 3)(far_high, far_low, relay_back)
+        keep, send = shared(normed, far_rows)
+        relay_back, finished, keep, send, partner = lax.optimization_barrier(
+            (relay_back, finished, keep, send, partner)
+        )
+        relay_sum = pl.pallas_call(
+            relay_kernel,
+            out_shape=shape(rows, D),
+            in_specs=[VMEM] * 2 + [ANY] * experts,
+            out_specs=VMEM,
+            scratch_shapes=[pltpu.VMEM((slots, D), BF16), pltpu.SemaphoreType.DMA((experts,))],
+            compiler_params=pltpu.CompilerParams(vmem_limit_bytes=32 << 20),
+        )(far_high, far_low, *relay_back)
         relayed = [across(relay_sum)]
-    back = exchange(finished)
-
-    sources = [state, keep, from_sib, from_far, back, *relayed]
-    kept = [(rows, D + HD)] + [(rows, D)] * 3 + [(slots, D)] + [(rows, D)] * len(relayed)
+        from_sib, from_far = spread(send, keep)
+    else:
+        finished = ffn(arrived, all_weights(far_gate, far_up, far_down), shares, place)
+        keep, send = shared(normed, grp_move(normed, 2))
+        from_sib, from_far = spread(send, keep)
+        partner = grp_move(own_cache, 2)
+    back = [exchange(finished[0])]
+
+    sources = [state, keep, from_sib, from_far, *relayed, *back]
+    kept = [(rows, D + HD)] + [(rows, D)] * (3 + len(relayed)) + [(slots, D)]
     final = pl.pallas_call(
-        functools.partial(combine_kernel, len(sources)),
+        functools.partial(combine_kernel, len(sources), len(back)),
         out_shape=shape(rows, D),
         in_specs=[VMEM] * 2 + [ANY] * len(sources),
         out_specs=HBM,
         scratch_shapes=[pltpu.VMEM(dims, source.dtype) for dims, source in zip(kept, sources)]
-        + [pltpu.VMEM((rows, D), BF16), pltpu.SemaphoreType.DMA((2, 8))],
-        compiler_params=pltpu.CompilerParams(vmem_limit_bytes=32 << 20),
+        + [pltpu.VMEM((rows, D), BF16), pltpu.SemaphoreType.DMA((2, 16))],
+        compiler_params=pltpu.CompilerParams(vmem_limit_bytes=56 << 20),
         cost_estimate=pl.CostEstimate(flops=4 * slots * rows * D, bytes_accessed=8 << 20, transcendentals=0),
     )(high, low, *sources)
 

time: 196 us -> 191 us (0.974)
  Pallas kernels: 43.6 us -> 47 us
  starting transfers between devices: 54.8 us -> 51.4 us
  other arithmetic: 5.63 us -> 3.46 us
    ppermute x0 -> x6, waiting for transfers between devices: none -> 13.7 us  [trade(): lax.ppermute(array, 'req', [(i, i ^ flip) for i in range(requests)])]
    ppermute x2, waiting for transfers between devices: 10.9 us -> 3.33 us  [over_y(): return lax.ppermute(array, 'req', [(i, i ^ 1) for i in range(8)])]
    all_to_all x4 -> x2, starting transfers between devices: 15.9 us -> 8.3 us  [exchange(): lax.all_to_all(split, 'req', split_axis=0, concat_axis=0, axis_index_grou...]
    ppermute x0 -> x6, starting transfers between devices: none -> 7.42 us  [trade(): lax.ppermute(array, 'req', [(i, i ^ flip) for i in range(requests)])]
    all_to_all x4 -> x2, waiting for transfers between devices: 7.52 us -> 0.71 us  [exchange(): lax.all_to_all(split, 'req', split_axis=0, concat_axis=0, axis_index_grou...]
    all_to_all x1 -> x0, starting transfers between devices: 3.37 us -> none  [local(): lax.all_to_all(jnp.broadcast_to(part[None], (requests, *part.shape)), 're...]
    ppermute x3, waiting for transfers between devices: 0.01 us -> 3.04 us  [gather_ring(): lax.ppermute(array, 'req', [(i, (i + 2 * d) % 8) for i in range(8)])]
    ppermute x2, starting transfers between devices: 2.48 us -> 4.96 us  [over_y(): return lax.ppermute(array, 'req', [(i, i ^ 1) for i in range(8)])]
  transfers between devices with their start and end apart: 36 -> 38, of which waited for: 21 -> 19; matrix products, arithmetic and copies ran while one was open for 4% -> 2% of each run, Pallas kernels for 14% -> 17%
where the time goes in v3:
time: 191 us; the launch traced here: 190 us
  waiting for transfers between devices  72.8 us (38%)
  starting transfers between devices  51.4 us (27%)
  Pallas kernels  47 us (25%)
  local copies, waits for them, and re-layouts  14.4 us (8%)
  other arithmetic  3.46 us (2%)
    ppermute x21, waiting for transfers between devices, grp_move(): lax.ppermute(array, 'grp', [(i, i ^ flip) for i in range(lax.axis_size('g...  30.2 us
    pallas_call x3, Pallas kernels, ffn(): pl.pallas_call(functools.partial(ffn_kernel, len(x_list), len(weights[0])...  26.3 us
    ppermute x2, waiting for transfers between devices, across(): lax.ppermute(array, 'req', [(i, i ^ requests // 2) for i in range(request...  21.8 us
    unnamed x88, local copies, waits for them, and re-layouts  14.3 us
    ppermute x6, waiting for transfers between devices, trade(): lax.ppermute(array, 'req', [(i, i ^ flip) for i in range(requests)])  13.7 us
    ppermute x21, starting transfers between devices, grp_move(): lax.ppermute(array, 'grp', [(i, i ^ flip) for i in range(lax.axis_size('g...  12.4 us
    all_to_all x2, starting transfers between devices, exchange(): lax.all_to_all(split, 'req', split_axis=0, concat_axis=0, axis_index_grou...  8.3 us
    ppermute x6, starting transfers between devices, trade(): lax.ppermute(array, 'req', [(i, i ^ flip) for i in range(requests)])  7.42 us
  transfers between devices with their start and end apart: 38, of which 19 were waited for; matrix products, arithmetic and copies ran while one was open for 2% of the time, Pallas kernels for 17%

profile of v3, /device:TPU:0, one launch (start us, length us, event | category | flops | bytes accessed | tf_op | source)
XLA Modules:
  0.0 190.4 jit_solution(14945558573205854356)
XLA Ops:
  0.6 3.0 %collective-permute-start.3 = (bf16[176,2048]{1,0:T(8,128)(2,1)}, bf16[176,2048]{1,0:T(8,128)(2,1)S(1)}, u32[]{:S(2)}, u32[]{:S(2)}) collective-permute-start(bf16[176,2048]{1,0:T(8,128)(2,1)} %bitcast.40), channel_id=1, source_target_pairs={{0,2},{1,3},{2,0},{3,1},{4,6},{5,7},{6,4},{7,5},{8,10},{9,11},{10,... | collective-permute-start | bytes 2162696 | tf_op jit(solution)/shard_map/ppermute | solution.py:413
  6.8 3.6 %collective-permute-start.2 = (bf16[32,2432]{1,0:T(8,128)(2,1)S(1)}, bf16[32,2432]{1,0:T(8,128)(2,1)S(1)}, u32[]{:S(2)}, u32[]{:S(2)}) collective-permute-start(bf16[32,2432]{1,0:T(8,128)(2,1)S(1)} %get-tuple-element.90.ring_0), channel_id=1, source_target_pairs={{0,24},{4,28},{8,0},{12,4},{16,8},{20,12},{24,16},{28,20},{1,25},{... | collective-permute-start | bytes 466952 | tf_op jit(solution)/shard_map/ppermute | solution.py:476
  16.8 3.5 %collective-permute-start.8 = (bf16[128,2048]{1,0:T(8,128)(2,1)S(1)}, bf16[128,2048]{1,0:T(8,128)(2,1)S(1)}, u32[]{:S(2)}, u32[]{:S(2)}) collective-permute-start(bf16[128,2048]{1,0:T(8,128)(2,1)S(1)} %get-tuple-element.157.refs_0_), channel_id=1, source_target_pairs={{0,4},{4,8},{8,12},{12,16},{16,20},{20,24},{24,28},{1,5},{5,9},{9,... | collective-permute-start | bytes 1572872 | tf_op jit(solution)/shard_map/ppermute | solution.py:418
  20.3 3.0 %collective-permute-done.1.ring_2 = bf16[32,2432]{1,0:T(8,128)(2,1)S(1)} collective-permute-done((bf16[32,2432]{1,0:T(8,128)(2,1)S(1)}, bf16[32,2432]{1,0:T(8,128)(2,1)S(1)}, u32[]{:S(2)}, u32[]{:S(2)}) %collective-permute-start.1) | collective-permute-done | bytes 155680 | tf_op jit(solution)/shard_map/ppermute | solution.py:476
  23.5 2.9 %collective-permute-start.9 = (bf16[128,2048]{1,0:T(8,128)(2,1)S(1)}, bf16[128,2048]{1,0:T(8,128)(2,1)S(1)}, u32[]{:S(2)}, u32[]{:S(2)}) collective-permute-start(bf16[128,2048]{1,0:T(8,128)(2,1)S(1)} %get-tuple-element.157.refs_0_), channel_id=1, source_target_pairs={{0,8},{4,12},{8,16},{12,20},{16,24},{20,28},{1,9},{5,13},{9,17},{1... | collective-permute-start | bytes 1572872 | tf_op jit(solution)/shard_map/ppermute | solution.py:418
  26.4 2.5 %collective-permute-start.4 = (bf16[80,2048]{1,0:T(8,128)(2,1)S(1)}, bf16[80,2048]{1,0:T(8,128)(2,1)S(1)}, u32[]{:S(2)}, u32[]{:S(2)}) collective-permute-start(bf16[80,2048]{1,0:T(8,128)(2,1)S(1)} %get-tuple-element.97.first_ref), channel_id=1, source_target_pairs={{0,4},{4,0},{8,12},{12,8},{16,20},{20,16},{24,28},{28,24},{1,5},{5... | collective-permute-start | bytes 983048 | tf_op jit(solution)/shard_map/ppermute | solution.py:452
  38.2 2.5 %collective-permute-start.7 = (bf16[128,2048]{1,0:T(8,128)(2,1)S(1)}, bf16[128,2048]{1,0:T(8,128)(2,1)S(1)}, u32[]{:S(2)}, u32[]{:S(2)}) collective-permute-start(bf16[128,2048]{1,0:T(8,128)(2,1)S(1)} %get-tuple-element.105.refs_1_), channel_id=1, source_target_pairs={{0,4},{4,0},{8,12},{12,8},{16,20},{20,16},{24,28},{28,24},{1,5},{5... | collective-permute-start | bytes 1572872 | tf_op jit(solution)/shard_map/ppermute | solution.py:452
  40.8 3.4 %shard_map.201.attn_ref = bf16[128,1024]{1,0:T(8,128)(2,1)S(1)} custom-call(s32[1,16]{1,0:T(1,128)S(1)} %copy-done.17, s32[2]{0:T(128)S(1)} %pad_add_fusion.place_ref, bf16[128,1024]{1,0:T(8,128)(2,1)S(1)} %get-tuple-element.106.q_ref, bf16[32,2048]{1,0:T(8,128)(2,1)S(1)} %get-tuple-element.107.prefix_ref, bf16[128,2048]{1,0:T(8,128)(2,1)S(1)} %get-tuple-element.157.refs_0_, ...), custom_call_target="tpu_custom_call" | custom-call | flops 20000000000 | bytes 4194304 | tf_op jit(solution)/shard_map/pallas_call | solution.py:532
  44.2 7.6 %collective-permute-done.6.refs_2_ = bf16[128,2048]{1,0:T(8,128)(2,1)S(1)} collective-permute-done((bf16[128,2048]{1,0:T(8,128)(2,1)S(1)}, bf16[128,2048]{1,0:T(8,128)(2,1)S(1)}, u32[]{:S(2)}, u32[]{:S(2)}) %collective-permute-start.6) | collective-permute-done | bytes 524320 | tf_op jit(solution)/shard_map/ppermute | solution.py:413
  55.8 3.6 %shard_map.202 = (bf16[128,2048]{1,0:T(8,128)(2,1)S(1)}, f32[128,2176]{1,0:T(8,128)S(1)}, bf16[80,2048]{1,0:T(8,128)(2,1)S(1)}, bf16[80,2048]{1,0:T(8,128)(2,1)S...) custom-call(bf16[128,1024]{1,0:T(8,128)(2,1)S(1)} %shard_map.201.attn_ref, ...), custom_call_target="tpu_custom_call" | custom-call | flops 536870912 | bytes 8388608 | tf_op jit(solution)/shard_map/pallas_call | solution.py:582
  61.1 7.3 %collective-permute-start.14 = (bf16[128,2048]{1,0:T(8,128)(2,1)S(1)}, bf16[128,2048]{1,0:T(8,128)(2,1)S(1)}, u32[]{:S(2)}, u32[]{:S(2)}) collective-permute-start(bf16[128,2048]{1,0:T(8,128)(2,1)S(1)} %get-tuple-element.153.refs_0_), channel_id=1, source_target_pairs={{0,16},{4,20},{8,24},{12,28},{16,0},{20,4},{24,8},{28,12},{1,17},{... | collective-permute-start | bytes 1572872 | tf_op jit(solution)/shard_map/ppermute | solution.py:529
  68.7 3.9 %collective-permute-done.18.refs_10_.refs_7_ = bf16[176,2048]{1,0:T(8,128)(2,1)S(1)} collective-permute-done((bf16[176,2048]{1,0:T(8,128)(2,1)S(1)}, bf16[176,2048]{1,0:T(8,128)(2,1)S(1)}, u32[]{:S(2)}, u32[]{:S(2)}) %collective-permute-start.18) | collective-permute-done | bytes 720928 | tf_op jit(solution)/shard_map/ppermute | solution.py:413
  72.6 3.6 %collective-permute-start.17 = (bf16[80,2048]{1,0:T(8,128)(2,1)S(1)}, bf16[80,2048]{1,0:T(8,128)(2,1)S(1)}, u32[]{:S(2)}, u32[]{:S(2)}) collective-permute-start(bf16[80,2048]{1,0:T(8,128)(2,1)S(1)} %get-tuple-element.120), channel_id=1, source_target_pairs={{0,12},{4,8},{8,4},{12,0},{16,28},{20,24},{24,20},{28,16},{1,13},{... | collective-permute-start | bytes 983048 | tf_op jit(solution)/shard_map/ppermute | solution.py:609
  76.3 10.8 %collective-permute-done.19.refs_14_.refs_11_ = bf16[176,2048]{1,0:T(8,128)(2,1)S(1)} collective-permute-done((bf16[176,2048]{1,0:T(8,128)(2,1)S(1)}, bf16[176,2048]{1,0:T(8,128)(2,1)S(1)}, u32[]{:S(2)}, u32[]{:S(2)}) %collective-permute-start.19) | collective-permute-done | bytes 720928 | tf_op jit(solution)/shard_map/ppermute | solution.py:413
  87.8 9.5 %collective-permute-done.17.refs_3_ = bf16[80,2048]{1,0:T(8,128)(2,1)S(1)} collective-permute-done((bf16[80,2048]{1,0:T(8,128)(2,1)S(1)}, bf16[80,2048]{1,0:T(8,128)(2,1)S(1)}, u32[]{:S(2)}, u32[]{:S(2)}) %collective-permute-start.17) | collective-permute-done | bytes 327712 | tf_op jit(solution)/shard_map/ppermute | solution.py:609
  98.8 2.5 %shard_map.203 = bf16[320,2048]{1,0:T(8,128)(2,1)} custom-call(bf16[320,128]{1,0:T(8,128)(2,1)} %copy-done.10, bf16[128,2048]{1,0:T(8,128)(2,1)} %copy-done.36), custom_call_target="tpu_custom_call" | custom-call | tf_op jit(solution)/shard_map/pallas_call | solution.py:640
  101.2 3.9 %all-to-all-start = ((bf16[4,80,2048]{2,1,0:T(8,128)(2,1)}), bf16[4,80,2048]{2,1,0:T(8,128)(2,1)S(1)}, u32[]{:S(2)}, u32[]{:S(2)}) async-start(bf16[4,80,2048]{2,1,0:T(8,128)(2,1)} %bitcast.38), calls=%async_computation | async-start | bytes 2621440 | tf_op jit(solution)/shard_map/all_to_all | solution.py:601
  113.7 8.1 %shard_map.204 = bf16[320,2048]{1,0:T(8,128)(2,1)} custom-call(s32[2]{0:T(128)} %copy-done.12, bf16[80,2048]{1,0:T(8,128)(2,1)} %copy-done.2, bf16[80,2048]{1,0:T(8,128)(2,1)} %copy-done.37, bf16[80,2048]{1,0:T(8,128)(2,1)} %copy-done.38, bf16[80,2048]{1,0:T(8,128)(2,1)} %copy-done.39, bf16[176,2048]{1,0:T(8,128)(2,1)} %bitcast.41, ...), custom_call_target="tpu_custom_call" | custom-call | flops 2768240640 | bytes 11272192 | tf_op jit(solution)/shard_map/pallas_call | solution.py:303
  123.8 8.1 %shard_map.205 = (bf16[80,2048]{1,0:T(8,128)(2,1)}, bf16[80,2048]{1,0:T(8,128)(2,1)}, bf16[80,2048]{1,0:T(8,128)(2,1)}, bf16[80,2048]{1,0:T(8,128)(2,1)}) custom-call(s32[2]{0:T(128)} %copy-done.12, bf16[320,2048]{1,0:T(8,128)(2,1)} %bitcast.39, bf16[176,2048]{1,0:T(8,128)(2,1)} %bitcast.42, bf16[176,2048]{1,0:T(8,128)(2,1)} %copy-done.27, ...), custom_call_target="tpu_custom_call" | custom-call | flops 2768240640 | bytes 11272192 | tf_op jit(solution)/shard_map/pallas_call | solution.py:303
  138.3 10.0 %shard_map.206 = (bf16[256,2048]{1,0:T(8,128)(2,1)}, bf16[256,2048]{1,0:T(8,128)(2,1)}) custom-call(s32[2]{0:T(128)} %copy-done.12, bf16[128,2048]{1,0:T(8,128)(2,1)} %copy-done.19, bf16[128,2048]{1,0:T(8,128)(2,1)} %collective-permute-done.26.refs_1_, bf16[128,2048]{1,0:T(8,128)(2,1)} %copy-done.42, bf16[128,2048]{1,0:T(8,128)(2,1)} %copy-done.43, ...), custom_call_target="tpu_custom_call" | custom-call | flops 4429185024 | bytes 12845056 | tf_op jit(solution)/shard_map/pallas_call | solution.py:303
  148.3 3.6 %collective-permute-done.29.refs_3_ = bf16[80,2048]{1,0:T(8,128)(2,1)S(1)} collective-permute-done((bf16[80,2048]{1,0:T(8,128)(2,1)}, bf16[80,2048]{1,0:T(8,128)(2,1)S(1)}, u32[]{:S(2)}, u32[]{:S(2)}) %collective-permute-start.29) | collective-permute-done | bytes 327712 | tf_op jit(solution)/shard_map/ppermute | solution.py:609
  152.7 4.4 %all-to-all-start.1 = ((bf16[4,80,2048]{2,1,0:T(8,128)(2,1)}), bf16[4,80,2048]{2,1,0:T(8,128)(2,1)}, u32[]{:S(2)}, u32[]{:S(2)}) async-start(bf16[4,80,2048]{2,1,0:T(8,128)(2,1)} %bitcast.23), calls=%async_computation.1 | async-start | bytes 2621440 | tf_op jit(solution)/shard_map/all_to_all | solution.py:601
  162.6 21.8 %collective-permute-done.35.refs_4_ = bf16[128,2048]{1,0:T(8,128)(2,1)S(1)} collective-permute-done((bf16[128,2048]{1,0:T(8,128)(2,1)S(1)}, bf16[128,2048]{1,0:T(8,128)(2,1)S(1)}, u32[]{:S(2)}, u32[]{:S(2)}) %collective-permute-start.35) | collective-permute-done | bytes 524320 | tf_op jit(solution)/shard_map/ppermute | solution.py:529
  185.4 4.9 %shard_map.208 = bf16[128,2048]{1,0:T(8,128)(2,1)} custom-call(bf16[128,320]{1,0:T(8,128)(2,1)} %copy-done.8, bf16[128,320]{1,0:T(8,128)(2,1)} %copy-done.9, f32[128,2176]{1,0:T(8,128)} %copy-done, bf16[256,2048]{1,0:T(8,128)(2,1)} %get-tuple-element.158.refs_1_, bf16[256,2048]{1,0:T(8,128)(2,1)} %collective-permute-done.33.refs_2_, ...), custom_call_target="tpu_custom_call" | custom-call | flops 335544320 | bytes 8388608 | tf_op jit(solution)/shard_map/pallas_call | solution.py:681
  (164 shorter events, 51.1 us)
Async XLA Ops:
  0.6 22.7 %collective-permute-start.3 = (bf16[176,2048]{1,0:T(8,128)(2,1)}, bf16[176,2048]{1,0:T(8,128)(2,1)S(1)}, u32[]{:S(2)}, u32[]{:S(2)}) collective-permute-start(bf16[176,2048]{1,0:T(8,128)(2,1)} %bitcast.40), channel_id=1, source_target_pairs={{0,2},{1,3},{2,0},{3,1},{4,6},{5,7},{6,4},{7,5},{8,10},{9,11},{10,... | collective-permute-start | bytes 2162696 | tf_op jit(solution)/shard_map/ppermute | solution.py:413
  6.8 13.5 %collective-permute-start.2 = (bf16[32,2432]{1,0:T(8,128)(2,1)S(1)}, bf16[32,2432]{1,0:T(8,128)(2,1)S(1)}, u32[]{:S(2)}, u32[]{:S(2)}) collective-permute-start(bf16[32,2432]{1,0:T(8,128)(2,1)S(1)} %get-tuple-element.90.ring_0), channel_id=1, source_target_pairs={{0,24},{4,28},{8,0},{12,4},{16,8},{20,12},{24,16},{28,20},{1,25},{... | collective-permute-start | bytes 466952 | tf_op jit(solution)/shard_map/ppermute | solution.py:476
  10.4 12.9 %collective-permute-start.1 = (bf16[32,2432]{1,0:T(8,128)(2,1)S(1)}, bf16[32,2432]{1,0:T(8,128)(2,1)S(1)}, u32[]{:S(2)}, u32[]{:S(2)}) collective-permute-start(bf16[32,2432]{1,0:T(8,128)(2,1)S(1)} %get-tuple-element.90.ring_0), channel_id=1, source_target_pairs={{0,16},{4,20},{8,24},{12,28},{16,0},{20,4},{24,8},{28,12},{1,17},{... | collective-permute-start | bytes 466952 | tf_op jit(solution)/shard_map/ppermute | solution.py:476
  10.4 12.9 %collective-permute-start = (bf16[32,2432]{1,0:T(8,128)(2,1)S(1)}, bf16[32,2432]{1,0:T(8,128)(2,1)S(1)}, u32[]{:S(2)}, u32[]{:S(2)}) collective-permute-start(bf16[32,2432]{1,0:T(8,128)(2,1)S(1)} %get-tuple-element.90.ring_0), channel_id=1, source_target_pairs={{0,8},{4,12},{8,16},{12,20},{16,24},{20,28},{24,0},{28,4},{1,9},{5... | collective-permute-start | bytes 466952 | tf_op jit(solution)/shard_map/ppermute | solution.py:476
  16.8 21.4 %collective-permute-start.8 = (bf16[128,2048]{1,0:T(8,128)(2,1)S(1)}, bf16[128,2048]{1,0:T(8,128)(2,1)S(1)}, u32[]{:S(2)}, u32[]{:S(2)}) collective-permute-start(bf16[128,2048]{1,0:T(8,128)(2,1)S(1)} %get-tuple-element.157.refs_0_), channel_id=1, source_target_pairs={{0,4},{4,8},{8,12},{12,16},{16,20},{20,24},{24,28},{1,5},{5,9},{9,... | collective-permute-start | bytes 1572872 | tf_op jit(solution)/shard_map/ppermute | solution.py:418
  23.5 17.2 %collective-permute-start.9 = (bf16[128,2048]{1,0:T(8,128)(2,1)S(1)}, bf16[128,2048]{1,0:T(8,128)(2,1)S(1)}, u32[]{:S(2)}, u32[]{:S(2)}) collective-permute-start(bf16[128,2048]{1,0:T(8,128)(2,1)S(1)} %get-tuple-element.157.refs_0_), channel_id=1, source_target_pairs={{0,8},{4,12},{8,16},{12,20},{16,24},{20,28},{1,9},{5,13},{9,17},{1... | collective-permute-start | bytes 1572872 | tf_op jit(solution)/shard_map/ppermute | solution.py:418
  37.4 17.8 %collective-permute-start.10 = (bf16[128,2048]{1,0:T(8,128)(2,1)S(1)}, bf16[128,2048]{1,0:T(8,128)(2,1)S(1)}, u32[]{:S(2)}, u32[]{:S(2)}) collective-permute-start(bf16[128,2048]{1,0:T(8,128)(2,1)S(1)} %get-tuple-element.104.refs_0_), channel_id=1, source_target_pairs={{0,1},{1,0},{2,3},{3,2},{4,5},{5,4},{6,7},{7,6},{8,9},{9,8},{10,11... | collective-permute-start | bytes 1572872 | tf_op jit(solution)/shard_map/ppermute | solution.py:413
  37.4 14.3 %collective-permute-start.6 = (bf16[128,2048]{1,0:T(8,128)(2,1)S(1)}, bf16[128,2048]{1,0:T(8,128)(2,1)S(1)}, u32[]{:S(2)}, u32[]{:S(2)}) collective-permute-start(bf16[128,2048]{1,0:T(8,128)(2,1)S(1)} %get-tuple-element.104.refs_0_), channel_id=1, source_target_pairs={{0,2},{1,3},{2,0},{3,1},{4,6},{5,7},{6,4},{7,5},{8,10},{9,11},{10,... | collective-permute-start | bytes 1572872 | tf_op jit(solution)/shard_map/ppermute | solution.py:413
  38.0 17.6 %collective-permute-start.11 = (bf16[128,2048]{1,0:T(8,128)(2,1)S(1)}, bf16[128,2048]{1,0:T(8,128)(2,1)S(1)}, u32[]{:S(2)}, u32[]{:S(2)}) collective-permute-start(bf16[128,2048]{1,0:T(8,128)(2,1)S(1)} %get-tuple-element.105.refs_1_), channel_id=1, source_target_pairs={{0,1},{1,0},{2,3},{3,2},{4,5},{5,4},{6,7},{7,6},{8,9},{9,8},{10,11... | collective-permute-start | bytes 1572872 | tf_op jit(solution)/shard_map/ppermute | solution.py:413
  38.2 14.9 %collective-permute-start.7 = (bf16[128,2048]{1,0:T(8,128)(2,1)S(1)}, bf16[128,2048]{1,0:T(8,128)(2,1)S(1)}, u32[]{:S(2)}, u32[]{:S(2)}) collective-permute-start(bf16[128,2048]{1,0:T(8,128)(2,1)S(1)} %get-tuple-element.105.refs_1_), channel_id=1, source_target_pairs={{0,4},{4,0},{8,12},{12,8},{16,20},{20,16},{24,28},{28,24},{1,5},{5... | collective-permute-start | bytes 1572872 | tf_op jit(solution)/shard_map/ppermute | solution.py:452
  53.6 19.0 %collective-permute-start.18 = (bf16[176,2048]{1,0:T(8,128)(2,1)S(1)}, bf16[176,2048]{1,0:T(8,128)(2,1)S(1)}, u32[]{:S(2)}, u32[]{:S(2)}) collective-permute-start(bf16[176,2048]{1,0:T(8,128)(2,1)S(1)} %bitcast.47), channel_id=1, source_target_pairs={{0,2},{1,3},{2,0},{3,1},{4,6},{5,7},{6,4},{7,5},{8,10},{9,11},{10,... | collective-permute-start | bytes 2162696 | tf_op jit(solution)/shard_map/ppermute | solution.py:413
  55.1 32.0 %collective-permute-start.19 = (bf16[176,2048]{1,0:T(8,128)(2,1)S(1)}, bf16[176,2048]{1,0:T(8,128)(2,1)S(1)}, u32[]{:S(2)}, u32[]{:S(2)}) collective-permute-start(bf16[176,2048]{1,0:T(8,128)(2,1)S(1)} %bitcast.51), channel_id=1, source_target_pairs={{0,2},{1,3},{2,0},{3,1},{4,6},{5,7},{6,4},{7,5},{8,10},{9,11},{10,... | collective-permute-start | bytes 2162696 | tf_op jit(solution)/shard_map/ppermute | solution.py:413
  61.1 36.1 %collective-permute-start.14 = (bf16[128,2048]{1,0:T(8,128)(2,1)S(1)}, bf16[128,2048]{1,0:T(8,128)(2,1)S(1)}, u32[]{:S(2)}, u32[]{:S(2)}) collective-permute-start(bf16[128,2048]{1,0:T(8,128)(2,1)S(1)} %get-tuple-element.153.refs_0_), channel_id=1, source_target_pairs={{0,16},{4,20},{8,24},{12,28},{16,0},{20,4},{24,8},{28,12},{1,17},{... | collective-permute-start | bytes 1572872 | tf_op jit(solution)/shard_map/ppermute | solution.py:529
  68.4 18.7 %collective-permute-start.15 = (bf16[80,2048]{1,0:T(8,128)(2,1)S(1)}, bf16[80,2048]{1,0:T(8,128)(2,1)S(1)}, u32[]{:S(2)}, u32[]{:S(2)}) collective-permute-start(bf16[80,2048]{1,0:T(8,128)(2,1)S(1)} %get-tuple-element.118), channel_id=1, source_target_pairs={{0,4},{4,0},{8,12},{12,8},{16,20},{20,16},{24,28},{28,24},{1,5},{5... | collective-permute-start | bytes 983048 | tf_op jit(solution)/shard_map/ppermute | solution.py:609
  68.7 19.1 %collective-permute-start.16 = (bf16[80,2048]{1,0:T(8,128)(2,1)S(1)}, bf16[80,2048]{1,0:T(8,128)(2,1)S(1)}, u32[]{:S(2)}, u32[]{:S(2)}) collective-permute-start(bf16[80,2048]{1,0:T(8,128)(2,1)S(1)} %get-tuple-element.119), channel_id=1, source_target_pairs={{0,8},{4,12},{8,0},{12,4},{16,24},{20,28},{24,16},{28,20},{1,9},{5... | collective-permute-start | bytes 983048 | tf_op jit(solution)/shard_map/ppermute | solution.py:609
  72.6 24.6 %collective-permute-start.17 = (bf16[80,2048]{1,0:T(8,128)(2,1)S(1)}, bf16[80,2048]{1,0:T(8,128)(2,1)S(1)}, u32[]{:S(2)}, u32[]{:S(2)}) collective-permute-start(bf16[80,2048]{1,0:T(8,128)(2,1)S(1)} %get-tuple-element.120), channel_id=1, source_target_pairs={{0,12},{4,8},{8,4},{12,0},{16,28},{20,24},{24,20},{28,16},{1,13},{... | collective-permute-start | bytes 983048 | tf_op jit(solution)/shard_map/ppermute | solution.py:609
  101.2 21.5 %all-to-all-start = ((bf16[4,80,2048]{2,1,0:T(8,128)(2,1)}), bf16[4,80,2048]{2,1,0:T(8,128)(2,1)S(1)}, u32[]{:S(2)}, u32[]{:S(2)}) async-start(bf16[4,80,2048]{2,1,0:T(8,128)(2,1)} %bitcast.38), calls=%async_computation | async-start | bytes 2621440 | tf_op jit(solution)/shard_map/all_to_all | solution.py:601
  108.6 14.1 %collective-permute-start.26 = (bf16[128,2048]{1,0:T(8,128)(2,1)S(1)}, bf16[128,2048]{1,0:T(8,128)(2,1)}, u32[]{:S(2)}, u32[]{:S(2)}) collective-permute-start(bf16[128,2048]{1,0:T(8,128)(2,1)S(1)} %get-tuple-element.153.refs_0_), channel_id=1, source_target_pairs={{0,2},{1,3},{2,0},{3,1},{4,6},{5,7},{6,4},{7,5},{8,10},{9,11},{10,... | collective-permute-start | bytes 1572872 | tf_op jit(solution)/shard_map/ppermute | solution.py:413
  132.5 19.4 %collective-permute-start.32 = (bf16[128,2048]{1,0:T(8,128)(2,1)S(1)}, bf16[128,2048]{1,0:T(8,128)(2,1)S(1)}, u32[]{:S(2)}, u32[]{:S(2)}) collective-permute-start(bf16[128,2048]{1,0:T(8,128)(2,1)S(1)} %get-tuple-element.157.refs_0_), channel_id=1, source_target_pairs={{0,2},{1,3},{2,0},{3,1},{4,6},{5,7},{6,4},{7,5},{8,10},{9,11},{10,... | collective-permute-start | bytes 1572872 | tf_op jit(solution)/shard_map/ppermute | solution.py:413
  134.0 14.3 %collective-permute-start.27 = (bf16[80,2048]{1,0:T(8,128)(2,1)}, bf16[80,2048]{1,0:T(8,128)(2,1)S(1)}, u32[]{:S(2)}, u32[]{:S(2)}) collective-permute-start(bf16[80,2048]{1,0:T(8,128)(2,1)} %get-tuple-element.148), channel_id=1, source_target_pairs={{0,4},{4,0},{8,12},{12,8},{16,20},{20,16},{24,28},{28,24},{1,5},{5... | collective-permute-start | bytes 983048 | tf_op jit(solution)/shard_map/ppermute | solution.py:609
  137.3 14.6 %collective-permute-start.29 = (bf16[80,2048]{1,0:T(8,128)(2,1)}, bf16[80,2048]{1,0:T(8,128)(2,1)S(1)}, u32[]{:S(2)}, u32[]{:S(2)}) collective-permute-start(bf16[80,2048]{1,0:T(8,128)(2,1)} %get-tuple-element.150), channel_id=1, source_target_pairs={{0,12},{4,8},{8,4},{12,0},{16,28},{20,24},{24,20},{28,16},{1,13},{... | collective-permute-start | bytes 983048 | tf_op jit(solution)/shard_map/ppermute | solution.py:609
  152.7 32.4 %all-to-all-start.1 = ((bf16[4,80,2048]{2,1,0:T(8,128)(2,1)}), bf16[4,80,2048]{2,1,0:T(8,128)(2,1)}, u32[]{:S(2)}, u32[]{:S(2)}) async-start(bf16[4,80,2048]{2,1,0:T(8,128)(2,1)} %bitcast.23), calls=%async_computation.1 | async-start | bytes 2621440 | tf_op jit(solution)/shard_map/all_to_all | solution.py:601
  158.5 25.9 %collective-permute-start.35 = (bf16[128,2048]{1,0:T(8,128)(2,1)S(1)}, bf16[128,2048]{1,0:T(8,128)(2,1)S(1)}, u32[]{:S(2)}, u32[]{:S(2)}) collective-permute-start(bf16[128,2048]{1,0:T(8,128)(2,1)S(1)} %shard_map.207), channel_id=1, source_target_pairs={{0,16},{4,20},{8,24},{12,28},{16,0},{20,4},{24,8},{28,12},{1,17},{... | collective-permute-start | bytes 1572872 | tf_op jit(solution)/shard_map/ppermute | solution.py:529
  159.9 24.5 %collective-permute-start.34 = (bf16[128,2048]{1,0:T(8,128)(2,1)S(1)}, bf16[128,2048]{1,0:T(8,128)(2,1)S(1)}, u32[]{:S(2)}, u32[]{:S(2)}) collective-permute-start(bf16[128,2048]{1,0:T(8,128)(2,1)S(1)} %add_convert_fusion), channel_id=1, source_target_pairs={{0,2},{1,3},{2,0},{3,1},{4,6},{5,7},{6,4},{7,5},{8,10},{9,11},{10,... | collective-permute-start | bytes 1572872 | tf_op jit(solution)/shard_map/ppermute | solution.py:413
  (58 other events, 398.9 us)

commit v4 on v3

--- a/solution.py
+++ b/solution.py
@@ -322,23 +322,35 @@
     )(place, *x_list, *weights[0], *weights[1], *weights[2])
 
 
-def combine_kernel(count, backs, high_ref, low_ref, *refs):
+def blend_kernel(state_hbm, keep_hbm, sib_hbm, far_hbm, out_ref, state, keep, sib, far, sems):
+    loads = []
+    for number, (source, target) in enumerate(((state_hbm, state), (keep_hbm, keep), (sib_hbm, sib), (far_hbm, far))):
+        loads.append(pltpu.make_async_copy(source.at[pl.ds(0, target.shape[0])], target, sems.at[number]))
+        loads[-1].start()
+    for load in loads:
+        load.wait()
+    step = 512
+    for at in range(0, D, step):
+        cols = slice(at, at + step)
+        shared = keep[:, cols].astype(F32) + sib[:, cols].astype(F32) + far[:, cols].astype(F32)
+        out_ref[:, cols] = state[:, cols] + state[:, D : D + 1] * shared
+
+
+def combine_kernel(count, backs, high_ref, low_ref, blend_ref, *refs):
     sources, out_ref, refs = refs[:count], refs[count], refs[count + 1 :]
-    *held, back, result, sems = refs
+    *relayed, back, result, sems = refs
     rows = result.shape[0]
-    targets = list(held)
+    targets = list(relayed)
     row = 0
     for source in sources[count - backs :]:
         targets.append(back.at[pl.ds(row, source.shape[0])])
         row += source.shape[0]
     loads = []
     for number, (source, target) in enumerate(zip(sources, targets)):
-        loads.append(pltpu.make_async_copy(source.at[pl.ds(0, target.shape[0])], target, sems.at[0, number]))
+        loads.append(pltpu.make_async_copy(source, target, sems.at[0, number]))
         loads[-1].start()
     for load in loads:
         load.wait()
-    state, keep, sib, far, *relayed = held
-    scale = state[:, D : D + 1]
     step = 512
     moves = []
     for at in range(0, D, step):
@@ -348,8 +360,7 @@
         )
         for ref in relayed:
             routed = routed + ref[:, cols].astype(F32)
-        shared = keep[:, cols].astype(F32) + sib[:, cols].astype(F32) + far[:, cols].astype(F32)
-        result[:, cols] = (state[:, cols] + scale * shared + routed).astype(BF16)
+        result[:, cols] = (blend_ref[:, cols] + routed).astype(BF16)
         window = (pl.ds(0, rows), pl.ds(at, step))
         moves.append(pltpu.make_async_copy(result.at[window], out_ref.at[window], sems.at[1, at // step]))
         moves[-1].start()
@@ -643,6 +654,7 @@
             in_specs=[VMEM] * 2,
             out_specs=[HBM],
             scratch_shapes=[pltpu.VMEM((slots, D), BF16), pltpu.SemaphoreType.DMA((1, 4))],
+            compiler_params=pltpu.CompilerParams(vmem_limit_bytes=8 << 20),
         )(far_pick, relay_rows)
         relay_arrived = exchange(relay_out)
         far_rows = grp_move(late_normed, 2)
@@ -656,9 +668,7 @@
         partner = grp_move(late_cache, 2)
         relay_finished, normed, far_rows = lax.optimization_barrier((relay_finished, normed, far_rows))
         keep, send = shared(normed, far_rows)
-        relay_back, finished, keep, send, partner = lax.optimization_barrier(
-            (relay_back, finished, keep, send, partner)
-        )
+        relay_back, keep, send, partner = lax.optimization_barrier((relay_back, keep, send, partner))
         relay_sum = pl.pallas_call(
             relay_kernel,
             out_shape=shape(rows, D),
@@ -676,18 +686,29 @@
         partner = grp_move(own_cache, 2)
     back = [exchange(finished[0])]
 
-    sources = [state, keep, from_sib, from_far, *relayed, *back]
-    kept = [(rows, D + HD)] + [(rows, D)] * (3 + len(relayed)) + [(slots, D)]
+    blend = pl.pallas_call(
+        blend_kernel,
+        out_shape=shape(rows, D, dtype=F32),
+        in_specs=[ANY] * 4,
+        out_specs=VMEM,
+        scratch_shapes=[pltpu.VMEM((rows, D + HD), F32)]
+        + [pltpu.VMEM((rows, D), BF16)] * 3
+        + [pltpu.SemaphoreType.DMA((4,))],
+        compiler_params=pltpu.CompilerParams(vmem_limit_bytes=56 << 20),
+        cost_estimate=pl.CostEstimate(flops=4 * rows * D, bytes_accessed=4 << 20, transcendentals=0),
+    )(state, keep, from_sib, from_far)
+    sources = [*relayed, *back]
+    kept = [(rows, D)] * len(relayed) + [(slots, D)]
     final = pl.pallas_call(
         functools.partial(combine_kernel, len(sources), len(back)),
         out_shape=shape(rows, D),
-        in_specs=[VMEM] * 2 + [ANY] * len(sources),
+        in_specs=[VMEM] * 3 + [ANY] * len(sources),
         out_specs=HBM,
-        scratch_shapes=[pltpu.VMEM(dims, source.dtype) for dims, source in zip(kept, sources)]
+        scratch_shapes=[pltpu.VMEM(dims, BF16) for dims in kept]
         + [pltpu.VMEM((rows, D), BF16), pltpu.SemaphoreType.DMA((2, 16))],
         compiler_params=pltpu.CompilerParams(vmem_limit_bytes=56 << 20),
-        cost_estimate=pl.CostEstimate(flops=4 * slots * rows * D, bytes_accessed=8 << 20, transcendentals=0),
-    )(high, low, *sources)
+        cost_estimate=pl.CostEstimate(flops=0, bytes_accessed=0, transcendentals=0),
+    )(high, low, blend, *sources)
 
     pair_row = grp // 4 * 2 + grp % 2
     flags = jnp.sum(

time: 191 us -> 187 us (0.979)
  waiting for transfers between devices: 72.8 us -> 69.7 us
    ppermute x2, waiting for transfers between devices: 21.8 us -> 7.1 us  [across(): lax.ppermute(array, 'req', [(i, i ^ requests // 2) for i in range(request...]
    ppermute x21, waiting for transfers between devices: 30.2 us -> 42.5 us  [grp_move(): lax.ppermute(array, 'grp', [(i, i ^ flip) for i in range(lax.axis_size('g...]
    pallas_call x0 -> x1, Pallas kernels: none -> 2.96 us  [local(): pl.pallas_call(blend_kernel, out_shape=shape(rows, D, dtype=F32), in_spec...]
    unnamed x88 -> x80, local copies, waits for them, and re-layouts: 14.3 us -> 13.1 us
  transfers between devices with their start and end apart: 38 -> 38, of which waited for: 19 -> 19; matrix products, arithmetic and copies ran while one was open for 2% -> 1% of each run, Pallas kernels for 17% -> 19%
where the time goes in v4:
time: 187 us; the launch traced here: 186 us
  waiting for transfers between devices  69.7 us (37%)
  starting transfers between devices  51.3 us (27%)
  Pallas kernels  48.5 us (26%)
  local copies, waits for them, and re-layouts  13.3 us (7%)
  other arithmetic  2.42 us (1%)
    ppermute x21, waiting for transfers between devices, grp_move(): lax.ppermute(array, 'grp', [(i, i ^ flip) for i in range(lax.axis_size('g...  42.5 us
    pallas_call x3, Pallas kernels, ffn(): pl.pallas_call(functools.partial(ffn_kernel, len(x_list), len(weights[0])...  26.3 us
    unnamed x80, local copies, waits for them, and re-layouts  13.1 us
    ppermute x6, waiting for transfers between devices, trade(): lax.ppermute(array, 'req', [(i, i ^ flip) for i in range(requests)])  12.9 us
    ppermute x21, starting transfers between devices, grp_move(): lax.ppermute(array, 'grp', [(i, i ^ flip) for i in range(lax.axis_size('g...  12.4 us
    all_to_all x2, starting transfers between devices, exchange(): lax.all_to_all(split, 'req', split_axis=0, concat_axis=0, axis_index_grou...  8.31 us
    ppermute x6, starting transfers between devices, trade(): lax.ppermute(array, 'req', [(i, i ^ flip) for i in range(requests)])  7.42 us
    ppermute x2, starting transfers between devices, across(): lax.ppermute(array, 'req', [(i, i ^ requests // 2) for i in range(request...  7.34 us
  transfers between devices with their start and end apart: 38, of which 19 were waited for; matrix products, arithmetic and copies ran while one was open for 1% of the time, Pallas kernels for 19%

profile of v4, /device:TPU:0, one launch (start us, length us, event | category | flops | bytes accessed | tf_op | source)
XLA Modules:
  0.0 186.5 jit_solution(10129303990267586748)
XLA Ops:
  0.6 3.0 %collective-permute-start.3 = (bf16[176,2048]{1,0:T(8,128)(2,1)}, bf16[176,2048]{1,0:T(8,128)(2,1)S(1)}, u32[]{:S(2)}, u32[]{:S(2)}) collective-permute-start(bf16[176,2048]{1,0:T(8,128)(2,1)} %bitcast.39), channel_id=1, source_target_pairs={{0,2},{1,3},{2,0},{3,1},{4,6},{5,7},{6,4},{7,5},{8,10},{9,11},{10,... | collective-permute-start | bytes 2162696 | tf_op jit(solution)/shard_map/ppermute | solution.py:424
  6.8 3.6 %collective-permute-start.2 = (bf16[32,2432]{1,0:T(8,128)(2,1)S(1)}, bf16[32,2432]{1,0:T(8,128)(2,1)S(1)}, u32[]{:S(2)}, u32[]{:S(2)}) collective-permute-start(bf16[32,2432]{1,0:T(8,128)(2,1)S(1)} %get-tuple-element.89.ring_0), channel_id=1, source_target_pairs={{0,24},{4,28},{8,0},{12,4},{16,8},{20,12},{24,16},{28,20},{1,25},{... | collective-permute-start | bytes 466952 | tf_op jit(solution)/shard_map/ppermute | solution.py:487
  16.8 3.5 %collective-permute-start.8 = (bf16[128,2048]{1,0:T(8,128)(2,1)S(1)}, bf16[128,2048]{1,0:T(8,128)(2,1)S(1)}, u32[]{:S(2)}, u32[]{:S(2)}) collective-permute-start(bf16[128,2048]{1,0:T(8,128)(2,1)S(1)} %get-tuple-element.155.refs_0_), channel_id=1, source_target_pairs={{0,4},{4,8},{8,12},{12,16},{16,20},{20,24},{24,28},{1,5},{5,9},{9,... | collective-permute-start | bytes 1572872 | tf_op jit(solution)/shard_map/ppermute | solution.py:429
  20.3 3.0 %collective-permute-done.1.ring_2 = bf16[32,2432]{1,0:T(8,128)(2,1)S(1)} collective-permute-done((bf16[32,2432]{1,0:T(8,128)(2,1)S(1)}, bf16[32,2432]{1,0:T(8,128)(2,1)S(1)}, u32[]{:S(2)}, u32[]{:S(2)}) %collective-permute-start.1) | collective-permute-done | bytes 155680 | tf_op jit(solution)/shard_map/ppermute | solution.py:487
  23.5 2.8 %collective-permute-start.9 = (bf16[128,2048]{1,0:T(8,128)(2,1)S(1)}, bf16[128,2048]{1,0:T(8,128)(2,1)S(1)}, u32[]{:S(2)}, u32[]{:S(2)}) collective-permute-start(bf16[128,2048]{1,0:T(8,128)(2,1)S(1)} %get-tuple-element.155.refs_0_), channel_id=1, source_target_pairs={{0,8},{4,12},{8,16},{12,20},{16,24},{20,28},{1,9},{5,13},{9,17},{1... | collective-permute-start | bytes 1572872 | tf_op jit(solution)/shard_map/ppermute | solution.py:429
  38.2 2.5 %collective-permute-start.7 = (bf16[128,2048]{1,0:T(8,128)(2,1)S(1)}, bf16[128,2048]{1,0:T(8,128)(2,1)S(1)}, u32[]{:S(2)}, u32[]{:S(2)}) collective-permute-start(bf16[128,2048]{1,0:T(8,128)(2,1)S(1)} %get-tuple-element.104.refs_1_), channel_id=1, source_target_pairs={{0,4},{4,0},{8,12},{12,8},{16,20},{20,16},{24,28},{28,24},{1,5},{5... | collective-permute-start | bytes 1572872 | tf_op jit(solution)/shard_map/ppermute | solution.py:463
  40.8 3.4 %shard_map.201.attn_ref = bf16[128,1024]{1,0:T(8,128)(2,1)S(1)} custom-call(s32[1,16]{1,0:T(1,128)S(1)} %copy-done.15, s32[2]{0:T(128)S(1)} %pad_add_fusion.place_ref, bf16[128,1024]{1,0:T(8,128)(2,1)S(1)} %get-tuple-element.105.q_ref, bf16[32,2048]{1,0:T(8,128)(2,1)S(1)} %get-tuple-element.106.prefix_ref, bf16[128,2048]{1,0:T(8,128)(2,1)S(1)} %get-tuple-element.155.refs_0_, ...), custom_call_target="tpu_custom_call" | custom-call | flops 20000000000 | bytes 4194304 | tf_op jit(solution)/shard_map/pallas_call | solution.py:543
  44.2 7.6 %collective-permute-done.6.refs_2_ = bf16[128,2048]{1,0:T(8,128)(2,1)S(1)} collective-permute-done((bf16[128,2048]{1,0:T(8,128)(2,1)S(1)}, bf16[128,2048]{1,0:T(8,128)(2,1)S(1)}, u32[]{:S(2)}, u32[]{:S(2)}) %collective-permute-start.6) | collective-permute-done | bytes 524320 | tf_op jit(solution)/shard_map/ppermute | solution.py:424
  55.8 3.6 %shard_map.202 = (bf16[128,2048]{1,0:T(8,128)(2,1)S(1)}, f32[128,2176]{1,0:T(8,128)S(1)}, bf16[80,2048]{1,0:T(8,128)(2,1)S(1)}, bf16[80,2048]{1,0:T(8,128)(2,1)S...) custom-call(bf16[128,1024]{1,0:T(8,128)(2,1)S(1)} %shard_map.201.attn_ref, ...), custom_call_target="tpu_custom_call" | custom-call | flops 536870912 | bytes 8388608 | tf_op jit(solution)/shard_map/pallas_call | solution.py:593
  60.4 7.3 %collective-permute-start.14 = (bf16[128,2048]{1,0:T(8,128)(2,1)S(1)}, bf16[128,2048]{1,0:T(8,128)(2,1)S(1)}, u32[]{:S(2)}, u32[]{:S(2)}) collective-permute-start(bf16[128,2048]{1,0:T(8,128)(2,1)S(1)} %get-tuple-element.151.refs_0_), channel_id=1, source_target_pairs={{0,16},{4,20},{8,24},{12,28},{16,0},{20,4},{24,8},{28,12},{1,17},{... | collective-permute-start | bytes 1572872 | tf_op jit(solution)/shard_map/ppermute | solution.py:540
  67.9 4.7 %collective-permute-done.18.refs_10_.refs_7_ = bf16[176,2048]{1,0:T(8,128)(2,1)S(1)} collective-permute-done((bf16[176,2048]{1,0:T(8,128)(2,1)S(1)}, bf16[176,2048]{1,0:T(8,128)(2,1)S(1)}, u32[]{:S(2)}, u32[]{:S(2)}) %collective-permute-start.18) | collective-permute-done | bytes 720928 | tf_op jit(solution)/shard_map/ppermute | solution.py:424
  72.7 3.6 %collective-permute-start.17 = (bf16[80,2048]{1,0:T(8,128)(2,1)S(1)}, bf16[80,2048]{1,0:T(8,128)(2,1)S(1)}, u32[]{:S(2)}, u32[]{:S(2)}) collective-permute-start(bf16[80,2048]{1,0:T(8,128)(2,1)S(1)} %get-tuple-element.119), channel_id=1, source_target_pairs={{0,12},{4,8},{8,4},{12,0},{16,28},{20,24},{24,20},{28,16},{1,13},{... | collective-permute-start | bytes 983048 | tf_op jit(solution)/shard_map/ppermute | solution.py:620
  76.3 10.8 %collective-permute-done.19.refs_14_.refs_11_ = bf16[176,2048]{1,0:T(8,128)(2,1)S(1)} collective-permute-done((bf16[176,2048]{1,0:T(8,128)(2,1)S(1)}, bf16[176,2048]{1,0:T(8,128)(2,1)S(1)}, u32[]{:S(2)}, u32[]{:S(2)}) %collective-permute-start.19) | collective-permute-done | bytes 720928 | tf_op jit(solution)/shard_map/ppermute | solution.py:424
  87.2 9.3 %collective-permute-done.17.refs_3_ = bf16[80,2048]{1,0:T(8,128)(2,1)S(1)} collective-permute-done((bf16[80,2048]{1,0:T(8,128)(2,1)S(1)}, bf16[80,2048]{1,0:T(8,128)(2,1)S(1)}, u32[]{:S(2)}, u32[]{:S(2)}) %collective-permute-start.17) | collective-permute-done | bytes 327712 | tf_op jit(solution)/shard_map/ppermute | solution.py:620
  97.9 3.9 %all-to-all-start = ((bf16[4,80,2048]{2,1,0:T(8,128)(2,1)}), bf16[4,80,2048]{2,1,0:T(8,128)(2,1)S(1)}, u32[]{:S(2)}, u32[]{:S(2)}) async-start(bf16[4,80,2048]{2,1,0:T(8,128)(2,1)} %bitcast.17), calls=%async_computation | async-start | bytes 2621440 | tf_op jit(solution)/shard_map/all_to_all | solution.py:612
  110.3 8.2 %shard_map.204 = bf16[320,2048]{1,0:T(8,128)(2,1)} custom-call(s32[2]{0:T(128)} %copy-done.11, bf16[80,2048]{1,0:T(8,128)(2,1)} %copy-done.2, bf16[80,2048]{1,0:T(8,128)(2,1)} %copy-done.33, bf16[80,2048]{1,0:T(8,128)(2,1)} %copy-done.34, bf16[80,2048]{1,0:T(8,128)(2,1)} %copy-done.35, bf16[176,2048]{1,0:T(8,128)(2,1)} %bitcast.40, ...), custom_call_target="tpu_custom_call" | custom-call | flops 2768240640 | bytes 11272192 | tf_op jit(solution)/shard_map/pallas_call | solution.py:303
  120.5 8.1 %shard_map.205 = (bf16[80,2048]{1,0:T(8,128)(2,1)}, bf16[80,2048]{1,0:T(8,128)(2,1)}, bf16[80,2048]{1,0:T(8,128)(2,1)}, bf16[80,2048]{1,0:T(8,128)(2,1)}) custom-call(s32[2]{0:T(128)} %copy-done.11, bf16[320,2048]{1,0:T(8,128)(2,1)} %bitcast.38, bf16[176,2048]{1,0:T(8,128)(2,1)} %bitcast.41, bf16[176,2048]{1,0:T(8,128)(2,1)} %copy-done.25, ...), custom_call_target="tpu_custom_call" | custom-call | flops 2768240640 | bytes 11272192 | tf_op jit(solution)/shard_map/pallas_call | solution.py:303
  135.0 10.0 %shard_map.206 = (bf16[256,2048]{1,0:T(8,128)(2,1)}, bf16[256,2048]{1,0:T(8,128)(2,1)}) custom-call(s32[2]{0:T(128)} %copy-done.11, bf16[128,2048]{1,0:T(8,128)(2,1)} %copy-done.17, bf16[128,2048]{1,0:T(8,128)(2,1)} %collective-permute-done.26.refs_1_, bf16[128,2048]{1,0:T(8,128)(2,1)} %copy-done.38, bf16[128,2048]{1,0:T(8,128)(2,1)} %copy-done.39, ...), custom_call_target="tpu_custom_call" | custom-call | flops 4429185024 | bytes 12845056 | tf_op jit(solution)/shard_map/pallas_call | solution.py:303
  145.0 3.6 %collective-permute-done.29.refs_3_ = bf16[80,2048]{1,0:T(8,128)(2,1)S(1)} collective-permute-done((bf16[80,2048]{1,0:T(8,128)(2,1)}, bf16[80,2048]{1,0:T(8,128)(2,1)S(1)}, u32[]{:S(2)}, u32[]{:S(2)}) %collective-permute-start.29) | collective-permute-done | bytes 327712 | tf_op jit(solution)/shard_map/ppermute | solution.py:620
  148.6 4.4 %all-to-all-start.1 = ((bf16[4,80,2048]{2,1,0:T(8,128)(2,1)}), bf16[4,80,2048]{2,1,0:T(8,128)(2,1)}, u32[]{:S(2)}, u32[]{:S(2)}) async-start(bf16[4,80,2048]{2,1,0:T(8,128)(2,1)} %bitcast.23), calls=%async_computation.1 | async-start | bytes 2621440 | tf_op jit(solution)/shard_map/all_to_all | solution.py:612
  157.5 12.7 %collective-permute-done.34.far_hbm = bf16[128,2048]{1,0:T(8,128)(2,1)S(1)} collective-permute-done((bf16[128,2048]{1,0:T(8,128)(2,1)S(1)}, bf16[128,2048]{1,0:T(8,128)(2,1)S(1)}, u32[]{:S(2)}, u32[]{:S(2)}) %collective-permute-start.34) | collective-permute-done | bytes 524320 | tf_op jit(solution)/shard_map/ppermute | solution.py:424
  171.0 3.0 %shard_map.207.blend_ref = f32[128,2048]{1,0:T(8,128)} custom-call(f32[128,2176]{1,0:T(8,128)} %copy-done, bf16[256,2048]{1,0:T(8,128)(2,1)} %get-tuple-element.156.keep_hbm, bf16[256,2048]{1,0:T(8,128)(2,1)} %collective-permute-done.33.sib_hbm, bf16[128,2048]{1,0:T(8,128)(2,1)} %copy-done.32), custom_call_target="tpu_custom_call" | custom-call | flops 1048576 | bytes 4194304 | tf_op jit(solution)/shard_map/pallas_call | solution.py:689
  174.0 7.1 %collective-permute-done.35.refs_0_ = bf16[128,2048]{1,0:T(8,128)(2,1)S(1)} collective-permute-done((bf16[128,2048]{1,0:T(8,128)(2,1)S(1)}, bf16[128,2048]{1,0:T(8,128)(2,1)S(1)}, u32[]{:S(2)}, u32[]{:S(2)}) %collective-permute-start.35) | collective-permute-done | bytes 524320 | tf_op jit(solution)/shard_map/ppermute | solution.py:540
  181.8 4.5 %shard_map.209 = bf16[128,2048]{1,0:T(8,128)(2,1)} custom-call(bf16[128,320]{1,0:T(8,128)(2,1)} %copy-done.8, bf16[128,320]{1,0:T(8,128)(2,1)} %copy-done.9, f32[128,2048]{1,0:T(8,128)} %shard_map.207.blend_ref, bf16[128,2048]{1,0:T(8,128)(2,1)} %copy-done.31, bf16[320,2048]{1,0:T(8,128)(2,1)} %bitcast.24.refs_1_), custom_call_target="tpu_custom_call" | custom-call | tf_op jit(solution)/shard_map/pallas_call | solution.py:702
  (157 shorter events, 51.0 us)
Async XLA Ops:
  0.6 22.7 %collective-permute-start.3 = (bf16[176,2048]{1,0:T(8,128)(2,1)}, bf16[176,2048]{1,0:T(8,128)(2,1)S(1)}, u32[]{:S(2)}, u32[]{:S(2)}) collective-permute-start(bf16[176,2048]{1,0:T(8,128)(2,1)} %bitcast.39), channel_id=1, source_target_pairs={{0,2},{1,3},{2,0},{3,1},{4,6},{5,7},{6,4},{7,5},{8,10},{9,11},{10,... | collective-permute-start | bytes 2162696 | tf_op jit(solution)/shard_map/ppermute | solution.py:424
  6.8 13.5 %collective-permute-start.2 = (bf16[32,2432]{1,0:T(8,128)(2,1)S(1)}, bf16[32,2432]{1,0:T(8,128)(2,1)S(1)}, u32[]{:S(2)}, u32[]{:S(2)}) collective-permute-start(bf16[32,2432]{1,0:T(8,128)(2,1)S(1)} %get-tuple-element.89.ring_0), channel_id=1, source_target_pairs={{0,24},{4,28},{8,0},{12,4},{16,8},{20,12},{24,16},{28,20},{1,25},{... | collective-permute-start | bytes 466952 | tf_op jit(solution)/shard_map/ppermute | solution.py:487
  10.4 12.9 %collective-permute-start.1 = (bf16[32,2432]{1,0:T(8,128)(2,1)S(1)}, bf16[32,2432]{1,0:T(8,128)(2,1)S(1)}, u32[]{:S(2)}, u32[]{:S(2)}) collective-permute-start(bf16[32,2432]{1,0:T(8,128)(2,1)S(1)} %get-tuple-element.89.ring_0), channel_id=1, source_target_pairs={{0,16},{4,20},{8,24},{12,28},{16,0},{20,4},{24,8},{28,12},{1,17},{... | collective-permute-start | bytes 466952 | tf_op jit(solution)/shard_map/ppermute | solution.py:487
  10.4 12.9 %collective-permute-start = (bf16[32,2432]{1,0:T(8,128)(2,1)S(1)}, bf16[32,2432]{1,0:T(8,128)(2,1)S(1)}, u32[]{:S(2)}, u32[]{:S(2)}) collective-permute-start(bf16[32,2432]{1,0:T(8,128)(2,1)S(1)} %get-tuple-element.89.ring_0), channel_id=1, source_target_pairs={{0,8},{4,12},{8,16},{12,20},{16,24},{20,28},{24,0},{28,4},{1,9},{5... | collective-permute-start | bytes 466952 | tf_op jit(solution)/shard_map/ppermute | solution.py:487
  16.8 21.4 %collective-permute-start.8 = (bf16[128,2048]{1,0:T(8,128)(2,1)S(1)}, bf16[128,2048]{1,0:T(8,128)(2,1)S(1)}, u32[]{:S(2)}, u32[]{:S(2)}) collective-permute-start(bf16[128,2048]{1,0:T(8,128)(2,1)S(1)} %get-tuple-element.155.refs_0_), channel_id=1, source_target_pairs={{0,4},{4,8},{8,12},{12,16},{16,20},{20,24},{24,28},{1,5},{5,9},{9,... | collective-permute-start | bytes 1572872 | tf_op jit(solution)/shard_map/ppermute | solution.py:429
  23.5 17.2 %collective-permute-start.9 = (bf16[128,2048]{1,0:T(8,128)(2,1)S(1)}, bf16[128,2048]{1,0:T(8,128)(2,1)S(1)}, u32[]{:S(2)}, u32[]{:S(2)}) collective-permute-start(bf16[128,2048]{1,0:T(8,128)(2,1)S(1)} %get-tuple-element.155.refs_0_), channel_id=1, source_target_pairs={{0,8},{4,12},{8,16},{12,20},{16,24},{20,28},{1,9},{5,13},{9,17},{1... | collective-permute-start | bytes 1572872 | tf_op jit(solution)/shard_map/ppermute | solution.py:429
  37.4 17.8 %collective-permute-start.10 = (bf16[128,2048]{1,0:T(8,128)(2,1)S(1)}, bf16[128,2048]{1,0:T(8,128)(2,1)S(1)}, u32[]{:S(2)}, u32[]{:S(2)}) collective-permute-start(bf16[128,2048]{1,0:T(8,128)(2,1)S(1)} %get-tuple-element.103.refs_0_), channel_id=1, source_target_pairs={{0,1},{1,0},{2,3},{3,2},{4,5},{5,4},{6,7},{7,6},{8,9},{9,8},{10,11... | collective-permute-start | bytes 1572872 | tf_op jit(solution)/shard_map/ppermute | solution.py:424
  37.5 14.3 %collective-permute-start.6 = (bf16[128,2048]{1,0:T(8,128)(2,1)S(1)}, bf16[128,2048]{1,0:T(8,128)(2,1)S(1)}, u32[]{:S(2)}, u32[]{:S(2)}) collective-permute-start(bf16[128,2048]{1,0:T(8,128)(2,1)S(1)} %get-tuple-element.103.refs_0_), channel_id=1, source_target_pairs={{0,2},{1,3},{2,0},{3,1},{4,6},{5,7},{6,4},{7,5},{8,10},{9,11},{10,... | collective-permute-start | bytes 1572872 | tf_op jit(solution)/shard_map/ppermute | solution.py:424
  38.1 17.6 %collective-permute-start.11 = (bf16[128,2048]{1,0:T(8,128)(2,1)S(1)}, bf16[128,2048]{1,0:T(8,128)(2,1)S(1)}, u32[]{:S(2)}, u32[]{:S(2)}) collective-permute-start(bf16[128,2048]{1,0:T(8,128)(2,1)S(1)} %get-tuple-element.104.refs_1_), channel_id=1, source_target_pairs={{0,1},{1,0},{2,3},{3,2},{4,5},{5,4},{6,7},{7,6},{8,9},{9,8},{10,11... | collective-permute-start | bytes 1572872 | tf_op jit(solution)/shard_map/ppermute | solution.py:424
  38.2 14.9 %collective-permute-start.7 = (bf16[128,2048]{1,0:T(8,128)(2,1)S(1)}, bf16[128,2048]{1,0:T(8,128)(2,1)S(1)}, u32[]{:S(2)}, u32[]{:S(2)}) collective-permute-start(bf16[128,2048]{1,0:T(8,128)(2,1)S(1)} %get-tuple-element.104.refs_1_), channel_id=1, source_target_pairs={{0,4},{4,0},{8,12},{12,8},{16,20},{20,16},{24,28},{28,24},{1,5},{5... | collective-permute-start | bytes 1572872 | tf_op jit(solution)/shard_map/ppermute | solution.py:463
  53.6 19.0 %collective-permute-start.18 = (bf16[176,2048]{1,0:T(8,128)(2,1)S(1)}, bf16[176,2048]{1,0:T(8,128)(2,1)S(1)}, u32[]{:S(2)}, u32[]{:S(2)}) collective-permute-start(bf16[176,2048]{1,0:T(8,128)(2,1)S(1)} %bitcast.46), channel_id=1, source_target_pairs={{0,2},{1,3},{2,0},{3,1},{4,6},{5,7},{6,4},{7,5},{8,10},{9,11},{10,... | collective-permute-start | bytes 2162696 | tf_op jit(solution)/shard_map/ppermute | solution.py:424
  55.1 32.0 %collective-permute-start.19 = (bf16[176,2048]{1,0:T(8,128)(2,1)S(1)}, bf16[176,2048]{1,0:T(8,128)(2,1)S(1)}, u32[]{:S(2)}, u32[]{:S(2)}) collective-permute-start(bf16[176,2048]{1,0:T(8,128)(2,1)S(1)} %bitcast.50), channel_id=1, source_target_pairs={{0,2},{1,3},{2,0},{3,1},{4,6},{5,7},{6,4},{7,5},{8,10},{9,11},{10,... | collective-permute-start | bytes 2162696 | tf_op jit(solution)/shard_map/ppermute | solution.py:424
  60.4 36.1 %collective-permute-start.14 = (bf16[128,2048]{1,0:T(8,128)(2,1)S(1)}, bf16[128,2048]{1,0:T(8,128)(2,1)S(1)}, u32[]{:S(2)}, u32[]{:S(2)}) collective-permute-start(bf16[128,2048]{1,0:T(8,128)(2,1)S(1)} %get-tuple-element.151.refs_0_), channel_id=1, source_target_pairs={{0,16},{4,20},{8,24},{12,28},{16,0},{20,4},{24,8},{28,12},{1,17},{... | collective-permute-start | bytes 1572872 | tf_op jit(solution)/shard_map/ppermute | solution.py:540
  67.7 19.5 %collective-permute-start.15 = (bf16[80,2048]{1,0:T(8,128)(2,1)S(1)}, bf16[80,2048]{1,0:T(8,128)(2,1)S(1)}, u32[]{:S(2)}, u32[]{:S(2)}) collective-permute-start(bf16[80,2048]{1,0:T(8,128)(2,1)S(1)} %get-tuple-element.117), channel_id=1, source_target_pairs={{0,4},{4,0},{8,12},{12,8},{16,20},{20,16},{24,28},{28,24},{1,5},{5... | collective-permute-start | bytes 983048 | tf_op jit(solution)/shard_map/ppermute | solution.py:620
  67.9 19.2 %collective-permute-start.16 = (bf16[80,2048]{1,0:T(8,128)(2,1)S(1)}, bf16[80,2048]{1,0:T(8,128)(2,1)S(1)}, u32[]{:S(2)}, u32[]{:S(2)}) collective-permute-start(bf16[80,2048]{1,0:T(8,128)(2,1)S(1)} %get-tuple-element.118), channel_id=1, source_target_pairs={{0,8},{4,12},{8,0},{12,4},{16,24},{20,28},{24,16},{28,20},{1,9},{5... | collective-permute-start | bytes 983048 | tf_op jit(solution)/shard_map/ppermute | solution.py:620
  72.7 23.8 %collective-permute-start.17 = (bf16[80,2048]{1,0:T(8,128)(2,1)S(1)}, bf16[80,2048]{1,0:T(8,128)(2,1)S(1)}, u32[]{:S(2)}, u32[]{:S(2)}) collective-permute-start(bf16[80,2048]{1,0:T(8,128)(2,1)S(1)} %get-tuple-element.119), channel_id=1, source_target_pairs={{0,12},{4,8},{8,4},{12,0},{16,28},{20,24},{24,20},{28,16},{1,13},{... | collective-permute-start | bytes 983048 | tf_op jit(solution)/shard_map/ppermute | solution.py:620
  97.9 21.5 %all-to-all-start = ((bf16[4,80,2048]{2,1,0:T(8,128)(2,1)}), bf16[4,80,2048]{2,1,0:T(8,128)(2,1)S(1)}, u32[]{:S(2)}, u32[]{:S(2)}) async-start(bf16[4,80,2048]{2,1,0:T(8,128)(2,1)} %bitcast.17), calls=%async_computation | async-start | bytes 2621440 | tf_op jit(solution)/shard_map/all_to_all | solution.py:612
  105.3 14.1 %collective-permute-start.26 = (bf16[128,2048]{1,0:T(8,128)(2,1)S(1)}, bf16[128,2048]{1,0:T(8,128)(2,1)}, u32[]{:S(2)}, u32[]{:S(2)}) collective-permute-start(bf16[128,2048]{1,0:T(8,128)(2,1)S(1)} %get-tuple-element.151.refs_0_), channel_id=1, source_target_pairs={{0,2},{1,3},{2,0},{3,1},{4,6},{5,7},{6,4},{7,5},{8,10},{9,11},{10,... | collective-permute-start | bytes 1572872 | tf_op jit(solution)/shard_map/ppermute | solution.py:424
  129.2 19.5 %collective-permute-start.32 = (bf16[128,2048]{1,0:T(8,128)(2,1)S(1)}, bf16[128,2048]{1,0:T(8,128)(2,1)S(1)}, u32[]{:S(2)}, u32[]{:S(2)}) collective-permute-start(bf16[128,2048]{1,0:T(8,128)(2,1)S(1)} %get-tuple-element.155.refs_0_), channel_id=1, source_target_pairs={{0,2},{1,3},{2,0},{3,1},{4,6},{5,7},{6,4},{7,5},{8,10},{9,11},{10,... | collective-permute-start | bytes 1572872 | tf_op jit(solution)/shard_map/ppermute | solution.py:424
  130.7 14.3 %collective-permute-start.27 = (bf16[80,2048]{1,0:T(8,128)(2,1)}, bf16[80,2048]{1,0:T(8,128)(2,1)S(1)}, u32[]{:S(2)}, u32[]{:S(2)}) collective-permute-start(bf16[80,2048]{1,0:T(8,128)(2,1)} %get-tuple-element.147), channel_id=1, source_target_pairs={{0,4},{4,0},{8,12},{12,8},{16,20},{20,16},{24,28},{28,24},{1,5},{5... | collective-permute-start | bytes 983048 | tf_op jit(solution)/shard_map/ppermute | solution.py:620
  134.0 14.6 %collective-permute-start.29 = (bf16[80,2048]{1,0:T(8,128)(2,1)}, bf16[80,2048]{1,0:T(8,128)(2,1)S(1)}, u32[]{:S(2)}, u32[]{:S(2)}) collective-permute-start(bf16[80,2048]{1,0:T(8,128)(2,1)} %get-tuple-element.149), channel_id=1, source_target_pairs={{0,12},{4,8},{8,4},{12,0},{16,28},{20,24},{24,20},{28,16},{1,13},{... | collective-permute-start | bytes 983048 | tf_op jit(solution)/shard_map/ppermute | solution.py:620
  148.6 33.1 %all-to-all-start.1 = ((bf16[4,80,2048]{2,1,0:T(8,128)(2,1)}), bf16[4,80,2048]{2,1,0:T(8,128)(2,1)}, u32[]{:S(2)}, u32[]{:S(2)}) async-start(bf16[4,80,2048]{2,1,0:T(8,128)(2,1)} %bitcast.23), calls=%async_computation.1 | async-start | bytes 2621440 | tf_op jit(solution)/shard_map/all_to_all | solution.py:612
  154.4 26.7 %collective-permute-start.35 = (bf16[128,2048]{1,0:T(8,128)(2,1)S(1)}, bf16[128,2048]{1,0:T(8,128)(2,1)S(1)}, u32[]{:S(2)}, u32[]{:S(2)}) collective-permute-start(bf16[128,2048]{1,0:T(8,128)(2,1)S(1)} %shard_map.208), channel_id=1, source_target_pairs={{0,16},{4,20},{8,24},{12,28},{16,0},{20,4},{24,8},{28,12},{1,17},{... | collective-permute-start | bytes 1572872 | tf_op jit(solution)/shard_map/ppermute | solution.py:540
  155.8 14.4 %collective-permute-start.34 = (bf16[128,2048]{1,0:T(8,128)(2,1)S(1)}, bf16[128,2048]{1,0:T(8,128)(2,1)S(1)}, u32[]{:S(2)}, u32[]{:S(2)}) collective-permute-start(bf16[128,2048]{1,0:T(8,128)(2,1)S(1)} %add_convert_fusion), channel_id=1, source_target_pairs={{0,2},{1,3},{2,0},{3,1},{4,6},{5,7},{6,4},{7,5},{8,10},{9,11},{10,... | collective-permute-start | bytes 1572872 | tf_op jit(solution)/shard_map/ppermute | solution.py:424
  (54 other events, 393.6 us)
